TPU v7x, 32 devices: a whole 2x2x4 slice. The times are simulated.
32 devices in a mesh: dp: 4 (over y, x), fsdp: 8 (over z, core).
Axes of the slice: x: 2, y: 2, z: 4, core: 2. Of those that a mesh axis runs over, the one named last changes fastest.
Arguments:
- tokens: bfloat16 [34816, 512], P(('dp', 'fsdp')), may hold values from -6 to 6
- frame_counts: int32 [32], P(('dp', 'fsdp')), may hold values from 1 to 17, as said below
- cotangent: bfloat16 [34816, 512], P(('dp', 'fsdp')), may hold values from -6 to 6
- w_qkv: float32 [2, 512, 1536], P(None, ('dp', 'fsdp'))
- w_out: float32 [2, 512, 512], P(None, ('dp', 'fsdp'))
- w_up: float32 [2, 512, 2048], P(None, ('dp', 'fsdp'))
- w_down: float32 [2, 2048, 512], P(None, ('dp', 'fsdp'))
- norm_params: float32 [2, 2, 2, 512], P(None, None, None, ('dp', 'fsdp'))
- first_qkv: float32 [2, 512, 1536], P(None, ('dp', 'fsdp')), may hold values from -448 to 448
- first_out: float32 [2, 512, 512], P(None, ('dp', 'fsdp')), may hold values from -448 to 448
- first_up: float32 [2, 512, 2048], P(None, ('dp', 'fsdp')), may hold values from -448 to 448
- first_down: float32 [2, 2048, 512], P(None, ('dp', 'fsdp')), may hold values from -512 to 512
- first_norm: float32 [2, 2, 2, 512], P(None, None, None, ('dp', 'fsdp')), may hold values from -1024 to 1024
- second_qkv: float32 [2, 512, 1536], P(None, ('dp', 'fsdp')), may hold values from 2785.28 to 44564.48
- second_out: float32 [2, 512, 512], P(None, ('dp', 'fsdp')), may hold values from 2785.28 to 44564.48
- second_up: float32 [2, 512, 2048], P(None, ('dp', 'fsdp')), may hold values from 2785.28 to 44564.48
- second_down: float32 [2, 2048, 512], P(None, ('dp', 'fsdp')), may hold values from 4177.92 to 69632
- second_norm: float32 [2, 2, 2, 512], P(None, None, None, ('dp', 'fsdp')), may hold values from 17408 to 278528
Outputs:
- block_out: bfloat16 [34816, 512], P(('dp', 'fsdp'))
- tokens_grad: float32 [34816, 512], P(('dp', 'fsdp'))
- new_qkv: float32 [2, 512, 1536], P(None, ('dp', 'fsdp'))
- new_out: float32 [2, 512, 512], P(None, ('dp', 'fsdp'))
- new_up: float32 [2, 512, 2048], P(None, ('dp', 'fsdp'))
- new_down: float32 [2, 2048, 512], P(None, ('dp', 'fsdp'))
- new_norm: float32 [2, 2, 2, 512], P(None, None, None, ('dp', 'fsdp'))
- copy_qkv: bfloat16 [2, 512, 1536], P(None, ('dp', 'fsdp'))
- copy_out: bfloat16 [2, 512, 512], P(None, ('dp', 'fsdp'))
- copy_up: bfloat16 [2, 512, 2048], P(None, ('dp', 'fsdp'))
- copy_down: bfloat16 [2, 2048, 512], P(None, ('dp', 'fsdp'))
- first_qkv_next: float32 [2, 512, 1536], P(None, ('dp', 'fsdp'))
- first_out_next: float32 [2, 512, 512], P(None, ('dp', 'fsdp'))
- first_up_next: float32 [2, 512, 2048], P(None, ('dp', 'fsdp'))
- first_down_next: float32 [2, 2048, 512], P(None, ('dp', 'fsdp'))
- first_norm_next: float32 [2, 2, 2, 512], P(None, None, None, ('dp', 'fsdp'))
- second_qkv_next: float32 [2, 512, 1536], P(None, ('dp', 'fsdp'))
- second_out_next: float32 [2, 512, 512], P(None, ('dp', 'fsdp'))
- second_up_next: float32 [2, 512, 2048], P(None, ('dp', 'fsdp'))
- second_down_next: float32 [2, 2048, 512], P(None, ('dp', 'fsdp'))
- second_norm_next: float32 [2, 2, 2, 512], P(None, None, None, ('dp', 'fsdp'))
- matrix_norms: float32 [2, 4, 2], replicated
Inputs may be any that keep to these rules, and one draw needn't show every extreme that they name: `frame_counts`: in every draw some clip holds 17 video frames and some clip holds 1.
All inputs are finite; a program needn't handle non-finite values.
Results may differ from a plain program's by a relative error of at most 0.02.
The roundings to bfloat16 on the way count: a program that leaves them out, or rounds other values in their place, can miss the bound.
Values may be sent and summed in bfloat16 or wider, within the bound.
No kernel may reach another device: no remote copies, remote signals or barrier semaphores. Data moves between devices by JAX's collectives and lax.ppermute only.
A program may use at most 256 MiB of HBM per device.

v0:
```python
import jax
import jax.numpy as jnp
from jax import lax
from jax.sharding import PartitionSpec as P

HEADS = 8
HEAD_DIM = 64
FRAMES = 17
WIN = 64
STEP = 5


NORM_EPS = 1e-05
ADAM_EPS = 1e-06
BETA_FIRST = 0.5
BETA_SECOND = 0.5
RATE = 0.25
DECAY_RATE = 0.01
MASKED = -1e30
SPATIAL_FORMS = (
    "gqhd,gkhd->ghqk",
    "ghqk,gkhd->gqhd",
    "ghqk,gqhd->gkhd",
    "gqhd,gkhd->ghqk",
    "ghqk,gkhd->gqhd",
    "ghqk,gqhd->gkhd",
)
TEMPORAL_FORMS = (
    "cqphd,ckphd->cphqk",
    "cphqk,ckphd->cqphd",
    "cphqk,cqphd->ckphd",
    "cqphd,ckphd->cphqk",
    "cphqk,ckphd->cqphd",
    "cphqk,cqphd->ckphd",
)


def layer_norm(inputs, gain_row, shift_row):
    center = inputs - jnp.mean(inputs, axis=-1, keepdims=True)
    spread = jnp.mean(center * center, axis=-1, keepdims=True)
    return center * lax.rsqrt(spread + NORM_EPS) * gain_row + shift_row


def gelu_pair(upward):
    cumulative = 0.5 * (1.0 + lax.erf(upward * 0.7071067811865476))
    return (
        upward * cumulative,
        cumulative + upward * jnp.exp(-0.5 * upward * upward) * 0.3989422804014327,
    )


def split_heads(projected, layout):
    columns = projected.shape[1] // 3
    return (
        projected[:, :columns].reshape(layout),
        projected[:, columns : 2 * columns].reshape(layout),
        projected[:, 2 * columns :].reshape(layout),
    )


def attend(projected, allowed, layout, einsum_forms):
    queries, key_rows, values = split_heads(projected, layout)
    scores = jnp.einsum(
        einsum_forms[0], queries, key_rows, preferred_element_type=jnp.float32
    ) * HEAD_DIM ** (-0.5)
    scores = jnp.where(allowed, scores, MASKED)
    summit = jnp.max(scores, axis=-1, keepdims=True)
    raised = jnp.exp(scores - summit)
    running = jnp.sum(raised, axis=-1, keepdims=True)
    weights = (raised / running).astype(jnp.bfloat16)
    attended = jnp.einsum(einsum_forms[1], weights, values, preferred_element_type=jnp.float32)
    return (
        attended.reshape(projected.shape[0], -1).astype(jnp.bfloat16),
        summit + jnp.log(running),
    )


def attend_back(projected, out_grad, log_total, allowed, layout, einsum_forms):
    queries, key_rows, values = split_heads(projected, layout)
    scale_factor = HEAD_DIM ** (-0.5)
    scores = (
        jnp.einsum(einsum_forms[0], queries, key_rows, preferred_element_type=jnp.float32)
        * scale_factor
    )
    scores = jnp.where(allowed, scores, MASKED)
    weights = jnp.exp(scores - log_total)
    out_heads = out_grad.reshape(queries.shape)
    value_grad = jnp.einsum(
        einsum_forms[2], weights.astype(jnp.bfloat16), out_heads, preferred_element_type=jnp.float32
    )
    weight_grad = jnp.einsum(einsum_forms[3], out_heads, values, preferred_element_type=jnp.float32)
    score_grad = (
        weights * (weight_grad - jnp.sum(weight_grad * weights, axis=-1, keepdims=True))
    ).astype(jnp.bfloat16)
    query_grad = (
        jnp.einsum(einsum_forms[4], score_grad, key_rows, preferred_element_type=jnp.float32)
        * scale_factor
    )
    key_grad = (
        jnp.einsum(einsum_forms[5], score_grad, queries, preferred_element_type=jnp.float32)
        * scale_factor
    )
    row_count = projected.shape[0]
    return jnp.concatenate(
        [
            query_grad.reshape(row_count, -1),
            key_grad.reshape(row_count, -1),
            value_grad.reshape(row_count, -1),
        ],
        axis=1,
    ).astype(jnp.bfloat16)


def fetch_forward(part_qkv, part_out, part_up, part_down, part_norm):
    return (
        lax.all_gather(part_qkv, ("dp", "fsdp"), axis=0, tiled=True),
        lax.all_gather(part_out, ("dp", "fsdp"), axis=0, tiled=True),
        lax.all_gather(part_up, ("dp", "fsdp"), axis=0, tiled=True),
        lax.all_gather(part_down, ("dp", "fsdp"), axis=0, tiled=True),
        lax.all_gather(part_norm, ("dp", "fsdp"), axis=2, tiled=True),
    )


def fetch_backward(part_qkv, part_out, part_up, part_down, part_norm):
    return (
        lax.all_gather(part_qkv, ("dp", "fsdp"), axis=0, tiled=True),
        lax.all_gather(part_out, ("dp", "fsdp"), axis=0, tiled=True),
        lax.all_gather(part_up, ("dp", "fsdp"), axis=0, tiled=True),
        lax.all_gather(part_down, ("dp", "fsdp"), axis=0, tiled=True),
        lax.all_gather(part_norm, ("dp", "fsdp"), axis=2, tiled=True),
    )


def reduce_grads(grad_qkv, grad_out, grad_up, grad_down, grad_norm):
    return (
        lax.psum_scatter(grad_qkv, ("dp", "fsdp"), scatter_dimension=0, tiled=True),
        lax.psum_scatter(grad_out, ("dp", "fsdp"), scatter_dimension=0, tiled=True),
        lax.psum_scatter(grad_up, ("dp", "fsdp"), scatter_dimension=0, tiled=True),
        lax.psum_scatter(grad_down, ("dp", "fsdp"), scatter_dimension=0, tiled=True),
        lax.psum_scatter(grad_norm, ("dp", "fsdp"), scatter_dimension=2, tiled=True),
    )


def block_forward(stream, gathered, allowed, frame_gate, layout, einsum_forms):
    weight_qkv, weight_out, weight_up, weight_down, gain_rows = gathered
    gains = gain_rows.astype(jnp.float32)
    normed = layer_norm(stream, gains[0, 0], gains[0, 1]).astype(jnp.bfloat16)
    projected = jnp.dot(normed, weight_qkv, preferred_element_type=jnp.float32).astype(jnp.bfloat16)
    attended, log_total = attend(projected, allowed, layout, einsum_forms)
    branch = jnp.dot(attended, weight_out, preferred_element_type=jnp.float32)
    middle = stream + branch * frame_gate
    hidden_in = layer_norm(middle, gains[1, 0], gains[1, 1]).astype(jnp.bfloat16)
    upward = jnp.dot(hidden_in, weight_up, preferred_element_type=jnp.float32)
    value_part, gelu_slope = gelu_pair(upward)
    hidden = value_part.astype(jnp.bfloat16)
    result = middle + jnp.dot(hidden, weight_down, preferred_element_type=jnp.float32)
    return (
        result,
        (stream, normed, projected, attended, log_total, middle, hidden_in, hidden, gelu_slope),
    )


def block_backward(upstream, kept, gathered, allowed, frame_gate, layout, einsum_forms):
    stream, normed, projected, attended, log_total, middle, hidden_in, hidden, gelu_slope = kept
    weight_qkv, weight_out, weight_up, weight_down, gain_rows = gathered
    gains = gain_rows.astype(jnp.float32)
    out_grad = upstream.astype(jnp.bfloat16)
    grad_down = jnp.einsum("tf,td->fd", hidden, out_grad, preferred_element_type=jnp.float32)
    hidden_grad = jnp.einsum("td,fd->tf", out_grad, weight_down, preferred_element_type=jnp.float32)
    up_grad = (hidden_grad * gelu_slope).astype(jnp.bfloat16)
    grad_up = jnp.einsum("td,tf->df", hidden_in, up_grad, preferred_element_type=jnp.float32)
    hidden_in_grad = jnp.einsum("tf,df->td", up_grad, weight_up, preferred_element_type=jnp.float32)
    ignored, pull_second = jax.vjp(layer_norm, middle, gains[1, 0], gains[1, 1])
    middle_part, gain_second, shift_second = pull_second(hidden_in_grad)
    middle_grad = upstream + middle_part
    branch_grad = (middle_grad * frame_gate).astype(jnp.bfloat16)
    grad_out = jnp.einsum("ti,tj->ij", attended, branch_grad, preferred_element_type=jnp.float32)
    attended_grad = jnp.einsum(
        "tj,ij->ti", branch_grad, weight_out, preferred_element_type=jnp.float32
    ).astype(jnp.bfloat16)
    projected_grad = attend_back(projected, attended_grad, log_total, allowed, layout, einsum_forms)
    grad_qkv = jnp.einsum("ti,tj->ij", normed, projected_grad, preferred_element_type=jnp.float32)
    normed_grad = jnp.einsum(
        "tj,ij->ti", projected_grad, weight_qkv, preferred_element_type=jnp.float32
    )
    unused, pull_first = jax.vjp(layer_norm, stream, gains[0, 0], gains[0, 1])
    stream_part, gain_first, shift_first = pull_first(normed_grad)
    grad_norm = jnp.stack(
        [jnp.stack([gain_first, shift_first]), jnp.stack([gain_second, shift_second])]
    )
    return (middle_grad + stream_part, (grad_qkv, grad_out, grad_up, grad_down, grad_norm))


def adam_parts(gradient, first_moment, second_moment):
    first_next = BETA_FIRST * first_moment + (1.0 - BETA_FIRST) * gradient
    second_next = BETA_SECOND * second_moment + (1.0 - BETA_SECOND) * gradient * gradient
    direction = (
        first_next
        / (1.0 - BETA_FIRST**STEP)
        / (jnp.sqrt(second_next / (1.0 - BETA_SECOND**STEP)) + ADAM_EPS)
    )
    return (first_next, second_next, direction)


def body(
    tokens,
    frame_counts,
    cotangent,
    w_qkv,
    w_out,
    w_up,
    w_down,
    norm_params,
    first_qkv,
    first_out,
    first_up,
    first_down,
    first_norm,
    second_qkv,
    second_out,
    second_up,
    second_down,
    second_norm,
):
    masters = (w_qkv, w_out, w_up, w_down, norm_params)
    frame_ids = jnp.arange(FRAMES)
    is_video = frame_ids[None, :] < frame_counts[:, None]
    allowed = (frame_ids[None, None, :] <= frame_ids[None, :, None]) & (
        is_video[:, :, None] & is_video[:, None, :]
        | (frame_ids[None, :, None] == frame_ids[None, None, :])
    )
    allowed = allowed[:, None, None, :, :]
    frame_gate = jnp.broadcast_to(
        is_video.astype(jnp.float32)[:, :, None], is_video.shape + (WIN,)
    ).reshape(-1, 1)
    settings = (
        ((-1, WIN, HEADS, HEAD_DIM), SPATIAL_FORMS, True, 1.0),
        ((-1, FRAMES, WIN, HEADS, HEAD_DIM), TEMPORAL_FORMS, allowed, frame_gate),
    )
    stream = tokens.astype(jnp.float32)
    saved = []
    fetched = []
    for layer_index in range(2):
        layout, einsum_forms, layer_allowed, layer_gate = settings[layer_index]
        gathered = fetch_forward(
            w_qkv[layer_index].astype(jnp.bfloat16),
            w_out[layer_index].astype(jnp.bfloat16),
            w_up[layer_index].astype(jnp.bfloat16),
            w_down[layer_index].astype(jnp.bfloat16),
            norm_params[layer_index].astype(jnp.bfloat16),
        )
        stream, kept = block_forward(
            stream, gathered, layer_allowed, layer_gate, layout, einsum_forms
        )
        saved.append(kept)
        fetched.append(gathered)
    block_out = stream.astype(jnp.bfloat16)
    upstream = cotangent.astype(jnp.float32)
    reduced = [None, None]
    for layer_index in (1, 0):
        layout, einsum_forms, layer_allowed, layer_gate = settings[layer_index]
        gathered = fetch_backward(
            w_qkv[layer_index].astype(jnp.bfloat16),
            w_out[layer_index].astype(jnp.bfloat16),
            w_up[layer_index].astype(jnp.bfloat16),
            w_down[layer_index].astype(jnp.bfloat16),
            norm_params[layer_index].astype(jnp.bfloat16),
        )
        upstream, local_grads = block_backward(
            upstream, saved[layer_index], gathered, layer_allowed, layer_gate, layout, einsum_forms
        )
        reduced[layer_index] = reduce_grads(
            local_grads[0], local_grads[1], local_grads[2], local_grads[3], local_grads[4]
        )
    stacked = [
        jnp.stack([reduced[0][member_index], reduced[1][member_index]]) for member_index in range(5)
    ]
    firsts = (first_qkv, first_out, first_up, first_down, first_norm)
    seconds = (second_qkv, second_out, second_up, second_down, second_norm)
    updates = [
        adam_parts(stacked[member_index], firsts[member_index], seconds[member_index])
        for member_index in range(5)
    ]
    directions = [
        updates[member_index][2] + DECAY_RATE * masters[member_index] for member_index in range(4)
    ]
    step_squares = jnp.stack(
        [jnp.sum(direction * direction, axis=(1, 2)) for direction in directions], axis=1
    )
    local_squares = jnp.stack(
        [
            jnp.stack([jnp.sum(matrix * matrix, axis=(1, 2)) for matrix in masters[:4]], axis=1),
            step_squares,
        ],
        axis=2,
    )
    matrix_norms = jnp.sqrt(lax.psum(local_squares, ("dp", "fsdp")))
    updated = [
        masters[member_index]
        - RATE
        * (matrix_norms[:, member_index, 0] / matrix_norms[:, member_index, 1])[:, None, None]
        * directions[member_index]
        for member_index in range(4)
    ]
    norm_updated = norm_params - RATE * updates[4][2]
    return (
        block_out,
        upstream,
        updated[0],
        updated[1],
        updated[2],
        updated[3],
        norm_updated,
        updated[0].astype(jnp.bfloat16),
        updated[1].astype(jnp.bfloat16),
        updated[2].astype(jnp.bfloat16),
        updated[3].astype(jnp.bfloat16),
        updates[0][0],
        updates[1][0],
        updates[2][0],
        updates[3][0],
        updates[4][0],
        updates[0][1],
        updates[1][1],
        updates[2][1],
        updates[3][1],
        updates[4][1],
        matrix_norms,
    )


def solution(mesh):
    in_specs = (
        P(("dp", "fsdp"), None),
        P(("dp", "fsdp")),
        P(("dp", "fsdp"), None),
        P(None, ("dp", "fsdp"), None),
        P(None, ("dp", "fsdp"), None),
        P(None, ("dp", "fsdp"), None),
        P(None, ("dp", "fsdp"), None),
        P(None, None, None, ("dp", "fsdp")),
        P(None, ("dp", "fsdp"), None),
        P(None, ("dp", "fsdp"), None),
        P(None, ("dp", "fsdp"), None),
        P(None, ("dp", "fsdp"), None),
        P(None, None, None, ("dp", "fsdp")),
        P(None, ("dp", "fsdp"), None),
        P(None, ("dp", "fsdp"), None),
        P(None, ("dp", "fsdp"), None),
        P(None, ("dp", "fsdp"), None),
        P(None, None, None, ("dp", "fsdp")),
    )
    out_specs = (
        P(("dp", "fsdp"), None),
        P(("dp", "fsdp"), None),
        P(None, ("dp", "fsdp"), None),
        P(None, ("dp", "fsdp"), None),
        P(None, ("dp", "fsdp"), None),
        P(None, ("dp", "fsdp"), None),
        P(None, None, None, ("dp", "fsdp")),
        P(None, ("dp", "fsdp"), None),
        P(None, ("dp", "fsdp"), None),
        P(None, ("dp", "fsdp"), None),
        P(None, ("dp", "fsdp"), None),
        P(None, ("dp", "fsdp"), None),
        P(None, ("dp", "fsdp"), None),
        P(None, ("dp", "fsdp"), None),
        P(None, ("dp", "fsdp"), None),
        P(None, None, None, ("dp", "fsdp")),
        P(None, ("dp", "fsdp"), None),
        P(None, ("dp", "fsdp"), None),
        P(None, ("dp", "fsdp"), None),
        P(None, ("dp", "fsdp"), None),
        P(None, None, None, ("dp", "fsdp")),
        P(),
    )
    return jax.shard_map(body, mesh=mesh, in_specs=in_specs, out_specs=out_specs, check_vma=False)
```

profile of v0, /device:TPU:0, one launch (start us, length us, event | category | flops | bytes accessed | tf_op | source)
XLA Modules:
  0.0 1832.3 jit_solution(6619226226079605546)
XLA Ops:
  16.4 44.7 %all-gather.5 = bf16[1,2,2,512]{2,1,0,3:T(2,128)(2,1)S(1)} all-gather(bf16[1,2,2,16]{2,1,0,3:T(2,128)(2,1)S(1)} %get-tuple-element.181), channel_id=7, replica_groups=mesh['dp'=4,'fsdp'=8] {'dp','fsdp'}, dimensions={3}, use_global_device_ids=true | all-gather | bytes 4224 | tf_op jit(solution)/shard_map/all_gather | solution.py:120
  61.3 6.9 slice_reduce_fusion.1
  68.2 38.3 %all-gather = bf16[1,2,2,512]{2,1,0,3:T(2,128)(2,1)S(1)} all-gather(bf16[1,2,2,16]{2,1,0,3:T(2,128)(2,1)S(1)} %get-tuple-element.182), channel_id=2, replica_groups=mesh['dp'=4,'fsdp'=8] {'dp','fsdp'}, dimensions={3}, use_global_device_ids=true | all-gather | bytes 4224 | tf_op jit(solution)/shard_map/all_gather | solution.py:120
  106.7 6.9 slice_reduce_fusion.5
  113.6 42.7 %all-gather.7 = bf16[1,512,512]{2,1,0:T(8,128)(2,1)} all-gather(bf16[1,16,512]{2,1,0:T(8,128)(2,1)S(1)} %get-tuple-element.179), channel_id=9, replica_groups=mesh['dp'=4,'fsdp'=8] {'dp','fsdp'}, dimensions={1}, use_global_device_ids=true | all-gather | bytes 540672 | tf_op jit(solution)/shard_map/all_gather | solution.py:117
  156.3 43.2 %all-gather.2 = bf16[1,512,512]{2,1,0:T(8,128)(2,1)} all-gather(bf16[1,16,512]{2,1,0:T(8,128)(2,1)S(1)} %get-tuple-element.180), channel_id=4, replica_groups=mesh['dp'=4,'fsdp'=8] {'dp','fsdp'}, dimensions={1}, use_global_device_ids=true | all-gather | bytes 540672 | tf_op jit(solution)/shard_map/all_gather | solution.py:117
  237.3 19.8 %multiply_convert_fusion.1 = (bf16[1088,2048]{1,0:T(8,128)(2,1)}, f32[1088,2048]{1,0:T(8,128)}) fusion(bf16[1,512,2048]{2,1,0:T(8,128)(2,1)} %all-gather.19.cloned.1.call-done, f32[1088,512]{1,0:T(8,128)S(1)} %get-tuple-element.186, f32[512]{0:T(512)S(1)} %get-tuple-element.127, f32[512]{0:T(512)S(1)} %get-tuple-element.126, f32[1088]{0:T(1024)S(1)} %fusion.106, ...), kind=kOutput, calls=%fused_computation.14 | convolution fusion | flops 2295627776 | bytes 17707520 | tf_op jit(solution)/shard_map/dot_general | solution.py:153
  305.6 8.2 multiply_convert_fusion
  313.8 50.6 %all-gather.27.cloned.1.call-done = bf16[1,2048,512]{2,1,0:T(8,128)(2,1)} async-done(((bf16[1,64,512]{2,1,0:T(8,128)(2,1)}), bf16[1,2048,512]{2,1,0:T(8,128)(2,1)}) %all-gather.27.cloned.1.call-update) | async-done | bytes 2097168 | tf_op jit(solution)/shard_map/all_gather | solution.py:119
  364.3 8.1 fusion.8
  382.4 7.7 convert_bitcast_fusion
  528.7 8.0 fusion.123
  537.4 7.1 fusion.121
  571.6 32.1 %reduce-scatter.33.cloned.1.call-done = f32[16,4]{1,0:T(8,128)} async-done(((f32[512,4]{1,0:T(8,128)}), f32[16,4]{1,0:T(8,128)}) %reduce-scatter.33.cloned.1.call-update) | async-done | bytes 272
  604.6 132.2 %reduce-scatter.31.cloned.1.call-done = f32[16,4]{1,0:T(8,128)} async-done(((f32[512,4]{1,0:T(8,128)}), f32[16,4]{1,0:T(8,128)}) %reduce-scatter.31.cloned.1.call-update) | async-done | bytes 272
  737.6 133.0 %reduce-scatter.21.cloned.1.call-done = f32[16,512]{1,0:T(8,128)} async-done(((f32[512,512]{1,0:T(8,128)}), f32[16,512]{1,0:T(8,128)}) %reduce-scatter.21.cloned.1.call-update) | async-done | bytes 32784 | tf_op jit(solution)/shard_map/reduce_scatter | solution.py:137
  870.6 133.7 %reduce-scatter.19.cloned.1.call-done = f32[16,512]{1,0:T(8,128)} async-done(((f32[512,512]{1,0:T(8,128)}), f32[16,512]{1,0:T(8,128)}) %reduce-scatter.19.cloned.1.call-update) | async-done | bytes 32784 | tf_op jit(solution)/shard_map/reduce_scatter | solution.py:137
  1005.3 102.6 %reduce-scatter.17.cloned.1.call-done = f32[16,1536]{1,0:T(8,128)} async-done(((f32[512,1536]{1,0:T(8,128)}), f32[16,1536]{1,0:T(8,128)}) %reduce-scatter.17.cloned.1.call-update) | async-done | bytes 98320 | tf_op jit(solution)/shard_map/reduce_scatter | solution.py:136
  1107.9 105.7 %reduce-scatter.15.cloned.1.call-done = f32[16,1536]{1,0:T(8,128)} async-done(((f32[512,1536]{1,0:T(8,128)}), f32[16,1536]{1,0:T(8,128)}) %reduce-scatter.15.cloned.1.call-update) | async-done | bytes 98320 | tf_op jit(solution)/shard_map/reduce_scatter | solution.py:136
  1214.8 143.2 %reduce-scatter.25.cloned.1.call-done = f32[16,2048]{1,0:T(8,128)} async-done(((f32[512,2048]{1,0:T(8,128)}), f32[16,2048]{1,0:T(8,128)}) %reduce-scatter.25.cloned.1.call-update) | async-done | bytes 131088 | tf_op jit(solution)/shard_map/reduce_scatter | solution.py:138
  1358.0 141.2 %reduce-scatter.23.cloned.1.call-done = f32[16,2048]{1,0:T(8,128)} async-done(((f32[512,2048]{1,0:T(8,128)}), f32[16,2048]{1,0:T(8,128)}) %reduce-scatter.23.cloned.1.call-update) | async-done | bytes 131088 | tf_op jit(solution)/shard_map/reduce_scatter | solution.py:138
  1500.5 139.9 %reduce-scatter.29.cloned.1.call-done = f32[64,512]{1,0:T(8,128)} async-done(((f32[2048,512]{1,0:T(8,128)}), f32[64,512]{1,0:T(8,128)}) %reduce-scatter.29.cloned.1.call-update) | async-done | bytes 131088 | tf_op jit(solution)/shard_map/reduce_scatter | solution.py:139
  1640.3 141.9 %reduce-scatter.27.cloned.1.call-done = f32[64,512]{1,0:T(8,128)} async-done(((f32[2048,512]{1,0:T(8,128)}), f32[64,512]{1,0:T(8,128)}) %reduce-scatter.27.cloned.1.call-update) | async-done | bytes 131088 | tf_op jit(solution)/shard_map/reduce_scatter | solution.py:139
  1784.4 36.9 %psum.7 = f32[2,4,2]{1,0,2:T(2,128)S(1)} all-reduce(f32[2,4,2]{1,0,2:T(2,128)S(1)} %pad_maximum_fusion.9), channel_id=1, replica_groups=mesh['dp'=4,'fsdp'=8] {'dp','fsdp'}, use_global_device_ids=true, to_apply=%region_38.39 | all-reduce | flops 16 | bytes 128 | tf_op jit(solution)/shard_map/psum | solution.py:297
  (439 shorter events, 281.5 us)
Async XLA Ops:
  7.2 192.2 %all-gather.17.cloned.1.call-start = ((), (), s32[]{:S(2)}) async-start(), calls=%async_computation.18 | async-start | bytes 1622016 | tf_op jit(solution)/shard_map/all_gather | solution.py:116
  9.0 228.3 %all-gather.19.cloned.1.call-start = ((), (), s32[]{:S(2)}) async-start(), calls=%async_computation.19 | async-start | bytes 2162688 | tf_op jit(solution)/shard_map/all_gather | solution.py:118
  10.7 246.5 %all-gather.21.cloned.1.call-start = ((), (), s32[]{:S(2)}) async-start(), calls=%async_computation.20 | async-start | bytes 2162688 | tf_op jit(solution)/shard_map/all_gather | solution.py:119
  12.4 253.7 %all-gather.23.cloned.1.call-start = ((), (), s32[]{:S(2)}) async-start(), calls=%async_computation.21 | async-start | bytes 1622016 | tf_op jit(solution)/shard_map/all_gather | solution.py:116
  13.0 292.6 %all-gather.25.cloned.1.call-start = ((), (), s32[]{:S(2)}) async-start(), calls=%async_computation.22 | async-start | bytes 2162688 | tf_op jit(solution)/shard_map/all_gather | solution.py:118
  13.5 350.8 %all-gather.27.cloned.1.call-start = ((), (), s32[]{:S(2)}) async-start(), calls=%async_computation.23 | async-start | bytes 2162688 | tf_op jit(solution)/shard_map/all_gather | solution.py:119
  14.1 589.6 %reduce-scatter.33.cloned.1.call-start = ((), (), s32[]{:S(2)}) async-start(), calls=%async_computation.25 | async-start | bytes 270336
  471.3 265.5 %reduce-scatter.31.cloned.1.call-start = ((), (), s32[]{:S(2)}) async-start(), calls=%async_computation.24 | async-start | bytes 270336
  506.7 363.9 %reduce-scatter.21.cloned.1.call-start = ((), (), s32[]{:S(2)}) async-start(), calls=%async_computation.13 | async-start | bytes 1081344 | tf_op jit(solution)/shard_map/reduce_scatter | solution.py:137
  510.2 494.2 %reduce-scatter.19.cloned.1.call-start = ((), (), s32[]{:S(2)}) async-start(), calls=%async_computation.12 | async-start | bytes 1081344 | tf_op jit(solution)/shard_map/reduce_scatter | solution.py:137
  514.1 593.8 %reduce-scatter.17.cloned.1.call-start = ((), (), s32[]{:S(2)}) async-start(), calls=%async_computation.11 | async-start | bytes 3244032 | tf_op jit(solution)/shard_map/reduce_scatter | solution.py:136
  521.0 692.6 %reduce-scatter.15.cloned.1.call-start = ((), (), s32[]{:S(2)}) async-start(), calls=%async_computation.10 | async-start | bytes 3244032 | tf_op jit(solution)/shard_map/reduce_scatter | solution.py:136
  528.1 829.9 %reduce-scatter.25.cloned.1.call-start = ((), (), s32[]{:S(2)}) async-start(), calls=%async_computation.15 | async-start | bytes 4325376 | tf_op jit(solution)/shard_map/reduce_scatter | solution.py:138
  536.8 962.4 %reduce-scatter.23.cloned.1.call-start = ((), (), s32[]{:S(2)}) async-start(), calls=%async_computation.14 | async-start | bytes 4325376 | tf_op jit(solution)/shard_map/reduce_scatter | solution.py:138
  544.6 1095.8 %reduce-scatter.29.cloned.1.call-start = ((), (), s32[]{:S(2)}) async-start(), calls=%async_computation.17 | async-start | bytes 4325376 | tf_op jit(solution)/shard_map/reduce_scatter | solution.py:139
  552.7 1229.6 %reduce-scatter.27.cloned.1.call-start = ((), (), s32[]{:S(2)}) async-start(), calls=%async_computation.16 | async-start | bytes 4325376 | tf_op jit(solution)/shard_map/reduce_scatter | solution.py:139
  569.4 929.8 %copy-start.43 = (f32[2,16,2048]{2,1,0:T(8,128)S(1)}, f32[2,16,2048]{2,1,0:T(8,128)}, u32[]{:S(2)}) copy-start(f32[2,16,2048]{2,1,0:T(8,128)} %param.23) | copy-start | bytes 786436
  569.4 929.8 %copy-start.62 = (f32[2,16,2048]{2,1,0:T(8,128)S(1)}, f32[2,16,2048]{2,1,0:T(8,128)}, u32[]{:S(2)}) copy-start(f32[2,16,2048]{2,1,0:T(8,128)} %param.28) | copy-start | bytes 786436
  569.4 929.8 %copy-start.63 = (f32[2,16,2048]{2,1,0:T(8,128)S(1)}, f32[2,16,2048]{2,1,0:T(8,128)}, u32[]{:S(2)}) copy-start(f32[2,16,2048]{2,1,0:T(8,128)} %param.33) | copy-start | bytes 786436
  571.6 1210.6 %copy-start.42 = (f32[2,64,512]{2,1,0:T(8,128)S(1)}, f32[2,64,512]{2,1,0:T(8,128)}, u32[]{:S(2)}) copy-start(f32[2,64,512]{2,1,0:T(8,128)} %param.24) | copy-start | bytes 786436
  571.6 1210.6 %copy-start.64 = (f32[2,64,512]{2,1,0:T(8,128)S(1)}, f32[2,64,512]{2,1,0:T(8,128)}, u32[]{:S(2)}) copy-start(f32[2,64,512]{2,1,0:T(8,128)} %param.29) | copy-start | bytes 786436
  571.6 1210.6 %copy-start.65 = (f32[2,64,512]{2,1,0:T(8,128)S(1)}, f32[2,64,512]{2,1,0:T(8,128)}, u32[]{:S(2)}) copy-start(f32[2,64,512]{2,1,0:T(8,128)} %param.34) | copy-start | bytes 786436
  1005.3 817.5 %copy-start.66 = (f32[2,16,512]{2,1,0:T(8,128)}, f32[2,16,512]{2,1,0:T(8,128)S(1)}, u32[]{:S(2)}) copy-start(f32[2,16,512]{2,1,0:T(8,128)S(1)} %get-tuple-element.155) | copy-start | bytes 196612
  1005.3 817.5 %copy-start.67 = (f32[2,16,512]{2,1,0:T(8,128)}, f32[2,16,512]{2,1,0:T(8,128)S(1)}, u32[]{:S(2)}) copy-start(f32[2,16,512]{2,1,0:T(8,128)S(1)} %get-tuple-element.156) | copy-start | bytes 196612
  (118 other events, 9953.8 us)
Sparse Core Ops, SparseCore 0:
  11.6 57.9 all-gather.16
  73.2 56.2 all-gather.18
  133.1 55.8 all-gather.20
  192.5 54.2 all-gather.22
  250.2 55.3 all-gather.24
  309.0 55.3 all-gather.26
  471.4 132.2 reduce-scatter.32
  606.6 130.1 reduce-scatter.30
  739.0 131.5 reduce-scatter.20
  872.8 131.5 reduce-scatter.18
  1009.8 98.0 reduce-scatter.16
  1113.2 100.3 reduce-scatter.14
  1215.9 142.0 reduce-scatter.24
  1360.1 139.0 reduce-scatter.22
  1501.3 138.9 reduce-scatter.28
  1642.5 139.7 reduce-scatter.26
where the time goes:
time: 1840 us; the launch traced here: 1830 us
  waiting for transfers between devices  1260 us (68%)
  blocking collectives  206 us (11%)
  matrix products  180 us (10%)
  local copies, waits for them, and re-layouts  133 us (7%)
  other arithmetic  33.7 us (2%)
    reduce_scatter x2, waiting for transfers between devices, reduce_grads(): lax.psum_scatter(grad_up, ('dp', 'fsdp'), scatter_dimension=0, tiled=True)  284 us
    reduce_scatter x2, waiting for transfers between devices, reduce_grads(): lax.psum_scatter(grad_down, ('dp', 'fsdp'), scatter_dimension=0, tiled=True)  282 us
    reduce_scatter x2, waiting for transfers between devices, reduce_grads(): lax.psum_scatter(grad_out, ('dp', 'fsdp'), scatter_dimension=0, tiled=True)  267 us
    reduce_scatter x2, waiting for transfers between devices, reduce_grads(): lax.psum_scatter(grad_qkv, ('dp', 'fsdp'), scatter_dimension=0, tiled=True)  208 us
    unnamed x18, waiting for transfers between devices  166 us
    all_gather x2, blocking collectives, fetch_forward(): lax.all_gather(part_out, ('dp', 'fsdp'), axis=0, tiled=True)  85.9 us
    all_gather x2, blocking collectives, fetch_forward(): lax.all_gather(part_norm, ('dp', 'fsdp'), axis=2, tiled=True)  82.9 us
    all_gather x2, waiting for transfers between devices, fetch_forward(): lax.all_gather(part_down, ('dp', 'fsdp'), axis=0, tiled=True)  50.6 us
  transfers between devices with their start and end apart: 16, of which 12 were waited for; matrix products, arithmetic and copies ran while one was open for 12% of the time, Pallas kernels for 0%

commit v1 on v0

--- a/solution.py
+++ b/solution.py
@@ -111,34 +111,37 @@
     ).astype(jnp.bfloat16)
 
 
-def fetch_forward(part_qkv, part_out, part_up, part_down, part_norm):
-    return (
-        lax.all_gather(part_qkv, ("dp", "fsdp"), axis=0, tiled=True),
-        lax.all_gather(part_out, ("dp", "fsdp"), axis=0, tiled=True),
-        lax.all_gather(part_up, ("dp", "fsdp"), axis=0, tiled=True),
-        lax.all_gather(part_down, ("dp", "fsdp"), axis=0, tiled=True),
-        lax.all_gather(part_norm, ("dp", "fsdp"), axis=2, tiled=True),
-    )
-
-
-def fetch_backward(part_qkv, part_out, part_up, part_down, part_norm):
-    return (
-        lax.all_gather(part_qkv, ("dp", "fsdp"), axis=0, tiled=True),
-        lax.all_gather(part_out, ("dp", "fsdp"), axis=0, tiled=True),
-        lax.all_gather(part_up, ("dp", "fsdp"), axis=0, tiled=True),
-        lax.all_gather(part_down, ("dp", "fsdp"), axis=0, tiled=True),
-        lax.all_gather(part_norm, ("dp", "fsdp"), axis=2, tiled=True),
-    )
-
-
-def reduce_grads(grad_qkv, grad_out, grad_up, grad_down, grad_norm):
-    return (
-        lax.psum_scatter(grad_qkv, ("dp", "fsdp"), scatter_dimension=0, tiled=True),
-        lax.psum_scatter(grad_out, ("dp", "fsdp"), scatter_dimension=0, tiled=True),
-        lax.psum_scatter(grad_up, ("dp", "fsdp"), scatter_dimension=0, tiled=True),
-        lax.psum_scatter(grad_down, ("dp", "fsdp"), scatter_dimension=0, tiled=True),
-        lax.psum_scatter(grad_norm, ("dp", "fsdp"), scatter_dimension=2, tiled=True),
-    )
+def pack_weights(part_qkv, part_out, part_up, part_down):
+    return jnp.concatenate(
+        [part_qkv[:, 512 * i : 512 * i + 512] for i in range(3)]
+        + [part_out]
+        + [part_up[:, 512 * i : 512 * i + 512] for i in range(4)]
+        + [part_down],
+        axis=0,
+    ).astype(jnp.bfloat16)
+
+
+def unpack_shards(packed, rows):
+    pieces = [packed[:, rows * i : rows * i + rows].reshape(-1, 512) for i in range(8)]
+    return (
+        jnp.concatenate(pieces[:3], axis=1),
+        pieces[3],
+        jnp.concatenate(pieces[4:], axis=1),
+        packed[:, 8 * rows :].reshape(-1, 512),
+    )
+
+
+def pack_grads(grad_qkv, grad_out, grad_up, grad_down, shards):
+    def cut(matrix):
+        return matrix.reshape(shards, -1, 512)
+
+    return jnp.concatenate(
+        [cut(grad_qkv[:, 512 * i : 512 * i + 512]) for i in range(3)]
+        + [cut(grad_out)]
+        + [cut(grad_up[:, 512 * i : 512 * i + 512]) for i in range(4)]
+        + [cut(grad_down)],
+        axis=1,
+    ).astype(jnp.bfloat16)
 
 
 def block_forward(stream, gathered, allowed, frame_gate, layout, einsum_forms):
@@ -238,17 +241,27 @@
         ((-1, FRAMES, WIN, HEADS, HEAD_DIM), TEMPORAL_FORMS, allowed, frame_gate),
     )
     stream = tokens.astype(jnp.float32)
+    axes = ("dp", "fsdp")
+    shards = lax.axis_size("dp") * lax.axis_size("fsdp")
+    rows = w_out.shape[1]
+    norm_rows = jnp.pad(
+        norm_params.astype(jnp.bfloat16).reshape(1, -1), ((0, rows - 1), (0, 512 - 8 * rows))
+    )
     saved = []
     fetched = []
     for layer_index in range(2):
         layout, einsum_forms, layer_allowed, layer_gate = settings[layer_index]
-        gathered = fetch_forward(
-            w_qkv[layer_index].astype(jnp.bfloat16),
-            w_out[layer_index].astype(jnp.bfloat16),
-            w_up[layer_index].astype(jnp.bfloat16),
-            w_down[layer_index].astype(jnp.bfloat16),
-            norm_params[layer_index].astype(jnp.bfloat16),
+        packed = pack_weights(
+            w_qkv[layer_index], w_out[layer_index], w_up[layer_index], w_down[layer_index]
         )
+        if layer_index == 0:
+            packed = jnp.concatenate([packed, norm_rows], axis=0)
+        packed = lax.all_gather(packed, axes, axis=0)
+        if layer_index == 0:
+            gains_all = packed[:, 12 * rows, : 8 * rows].reshape(shards, 2, 2, 2, rows)
+            gains_all = gains_all.transpose(1, 2, 3, 0, 4).reshape(2, 2, 2, -1)
+            packed = packed[:, : 12 * rows]
+        gathered = unpack_shards(packed, rows) + (gains_all[layer_index],)
         stream, kept = block_forward(
             stream, gathered, layer_allowed, layer_gate, layout, einsum_forms
         )
@@ -257,29 +270,31 @@
     block_out = stream.astype(jnp.bfloat16)
     upstream = cotangent.astype(jnp.float32)
     reduced = [None, None]
+    norm_grads = [None, None]
     for layer_index in (1, 0):
         layout, einsum_forms, layer_allowed, layer_gate = settings[layer_index]
-        gathered = fetch_backward(
-            w_qkv[layer_index].astype(jnp.bfloat16),
-            w_out[layer_index].astype(jnp.bfloat16),
-            w_up[layer_index].astype(jnp.bfloat16),
-            w_down[layer_index].astype(jnp.bfloat16),
-            norm_params[layer_index].astype(jnp.bfloat16),
+        upstream, local_grads = block_backward(
+            upstream,
+            saved[layer_index],
+            fetched[layer_index],
+            layer_allowed,
+            layer_gate,
+            layout,
+            einsum_forms,
         )
-        upstream, local_grads = block_backward(
-            upstream, saved[layer_index], gathered, layer_allowed, layer_gate, layout, einsum_forms
-        )
-        reduced[layer_index] = reduce_grads(
-            local_grads[0], local_grads[1], local_grads[2], local_grads[3], local_grads[4]
-        )
+        norm_grads[layer_index] = local_grads[4]
+        packed = pack_grads(*local_grads[:4], shards)
+        summed = lax.psum_scatter(packed, axes, scatter_dimension=0, tiled=False)
+        reduced[layer_index] = unpack_shards(summed[None].astype(jnp.float32), rows)
+    norm_parts = jnp.stack(norm_grads).reshape(8, shards, rows).transpose(1, 0, 2)
     stacked = [
-        jnp.stack([reduced[0][member_index], reduced[1][member_index]]) for member_index in range(5)
+        jnp.stack([reduced[0][member_index], reduced[1][member_index]]) for member_index in range(4)
     ]
     firsts = (first_qkv, first_out, first_up, first_down, first_norm)
     seconds = (second_qkv, second_out, second_up, second_down, second_norm)
     updates = [
         adam_parts(stacked[member_index], firsts[member_index], seconds[member_index])
-        for member_index in range(5)
+        for member_index in range(4)
     ]
     directions = [
         updates[member_index][2] + DECAY_RATE * masters[member_index] for member_index in range(4)
@@ -294,7 +309,18 @@
         ],
         axis=2,
     )
-    matrix_norms = jnp.sqrt(lax.psum(local_squares, ("dp", "fsdp")))
+    message = jnp.concatenate(
+        [
+            norm_parts.reshape(shards, -1),
+            jnp.broadcast_to(local_squares.reshape(1, 16), (shards, 16)),
+        ],
+        axis=1,
+    )
+    arrived = jnp.sum(lax.all_to_all(message, axes, 0, 0, tiled=True), axis=0)
+    matrix_norms = jnp.sqrt(arrived[-16:].reshape(2, 4, 2))
+    updates.append(
+        adam_parts(arrived[:-16].reshape(2, 2, 2, rows), firsts[4], seconds[4])
+    )
     updated = [
         masters[member_index]
         - RATE

time: 1840 us -> 699 us (0.38)
  waiting for transfers between devices: 1260 us -> 325 us
  blocking collectives: 206 us -> 0 us
  matrix products: 180 us -> 130 us
  local copies, waits for them, and re-layouts: 133 us -> 168 us
    reduce_scatter x8 -> x2, waiting for transfers between devices: 1040 us -> 189 us  [body(): summed = lax.psum_scatter(packed, axes, scatter_dimension=0, tiled=False)]
    all_gather x4 -> x0, blocking collectives: 169 us -> none  [the longest x2 85.9 us: fetch_forward(): lax.all_gather(part_out, ('dp', 'fsdp'), axis=0, tiled=True)]
    unnamed x18 -> x4, waiting for transfers between devices: 166 us -> 0.07 us
    all_gather x6 -> x2, waiting for transfers between devices: 54.9 us -> 135 us  [body(): packed = lax.all_gather(packed, axes, axis=0)]
    psum x1 -> x0, blocking collectives: 36.9 us -> none  [body(): matrix_norms = jnp.sqrt(lax.psum(local_squares, ('dp', 'fsdp')))]
  transfers between devices with their start and end apart: 16 -> 5, of which waited for: 12 -> 5; matrix products, arithmetic and copies ran while one was open for 12% -> 8% of each run, Pallas kernels for 0% -> 0%
where the time goes in v1:
time: 699 us; the launch traced here: 688 us
  waiting for transfers between devices  325 us (46%)
  local copies, waits for them, and re-layouts  168 us (24%)
  matrix products  130 us (19%)
  other arithmetic  43.4 us (6%)
  between operations  16.9 us (2%)
    reduce_scatter x2, waiting for transfers between devices, body(): summed = lax.psum_scatter(packed, axes, scatter_dimension=0, tiled=False)  189 us
    all_gather x2, waiting for transfers between devices, body(): packed = lax.all_gather(packed, axes, axis=0)  135 us
    unnamed x322, local copies, waits for them, and re-layouts  36.4 us
    another operation x6, local copies, waits for them, and re-layouts  14.7 us
  transfers between devices with their start and end apart: 5, of which 5 were waited for; matrix products, arithmetic and copies ran while one was open for 8% of the time, Pallas kernels for 0%

profile of v1, /device:TPU:0, one launch (start us, length us, event | category | flops | bytes accessed | tf_op | source)
XLA Modules:
  0.0 687.7 jit_solution(4904288197825771096)
XLA Ops:
  15.4 68.8 %all-gather.4.cloned.1.call-done = bf16[32,192,512]{2,1,0:T(8,128)(2,1)} async-done(((bf16[1,192,512]{2,1,0:T(8,128)(2,1)}), bf16[32,192,512]{2,1,0:T(8,128)(2,1)}) %all-gather.4.cloned.1.call-update) | async-done | bytes 6291472 | tf_op jit(solution)/shard_map/all_gather | solution.py:259
  91.6 66.2 %all-gather.6.cloned.1.call-done = bf16[6656,512]{1,0:T(8,128)(2,1)} async-done(((bf16[208,512]{1,0:T(8,128)(2,1)}), bf16[6656,512]{1,0:T(8,128)(2,1)}) %all-gather.6.cloned.1.call-update) | async-done | bytes 6815760 | tf_op jit(solution)/shard_map/all_gather | solution.py:259
  182.1 4.3 copy.179
  203.6 6.2 multiply_convert_fusion.1
  228.7 6.7 fusion.40
  252.1 4.8 multiply_convert_fusion
  256.9 5.3 fusion.5
  272.6 7.8 %convert_bitcast_fusion = bf16[1,17,64,8,64]{4,1,3,2,0:T(8,128)(2,1)} fusion(f32[64,8,17]{2,1,0:T(8,128)S(1)} %copy-done.41, f32[64,8,17,17]{2,3,1,0:T(8,128)} %copy-done.1, pred[17,17]{0,1:T(8,128)(4,1)S(1)} %fusion.94, bf16[17,64,8,64]{3,2,1,0:T(8,128)(2,1)} %reshape.797), kind=kOutput, calls=%fused_computation.70 | convolution fusion | flops 20088832 | bytes 2855201 | tf_op jit(solution)/shard_map/cphqk,cqphd->ckphd/dot_general | solution.py:88
  280.5 5.0 multiply_reduce_fusion
  322.4 4.4 convolution_convert_fusion.5
  326.9 4.9 fusion.10
  335.6 4.7 convolution_convert_fusion.6
  348.8 4.4 copy.183
  353.2 5.7 convert_bitcast_fusion.2
  372.6 4.3 copy.185
  377.0 4.3 reshape.804
  381.3 4.9 copy.178
  390.3 4.9 copy.182
  416.8 4.4 convolution_convert_fusion.4
  424.1 6.5 convolution_convert_fusion.3
  443.6 4.7 fusion.59
  456.9 70.5 %reduce-scatter.3.cloned.1.call-done = bf16[1,192,512]{2,1,0:T(8,128)(2,1)} async-done(((bf16[32,192,512]{2,1,0:T(8,128)(2,1)}), bf16[1,192,512]{2,1,0:T(8,128)(2,1)}) %reduce-scatter.3.cloned.1.call-update) | async-done | bytes 196624 | tf_op jit(solution)/shard_map/reduce_scatter | solution.py:287
  528.4 119.0 %reduce-scatter.5.cloned.1.call-done = bf16[1,192,512]{2,1,0:T(8,128)(2,1)} async-done(((bf16[32,192,512]{2,1,0:T(8,128)(2,1)}), bf16[1,192,512]{2,1,0:T(8,128)(2,1)}) %reduce-scatter.5.cloned.1.call-update) | async-done | bytes 196624 | tf_op jit(solution)/shard_map/reduce_scatter | solution.py:287
  664.7 6.4 fusion.38
  (499 shorter events, 241.6 us)
Async XLA Ops:
  7.2 77.0 %all-gather.4.cloned.1.call-start = ((), (), s32[]{:S(2)}) async-start(), calls=%async_computation.3 | async-start | bytes 6488064 | tf_op jit(solution)/shard_map/all_gather | solution.py:259
  11.9 145.9 %all-gather.6.cloned.1.call-start = ((), (), s32[]{:S(2)}) async-start(), calls=%async_computation.6 | async-start | bytes 7028736 | tf_op jit(solution)/shard_map/all_gather | solution.py:259
  13.6 513.8 %reduce-scatter.3.cloned.1.call-start = ((), (), s32[]{:S(2)}) async-start(), calls=%async_computation.4 | async-start | bytes 6488064 | tf_op jit(solution)/shard_map/reduce_scatter | solution.py:287
  14.7 151.5 %copy-start.89 = (f32[1088]{0:T(1024)}, f32[1088]{0:T(1024)S(1)}, u32[]{:S(2)}) copy-start(f32[1088]{0:T(1024)S(1)} %broadcast_multiply_fusion.3) | copy-start | bytes 13060
  15.3 76.3 %copy-start.96 = (f32[1088]{0:T(1024)}, f32[1088]{0:T(1024)S(1)}, u32[]{:S(2)}) copy-start(f32[1088]{0:T(1024)S(1)} %fusion.58) | copy-start | bytes 13060
  15.4 150.8 %copy-start.98 = (f32[1088]{0:T(1024)}, f32[1088]{0:T(1024)S(1)}, u32[]{:S(2)}) copy-start(f32[1088]{0:T(1024)S(1)} %fusion.96) | copy-start | bytes 13060
  165.9 47.0 %copy-start.102 = (f32[1,1,512]{2,1,0:T(1,128)}, f32[1,1,512]{2,1,0:T(1,128)S(1)}, u32[]{:S(2)}) copy-start(f32[1,1,512]{2,1,0:T(1,128)S(1)} %get-tuple-element.217) | copy-start | bytes 6148
  165.9 84.4 %copy-start.124 = (f32[1,1,512]{2,1,0:T(1,128)}, f32[1,1,512]{2,1,0:T(1,128)S(1)}, u32[]{:S(2)}) copy-start(f32[1,1,512]{2,1,0:T(1,128)S(1)} %get-tuple-element.216) | copy-start | bytes 6148
  165.9 100.0 %copy-start.112 = (f32[1,1,512]{2,1,0:T(1,128)}, f32[1,1,512]{2,1,0:T(1,128)S(1)}, u32[]{:S(2)}) copy-start(f32[1,1,512]{2,1,0:T(1,128)S(1)} %get-tuple-element.215) | copy-start | bytes 6148
  165.9 154.0 %copy-start.92 = (f32[1,1,512]{2,1,0:T(1,128)}, f32[1,1,512]{2,1,0:T(1,128)S(1)}, u32[]{:S(2)}) copy-start(f32[1,1,512]{2,1,0:T(1,128)S(1)} %get-tuple-element.218) | copy-start | bytes 6148
  166.2 35.6 %copy-start.114 = (f32[1,1,512]{2,1,0:T(1,128)}, f32[1,1,512]{2,1,0:T(1,128)S(1)}, u32[]{:S(2)}) copy-start(f32[1,1,512]{2,1,0:T(1,128)S(1)} %get-tuple-element.219) | copy-start | bytes 6148
  166.2 35.6 %copy-start.128 = (f32[1,1,512]{2,1,0:T(1,128)}, f32[1,1,512]{2,1,0:T(1,128)S(1)}, u32[]{:S(2)}) copy-start(f32[1,1,512]{2,1,0:T(1,128)S(1)} %get-tuple-element.220) | copy-start | bytes 6148
  212.4 35.1 %copy-start.2 = (f32[1088,512]{1,0:T(8,128)}, f32[1088,512]{1,0:T(8,128)S(1)}, u32[]{:S(2)}) copy-start(f32[1088,512]{1,0:T(8,128)S(1)} %get-tuple-element.230) | copy-start | bytes 6684676
  249.8 16.2 %copy-start.10 = (f32[1088,512]{1,0:T(8,128)}, f32[1088,512]{1,0:T(8,128)S(1)}, u32[]{:S(2)}) copy-start(f32[1088,512]{1,0:T(8,128)S(1)} %get-tuple-element.234) | copy-start | bytes 6684676
  249.9 16.1 %copy-start.94 = (f32[1088]{0:T(1024)}, f32[1088]{0:T(1024)S(1)}, u32[]{:S(2)}) copy-start(f32[1088]{0:T(1024)S(1)} %broadcast_multiply_fusion) | copy-start | bytes 13060
  250.4 15.6 %copy-start.104 = (f32[1088]{0:T(1024)}, f32[1088]{0:T(1024)S(1)}, u32[]{:S(2)}) copy-start(f32[1088]{0:T(1024)S(1)} %fusion.99) | copy-start | bytes 13060
  414.1 233.3 %reduce-scatter.5.cloned.1.call-start = ((), (), s32[]{:S(2)}) async-start(), calls=%async_computation.5 | async-start | bytes 6488064 | tf_op jit(solution)/shard_map/reduce_scatter | solution.py:287
  423.2 14.2 %slice-start.9 = ((s8[4456448]{0:T(1024)(128)(4,1)}), s8[4194304]{0:T(1024)(128)(4,1)S(1)}, s32[]{:S(2)}) async-start(s8[4456448]{0:T(1024)(128)(4,1)} %bitcast.366), calls=%async_computation.16 | async-start | bytes 8388608
  456.9 193.2 %copy-start.62 = (f32[2,16,512]{2,1,0:T(8,128)S(1)}, f32[2,16,512]{2,1,0:T(8,128)}, u32[]{:S(2)}) copy-start(f32[2,16,512]{2,1,0:T(8,128)} %param.22) | copy-start | bytes 196612
  456.9 195.3 %copy-start.51 = (f32[2,16,1536]{2,1,0:T(8,128)S(1)}, f32[2,16,1536]{2,1,0:T(8,128)}, u32[]{:S(2)}) copy-start(f32[2,16,1536]{2,1,0:T(8,128)} %param.21) | copy-start | bytes 589828
  456.9 197.7 %copy-start.50 = (f32[2,16,2048]{2,1,0:T(8,128)S(1)}, f32[2,16,2048]{2,1,0:T(8,128)}, u32[]{:S(2)}) copy-start(f32[2,16,2048]{2,1,0:T(8,128)} %param.23) | copy-start | bytes 786436
  654.6 21.5 %copy-start.59 = (f32[2,16,1536]{2,1,0:T(8,128)}, f32[2,16,1536]{2,1,0:T(8,128)S(1)}, u32[]{:S(2)}) copy-start(f32[2,16,1536]{2,1,0:T(8,128)S(1)} %get-tuple-element.145) | copy-start | bytes 589828
  657.1 22.7 %copy-start.57 = (f32[2,16,2048]{2,1,0:T(8,128)}, f32[2,16,2048]{2,1,0:T(8,128)S(1)}, u32[]{:S(2)}) copy-start(f32[2,16,2048]{2,1,0:T(8,128)S(1)} %get-tuple-element.149) | copy-start | bytes 786436
  660.5 11.5 %all-to-all-start = ((f32[32,1,144]{2,1,0:T(1,128)}), f32[32,1,144]{2,1,0:T(1,128)}, u32[]{:S(2)}, u32[]{:S(2)}) async-start(f32[32,1,144]{2,1,0:T(1,128)} %all_to_all.6), calls=%async_computation.2 | async-start | bytes 65536 | tf_op jit(solution)/shard_map/all_to_all | solution.py:319
  (124 other events, 461.7 us)
Sparse Core Ops, SparseCore 0:
  12.0 72.1 all-gather.3
  87.6 70.1 all-gather.5
  414.2 113.1 reduce-scatter.2
  533.8 113.5 reduce-scatter.4

commit v2 on v0

v2 whole, which is shorter than its diff:
```python
import jax
import jax.numpy as jnp
from jax import lax
from jax.experimental import pallas as pl
from jax.experimental.pallas import tpu as pltpu
from jax.sharding import PartitionSpec as P

HEADS = 8
HEAD_DIM = 64
FRAMES = 17
WIN = 64
STEP = 5
WIDTH = 512
BLOCKS = 32
SLAB = WIDTH // BLOCKS
TILES = 4
TILE = FRAMES * WIN // TILES
SPOTS = WIN // TILES
SCALE = HEAD_DIM ** (-0.5)
VMEM_BYTES = 56 * 2**20
COST = pl.CostEstimate(flops=10**8, bytes_accessed=10**5, transcendentals=0)

NORM_EPS = 1e-05
ADAM_EPS = 1e-06
BETA_FIRST = 0.5
BETA_SECOND = 0.5
RATE = 0.25
DECAY_RATE = 0.01
MASKED = -1e30


def row_norm(inputs):
    center = inputs - jnp.mean(inputs, axis=-1, keepdims=True)
    spread = jnp.mean(center * center, axis=-1, keepdims=True)
    scale = lax.rsqrt(spread + NORM_EPS)
    return center * scale, scale


def row_norm_back(grad, gain_row, normal, scale):
    scaled = grad * gain_row
    first = jnp.mean(scaled, axis=-1, keepdims=True)
    second = jnp.mean(scaled * normal, axis=-1, keepdims=True)
    return scale * (scaled - first - normal * second)


def fold_rows(array):
    return jnp.sum(array.reshape(-1, 8, array.shape[-1]), axis=0)


def gelu_pair(upward):
    bell = jnp.exp(-0.5 * upward * upward)
    place = 1.0 / (1.0 + 0.23164189 * jnp.abs(upward))
    tail = 0.5 * 1.061405429
    for factor in (-1.453152027, 1.421413741, -0.284496736, 0.254829592):
        tail = tail * place + 0.5 * factor
    tail = tail * place * bell
    cumulative = jnp.where(upward >= 0.0, 1.0 - tail, tail)
    return upward * cumulative, cumulative + 0.3989422804014327 * upward * bell


def dot_nn(left, right):
    return lax.dot_general(
        left, right, (((1,), (0,)), ((), ())), preferred_element_type=jnp.float32
    )


def dot_nt(left, right):
    return lax.dot_general(
        left, right, (((1,), (1,)), ((), ())), preferred_element_type=jnp.float32
    )


def dot_tn(left, right):
    return lax.dot_general(
        left, right, (((0,), (0,)), ((), ())), preferred_element_type=jnp.float32
    )


def slab(weights, index):
    return weights[:, SLAB * index : SLAB * index + SLAB, :].reshape(WIDTH, WIDTH)


def down_rows(weights, index):
    part = BLOCKS // 4
    return weights[part * index : part * index + part].reshape(WIDTH, WIDTH)


def weight_spec(array, index):
    return pl.BlockSpec(
        (BLOCKS, 4 * SLAB, WIDTH), lambda i: (0, index, 0), pipeline_mode=pl.Buffered(1)
    )


def stack_heads(pair):
    lane = lax.broadcasted_iota(jnp.int32, pair.shape, 1)
    zero = jnp.zeros_like(pair)
    return jnp.concatenate(
        [jnp.where(lane < HEAD_DIM, pair, zero), jnp.where(lane < HEAD_DIM, zero, pair)], axis=0
    )


def merge_heads(stacked):
    rows = stacked.shape[0] // 2
    lane = lax.broadcasted_iota(jnp.int32, (rows, 2 * HEAD_DIM), 1)
    return jnp.where(lane < HEAD_DIM, stacked[:rows], stacked[rows:])


def soft_weights(scores):
    raised = jnp.exp(scores - jnp.max(scores, axis=-1, keepdims=True))
    return raised * (1.0 / jnp.sum(raised, axis=-1, keepdims=True))


def attention_grads(weights, out_grad, queries, keys, values):
    value_grad = dot_tn(weights.astype(jnp.bfloat16), out_grad)
    weight_grad = dot_nt(out_grad, values)
    weights = weights.astype(jnp.float32)
    total = jnp.sum(weight_grad * weights, axis=-1, keepdims=True)
    score_grad = (weights * (weight_grad - total)).astype(jnp.bfloat16)
    query_grad = merge_heads(dot_nn(score_grad, keys)) * SCALE
    key_grad = dot_tn(score_grad, queries)
    return query_grad, key_grad, value_grad


def first_attention_kernel(
    tokens, weights, gains, normed_out, projected_out, probs, attended, middle_out, hidden_in_out,
    projected,
):
    step = pl.program_id(0)

    @pl.when(step < TILES)
    def _():
        normal, _ = row_norm(tokens[...].astype(jnp.float32))
        normed = (normal * gains[0:1, :] + gains[1:2, :]).astype(jnp.bfloat16)
        normed_out[...] = normed
        rows = pl.ds(pl.multiple_of(step * TILE, TILE), TILE)
        for index in range(3):
            part = dot_nn(normed, slab(weights, index)).astype(jnp.bfloat16)
            projected[rows, WIDTH * index : WIDTH * index + WIDTH] = part
            projected_out[:, WIDTH * index : WIDTH * index + WIDTH] = part

    @pl.when(step == TILES)
    def _():
        def one_frame(frame, carry):
            rows = pl.ds(pl.multiple_of(frame * WIN, WIN), WIN)
            for pair in range(HEADS // 2):
                lanes = 128 * pair
                queries = stack_heads(projected[rows, lanes : lanes + 128] * SCALE)
                keys = projected[rows, WIDTH + lanes : WIDTH + lanes + 128]
                values = projected[rows, 2 * WIDTH + lanes : 2 * WIDTH + lanes + 128]
                share = soft_weights(dot_nt(queries, keys)).astype(jnp.bfloat16)
                probs[frame, pair] = share
                attended[rows, lanes : lanes + 128] = merge_heads(dot_nn(share, values)).astype(
                    jnp.bfloat16
                )
            return carry

        lax.fori_loop(0, FRAMES, one_frame, 0)

    @pl.when(step > TILES)
    def _():
        rows = pl.ds(pl.multiple_of((step - TILES - 1) * TILE, TILE), TILE)
        middle = tokens[...].astype(jnp.float32) + dot_nn(attended[rows, :], slab(weights, 3))
        middle_out[...] = middle
        normal, _ = row_norm(middle)
        hidden_in_out[...] = (normal * gains[2:3, :] + gains[3:4, :]).astype(jnp.bfloat16)


def first_attention(tokens, weights, gains):
    count = tokens.shape[0]

    def early(width):
        return pl.BlockSpec((TILE, width), lambda i: (jnp.minimum(i, TILES - 1), 0))

    def late(width):
        return pl.BlockSpec((TILE, width), lambda i: (jnp.maximum(i - TILES - 1, 0), 0))

    def whole_out(*shape):
        return pl.BlockSpec(shape, lambda i: (0,) * len(shape))

    def out(width, kind):
        return jax.ShapeDtypeStruct((count, width), kind)

    return pl.pallas_call(
        first_attention_kernel,
        grid=(2 * TILES + 1,),
        in_specs=[
            pl.BlockSpec(
                (TILE, WIDTH), lambda i: (jnp.where(i < TILES, i, jnp.maximum(i - TILES - 1, 0)), 0)
            ),
            weight_spec(weights, 0),
            whole_out(4, WIDTH),
        ],
        out_specs=[
            early(WIDTH),
            early(3 * WIDTH),
            whole_out(FRAMES, HEADS // 2, 2 * WIN, WIN),
            whole_out(count, WIDTH),
            late(WIDTH),
            late(WIDTH),
        ],
        out_shape=[
            out(WIDTH, jnp.bfloat16),
            out(3 * WIDTH, jnp.bfloat16),
            jax.ShapeDtypeStruct((FRAMES, HEADS // 2, 2 * WIN, WIN), jnp.bfloat16),
            out(WIDTH, jnp.bfloat16),
            out(WIDTH, jnp.float32),
            out(WIDTH, jnp.bfloat16),
        ],
        scratch_shapes=[pltpu.VMEM((count, 3 * WIDTH), jnp.bfloat16)],
        compiler_params=pltpu.CompilerParams(vmem_limit_bytes=VMEM_BYTES),
        cost_estimate=COST,
        name="first_attention",
    )(tokens, weights, gains)


def first_mlp_kernel(middle, hidden_in, weights_up, weights_down, hidden_out, slope_out, result_out):
    result = middle[...]
    for index in range(4):
        columns = slice(WIDTH * index, WIDTH * index + WIDTH)
        value, slope = gelu_pair(dot_nn(hidden_in[...], slab(weights_up, index)))
        hidden = value.astype(jnp.bfloat16)
        hidden_out[:, columns] = hidden
        slope_out[:, columns] = slope.astype(jnp.bfloat16)
        result = result + dot_nn(hidden, down_rows(weights_down, index))
    result_out[...] = result


def first_mlp(middle, hidden_in, weights, weights_at):
    count = middle.shape[0]

    def tile(width):
        return pl.BlockSpec((TILE, width), lambda i: (i, 0))

    return pl.pallas_call(
        first_mlp_kernel,
        grid=(TILES,),
        in_specs=[
            tile(WIDTH),
            tile(WIDTH),
            weight_spec(weights, weights_at),
            weight_spec(weights, weights_at + 1),
        ],
        out_specs=[tile(4 * WIDTH), tile(4 * WIDTH), tile(WIDTH)],
        out_shape=[
            jax.ShapeDtypeStruct((count, 4 * WIDTH), jnp.bfloat16),
            jax.ShapeDtypeStruct((count, 4 * WIDTH), jnp.bfloat16),
            jax.ShapeDtypeStruct((count, WIDTH), jnp.float32),
        ],
        compiler_params=pltpu.CompilerParams(vmem_limit_bytes=VMEM_BYTES),
        cost_estimate=COST,
        name="first_mlp",
    )(middle, hidden_in, weights, weights)


def second_kernel(
    frame_count, inputs, cotangent, weights, weights_up, weights_down, gains, result_out, grad_out, normed_out, projected_grad_out,
    attended_out, branch_grad_out, hidden_in_out, up_grad_out, hidden_out, sums, caps, projected,
    slopes,
):
    @pl.when(pl.program_id(0) == 0)
    def _():
        row = lax.broadcasted_iota(jnp.int32, caps.shape, 0)
        column = lax.broadcasted_iota(jnp.int32, caps.shape, 1)
        late, soon = row // SPOTS, column // SPOTS
        video = (late < frame_count[0]) & (soon < frame_count[0])
        allowed = (row % SPOTS == column % SPOTS) & ((soon == late) | ((soon < late) & video))
        caps[...] = jnp.where(allowed, 3.0e38, MASKED)
        sums[...] = jnp.zeros_like(sums)

    def flat(ref):
        return ref[...].reshape(TILE, ref.shape[-1])

    def keep(ref, value):
        ref[...] = value.reshape(ref.shape).astype(ref.dtype)

    inside = lax.broadcasted_iota(jnp.int32, (TILE, 1), 0) // SPOTS < frame_count[0]
    gate = jnp.where(inside, 1.0, 0.0)
    stream = flat(inputs)
    normal_first, scale_first = row_norm(stream)
    normed = (normal_first * gains[0:1, :] + gains[1:2, :]).astype(jnp.bfloat16)
    keep(normed_out, normed)
    for index in range(3):
        part = dot_nn(normed, slab(weights, index))
        projected[:, WIDTH * index : WIDTH * index + WIDTH] = (
            part * SCALE if index == 0 else part
        ).astype(jnp.bfloat16)
    for pair in range(HEADS // 2):
        lanes = 128 * pair
        queries = stack_heads(projected[:, lanes : lanes + 128])
        keys = projected[:, WIDTH + lanes : WIDTH + lanes + 128]
        values = projected[:, 2 * WIDTH + lanes : 2 * WIDTH + lanes + 128]
        scores = dot_nt(queries, keys)
        cap = caps[...]
        share = soft_weights(jnp.minimum(scores, jnp.concatenate([cap, cap], axis=0)))
        part = merge_heads(dot_nn(share.astype(jnp.bfloat16), values)).astype(jnp.bfloat16)
        attended_out[:, :, lanes : lanes + 128] = part.reshape(FRAMES, SPOTS, 128)
    attended = flat(attended_out)
    middle = stream + gate * dot_nn(attended, slab(weights, 3))
    normal_second, scale_second = row_norm(middle)
    hidden_in = (normal_second * gains[2:3, :] + gains[3:4, :]).astype(jnp.bfloat16)
    keep(hidden_in_out, hidden_in)
    result = middle
    for index in range(4):
        columns = slice(WIDTH * index, WIDTH * index + WIDTH)
        value, slope = gelu_pair(dot_nn(hidden_in, slab(weights_up, index)))
        hidden = value.astype(jnp.bfloat16)
        hidden_out[:, :, columns] = hidden.reshape(FRAMES, SPOTS, WIDTH)
        slopes[:, columns] = slope
        result = result + dot_nn(hidden, down_rows(weights_down, index))
    keep(result_out, result)

    out_grad = flat(cotangent)
    hidden_in_grad = jnp.zeros((TILE, WIDTH), jnp.float32)
    for index in range(4):
        columns = slice(WIDTH * index, WIDTH * index + WIDTH)
        up_grad = (dot_nt(out_grad, down_rows(weights_down, index)) * slopes[:, columns]).astype(
            jnp.bfloat16
        )
        up_grad_out[:, :, columns] = up_grad.reshape(FRAMES, SPOTS, WIDTH)
        hidden_in_grad = hidden_in_grad + dot_nt(up_grad, slab(weights_up, index))
    sums[2] += fold_rows(hidden_in_grad * normal_second)
    sums[3] += fold_rows(hidden_in_grad)
    middle_grad = out_grad.astype(jnp.float32) + row_norm_back(
        hidden_in_grad, gains[2:3, :], normal_second, scale_second
    )
    branch_grad = (middle_grad * gate).astype(jnp.bfloat16)
    keep(branch_grad_out, branch_grad)
    attended_grad = dot_nt(branch_grad, slab(weights, 3)).astype(jnp.bfloat16)
    for pair in range(HEADS // 2):
        lanes = 128 * pair
        queries = stack_heads(projected[:, lanes : lanes + 128])
        keys = projected[:, WIDTH + lanes : WIDTH + lanes + 128]
        values = projected[:, 2 * WIDTH + lanes : 2 * WIDTH + lanes + 128]
        scores = dot_nt(queries, keys)
        cap = caps[...]
        share = soft_weights(jnp.minimum(scores, jnp.concatenate([cap, cap], axis=0)))
        parts = attention_grads(
            share, stack_heads(attended_grad[:, lanes : lanes + 128]), queries, keys, values
        )
        for index in range(3):
            start = WIDTH * index + lanes
            projected_grad_out[:, :, start : start + 128] = (
                parts[index].astype(jnp.bfloat16).reshape(FRAMES, SPOTS, 128)
            )
    normed_grad = jnp.zeros((TILE, WIDTH), jnp.float32)
    for index in range(3):
        part = projected_grad_out[:, :, WIDTH * index : WIDTH * index + WIDTH]
        normed_grad = normed_grad + dot_nt(part.reshape(TILE, WIDTH), slab(weights, index))
    sums[0] += fold_rows(normed_grad * normal_first)
    sums[1] += fold_rows(normed_grad)
    keep(
        grad_out,
        middle_grad + row_norm_back(normed_grad, gains[0:1, :], normal_first, scale_first),
    )


def second_block(frame_counts, inputs, cotangent, weights, gains):
    def tile(width):
        return pl.BlockSpec((FRAMES, SPOTS, width), lambda i: (0, i, 0))

    def whole(*shape):
        return pl.BlockSpec(shape, lambda i: (0,) * len(shape), pipeline_mode=pl.Buffered(1))

    widths = (
        (1, jnp.bfloat16),
        (1, jnp.float32),
        (1, jnp.bfloat16),
        (3, jnp.bfloat16),
        (1, jnp.bfloat16),
        (1, jnp.bfloat16),
        (1, jnp.bfloat16),
        (4, jnp.bfloat16),
        (4, jnp.bfloat16),
    )
    outs = pl.pallas_call(
        second_kernel,
        grid=(WIN // SPOTS,),
        in_specs=[
            pl.BlockSpec(memory_space=pltpu.SMEM),
            tile(WIDTH),
            tile(WIDTH),
            weight_spec(weights, 0),
            weight_spec(weights, 1),
            weight_spec(weights, 2),
            whole(4, WIDTH),
        ],
        out_specs=[tile(width * WIDTH) for width, kind in widths]
        + [pl.BlockSpec((4, 8, WIDTH), lambda i: (0, 0, 0))],
        out_shape=[
            jax.ShapeDtypeStruct((FRAMES, WIN, width * WIDTH), kind) for width, kind in widths
        ]
        + [jax.ShapeDtypeStruct((4, 8, WIDTH), jnp.float32)],
        scratch_shapes=[
            pltpu.VMEM((TILE, TILE), jnp.float32),
            pltpu.VMEM((TILE, 3 * WIDTH), jnp.bfloat16),
            pltpu.VMEM((TILE, 4 * WIDTH), jnp.float32),
        ],
        compiler_params=pltpu.CompilerParams(vmem_limit_bytes=VMEM_BYTES),
        cost_estimate=COST,
        name="second_block",
    )(
        frame_counts,
        inputs.reshape(FRAMES, WIN, WIDTH),
        cotangent.reshape(FRAMES, WIN, WIDTH),
        weights,
        weights,
        weights,
        gains,
    )
    return [array.reshape(FRAMES * WIN, -1) for array in outs[:-1]] + [outs[-1]]


def first_back_kernel(
    upstream, slopes, middle, weights, weights_up, weights_down, gains, out_grad_out, up_grad_out, branch_grad_out,
    attended_grad_out, middle_grad_out, sums,
):
    @pl.when(pl.program_id(0) == 0)
    def _():
        sums[...] = jnp.zeros_like(sums)

    out_grad = upstream[...].astype(jnp.bfloat16)
    out_grad_out[...] = out_grad
    hidden_in_grad = jnp.zeros((TILE, WIDTH), jnp.float32)
    for index in range(4):
        columns = slice(WIDTH * index, WIDTH * index + WIDTH)
        up_grad = (dot_nt(out_grad, down_rows(weights_down, index)) * slopes[:, columns]).astype(
            jnp.bfloat16
        )
        up_grad_out[:, columns] = up_grad
        hidden_in_grad = hidden_in_grad + dot_nt(up_grad, slab(weights_up, index))
    normal, scale = row_norm(middle[...])
    sums[0] += fold_rows(hidden_in_grad * normal)
    sums[1] += fold_rows(hidden_in_grad)
    middle_grad = upstream[...] + row_norm_back(hidden_in_grad, gains[2:3, :], normal, scale)
    middle_grad_out[...] = middle_grad
    branch_grad = middle_grad.astype(jnp.bfloat16)
    branch_grad_out[...] = branch_grad
    attended_grad_out[...] = dot_nt(branch_grad, slab(weights, 3)).astype(jnp.bfloat16)


def first_back(upstream, slopes, middle, weights, late_weights, late_at, gains):
    count = upstream.shape[0]

    def tile(width):
        return pl.BlockSpec((TILE, width), lambda i: (i, 0))

    def whole(*shape):
        return pl.BlockSpec(shape, lambda i: (0,) * len(shape), pipeline_mode=pl.Buffered(1))

    def out(width, kind):
        return jax.ShapeDtypeStruct((count, width), kind)

    return pl.pallas_call(
        first_back_kernel,
        grid=(TILES,),
        in_specs=[
            tile(WIDTH),
            tile(4 * WIDTH),
            tile(WIDTH),
            weight_spec(weights, 0),
            weight_spec(late_weights, late_at),
            weight_spec(late_weights, late_at + 1),
            whole(4, WIDTH),
        ],
        out_specs=[tile(WIDTH), tile(4 * WIDTH), tile(WIDTH), tile(WIDTH), tile(WIDTH)]
        + [pl.BlockSpec((2, 8, WIDTH), lambda i: (0, 0, 0))],
        out_shape=[
            out(WIDTH, jnp.bfloat16),
            out(4 * WIDTH, jnp.bfloat16),
            out(WIDTH, jnp.bfloat16),
            out(WIDTH, jnp.bfloat16),
            out(WIDTH, jnp.float32),
            jax.ShapeDtypeStruct((2, 8, WIDTH), jnp.float32),
        ],
        compiler_params=pltpu.CompilerParams(vmem_limit_bytes=VMEM_BYTES),
        cost_estimate=COST,
        name="first_back",
    )(upstream, slopes, middle, weights, late_weights, late_weights, gains)


def first_attention_back_kernel(projected, probs, attended_grad, projected_grad):
    def one_frame(frame, carry):
        rows = pl.ds(pl.multiple_of(frame * WIN, WIN), WIN)
        for pair in range(HEADS // 2):
            lanes = 128 * pair
            parts = attention_grads(
                probs[frame, pair],
                stack_heads(attended_grad[rows, lanes : lanes + 128]),
                stack_heads(projected[rows, lanes : lanes + 128] * SCALE),
                projected[rows, WIDTH + lanes : WIDTH + lanes + 128],
                projected[rows, 2 * WIDTH + lanes : 2 * WIDTH + lanes + 128],
            )
            for index in range(3):
                start = WIDTH * index + lanes
                projected_grad[rows, start : start + 128] = parts[index].astype(jnp.bfloat16)
        return carry

    lax.fori_loop(0, FRAMES, one_frame, 0)


def first_attention_back(projected, probs, attended_grad):
    return pl.pallas_call(
        first_attention_back_kernel,
        out_shape=jax.ShapeDtypeStruct(projected.shape, jnp.bfloat16),
        compiler_params=pltpu.CompilerParams(vmem_limit_bytes=VMEM_BYTES),
        cost_estimate=COST,
        name="first_attention_back",
    )(projected, probs, attended_grad)


def first_input_back_kernel(projected_grad, tokens, middle_grad, weights, gains, grad_out, sums):
    @pl.when(pl.program_id(0) == 0)
    def _():
        sums[...] = jnp.zeros_like(sums)

    normed_grad = jnp.zeros((TILE, WIDTH), jnp.float32)
    for index in range(3):
        part = projected_grad[:, WIDTH * index : WIDTH * index + WIDTH]
        normed_grad = normed_grad + dot_nt(part, slab(weights, index))
    normal, scale = row_norm(tokens[...].astype(jnp.float32))
    sums[0] += fold_rows(normed_grad * normal)
    sums[1] += fold_rows(normed_grad)
    grad_out[...] = middle_grad[...] + row_norm_back(normed_grad, gains[0:1, :], normal, scale)


def first_input_back(projected_grad, tokens, middle_grad, weights, gains):
    count = tokens.shape[0]

    def tile(width):
        return pl.BlockSpec((TILE, width), lambda i: (i, 0))

    def whole(*shape):
        return pl.BlockSpec(shape, lambda i: (0,) * len(shape), pipeline_mode=pl.Buffered(1))

    return pl.pallas_call(
        first_input_back_kernel,
        grid=(TILES,),
        in_specs=[
            tile(3 * WIDTH),
            tile(WIDTH),
            tile(WIDTH),
            whole(BLOCKS, 3 * SLAB, WIDTH),
            whole(4, WIDTH),
        ],
        out_specs=[tile(WIDTH), pl.BlockSpec((2, 8, WIDTH), lambda i: (0, 0, 0))],
        out_shape=[
            jax.ShapeDtypeStruct((count, WIDTH), jnp.float32),
            jax.ShapeDtypeStruct((2, 8, WIDTH), jnp.float32),
        ],
        compiler_params=pltpu.CompilerParams(vmem_limit_bytes=VMEM_BYTES),
        cost_estimate=COST,
        name="first_input_back",
    )(projected_grad, tokens, middle_grad, weights, gains)


def outer_kernel(core, left, right, mine, other):
    first = core[0] == 0
    for half in range(2):
        columns = slice(256 * half, 256 * half + 256)
        part = dot_tn(left[:, columns], right[...]).astype(jnp.bfloat16)
        blocks = mine.shape[0] // 2
        part = part.reshape(blocks, 2, -1, WIDTH)
        even, odd = part[:, 0], part[:, 1]
        place = slice(blocks * half, blocks * half + blocks)
        mine[place] = jnp.where(first, even, odd)
        other[place] = jnp.where(first, odd, even)


def outer_call(core, left, right, left_spec, right_spec, parts, out_spec, rows, name):
    count = left.shape[0]
    return pl.pallas_call(
        outer_kernel,
        grid=(parts,),
        in_specs=[pl.BlockSpec(memory_space=pltpu.SMEM), left_spec, right_spec],
        out_specs=[out_spec, out_spec],
        out_shape=[jax.ShapeDtypeStruct((BLOCKS // 2, rows, WIDTH), jnp.bfloat16)] * 2,
        compiler_params=pltpu.CompilerParams(vmem_limit_bytes=VMEM_BYTES),
        cost_estimate=COST,
        name=name,
    )(core, left, right)


def outer_columns(core, left, right, name):
    count, width = right.shape
    parts = width // WIDTH
    return outer_call(
        core,
        left,
        right,
        pl.BlockSpec((count, WIDTH), lambda i: (0, 0)),
        pl.BlockSpec((count, WIDTH), lambda i: (0, i)),
        parts,
        pl.BlockSpec((BLOCKS // 2, SLAB, WIDTH), lambda i: (0, i, 0)),
        SLAB * parts,
        name,
    )


def outer_rows(core, left, right, name):
    count, width = left.shape
    parts = width // WIDTH
    return outer_call(
        core,
        left,
        right,
        pl.BlockSpec((count, WIDTH), lambda i: (0, i)),
        pl.BlockSpec((count, WIDTH), lambda i: (0, 0)),
        parts,
        pl.BlockSpec((BLOCKS // 2 // parts, width // BLOCKS, WIDTH), lambda i: (i, 0, 0)),
        width // BLOCKS,
        name,
    )


def fold_cores_kernel(place, *refs):
    ins, outs = refs[:-4], refs[-4:]
    for which in range(4):

        @pl.when(pl.program_id(0) == which)
        def _(out=outs[which]):
            start = 0
            for index in range(0, len(ins), 2):
                rows = ins[index].shape[-2]
                out[:, start : start + rows, :] = (
                    ins[index][0].astype(jnp.float32) + ins[index + 1][0].astype(jnp.float32)
                ).astype(jnp.bfloat16)
                start += rows


def fold_cores(place, pairs, name):
    flat = [array.reshape(4, 4, -1, WIDTH) for pair in pairs for array in pair]
    total = sum(pair[0].shape[1] for pair in pairs)
    return pl.pallas_call(
        fold_cores_kernel,
        grid_spec=pltpu.PrefetchScalarGridSpec(
            num_scalar_prefetch=1,
            grid=(4,),
            in_specs=[
                pl.BlockSpec((1,) + array.shape[1:], lambda i, place: (place[0] ^ i, 0, 0, 0))
                for array in flat
            ],
            out_specs=[pl.BlockSpec((4, total, WIDTH), lambda i, place: (0, 0, 0))] * 4,
        ),
        out_shape=[jax.ShapeDtypeStruct((4, total, WIDTH), jnp.bfloat16)] * 4,
        compiler_params=pltpu.CompilerParams(vmem_limit_bytes=VMEM_BYTES),
        cost_estimate=COST,
        name=name,
    )(place, *flat)


def fold_planes_kernel(place, *refs):
    ins, outs = refs[:4], refs[4:]
    for which in range(4):
        block = place[1] ^ which
        total = ins[0][block].astype(jnp.float32)
        for ref in ins[1:]:
            total = total + ref[block].astype(jnp.float32)
        outs[which][...] = total.astype(jnp.bfloat16)


def fold_planes(place, pieces, name):
    total = pieces[0].shape[1]
    return pl.pallas_call(
        fold_planes_kernel,
        in_specs=[pl.BlockSpec(memory_space=pltpu.SMEM)]
        + [pl.BlockSpec(memory_space=pltpu.VMEM)] * 4,
        out_shape=[jax.ShapeDtypeStruct((total, WIDTH), jnp.bfloat16)] * 4,
        compiler_params=pltpu.CompilerParams(vmem_limit_bytes=VMEM_BYTES),
        cost_estimate=COST,
        name=name,
    )(place, *pieces)


def arrange_kernel(place, *refs):
    ins, out = refs[:-1], refs[-1]
    across, plane, core = place[0], place[1], place[2]
    for index, ref in enumerate(ins):
        column = (across ^ (index % 4)) * 8 + (core ^ (index // 4))
        for way in range(4):
            out[column + (plane ^ way) * 2] = ref[way]


def arrange(place, pieces, name):
    rows = pieces[0].shape[1]
    return pl.pallas_call(
        arrange_kernel,
        in_specs=[pl.BlockSpec(memory_space=pltpu.SMEM)]
        + [pl.BlockSpec(memory_space=pltpu.VMEM)] * 8,
        out_shape=jax.ShapeDtypeStruct((BLOCKS, rows, WIDTH), jnp.bfloat16),
        compiler_params=pltpu.CompilerParams(vmem_limit_bytes=VMEM_BYTES),
        cost_estimate=COST,
        name=name,
    )(place, *pieces)


def adam_parts(gradient, first_moment, second_moment):
    first_next = BETA_FIRST * first_moment + (1.0 - BETA_FIRST) * gradient
    second_next = BETA_SECOND * second_moment + (1.0 - BETA_SECOND) * gradient * gradient
    direction = (
        first_next
        / (1.0 - BETA_FIRST**STEP)
        / (jnp.sqrt(second_next / (1.0 - BETA_SECOND**STEP)) + ADAM_EPS)
    )
    return (first_next, second_next, direction)


def pack_weights(part_qkv, part_out, part_up, part_down):
    return jnp.concatenate(
        [part_qkv[:, WIDTH * i : WIDTH * i + WIDTH] for i in range(3)]
        + [part_out]
        + [part_up[:, WIDTH * i : WIDTH * i + WIDTH] for i in range(4)]
        + [part_down],
        axis=0,
    ).astype(jnp.bfloat16)


def to_blocks(packed, rows):
    if rows == SLAB:
        return packed
    packed = packed[:, : 12 * rows]
    slabs = packed[:, : 8 * rows].reshape(BLOCKS, -1, 8, rows, WIDTH).transpose(0, 2, 1, 3, 4)
    return jnp.concatenate(
        [
            slabs.reshape(BLOCKS, 8 * SLAB, WIDTH),
            packed[:, 8 * rows :].reshape(BLOCKS, 4 * SLAB, WIDTH),
        ],
        axis=1,
    )


def from_blocks(grads, rows, narrow):
    if rows == SLAB:
        return grads
    slabs = grads[:, : narrow * SLAB].reshape(BLOCKS, narrow, -1, rows, WIDTH)
    slabs = slabs.transpose(0, 2, 1, 3, 4).reshape(-1, narrow * rows, WIDTH)
    if grads.shape[1] == narrow * SLAB:
        return slabs
    wide = grads[:, narrow * SLAB :].reshape(slabs.shape[0], -1, WIDTH)
    return jnp.concatenate([slabs, wide], axis=1)


def swap(array, mask):
    count = lax.axis_size("dp") * lax.axis_size("fsdp")
    return lax.ppermute(array, ("dp", "fsdp"), [(device, device ^ mask) for device in range(count)])


def after(value, *others):
    return lax.optimization_barrier((value, *others))[0]


def gather_by_chips(shards):
    results = []
    steps = [(), ()]
    for shard in shards:
        shard = after(shard, *steps[0])
        steps[0] = [swap(shard, 2 * way) for way in (1, 2, 3)]
        pieces = after(jnp.stack([shard] + steps[0]), *steps[1])
        steps[1] = [swap(pieces, 8 * way) for way in (1, 2, 3)]
        results.append([pieces] + steps[1])
    return results


def gather_cores(pieces, place, name):
    return arrange(place, pieces + [swap(piece, 1) for piece in pieces], "arrange_" + name)


def scatter_cores(pairs, place, name):
    return fold_cores(place, [(mine, swap(other, 1)) for mine, other in pairs], "cores_" + name)


def scatter_chips(pieces, place, name, *others):
    pieces = [pieces[0]] + [swap(pieces[way], 8 * way) for way in (3, 1, 2)]
    pieces = [after(pieces[0], *others)] + pieces[1:]
    return fold_planes(place, pieces, "planes_" + name)


def scatter_planes(pieces):
    pieces = [pieces[0]] + [swap(pieces[way], 2 * way) for way in (3, 2, 1)]
    return sum(piece.astype(jnp.float32) for piece in pieces)


def scatter_whole(pairs, rows, narrow):
    grads = jnp.concatenate(
        [jnp.stack(pair, axis=1).reshape(BLOCKS, -1, WIDTH) for pair in pairs], axis=1
    )
    summed = lax.psum_scatter(
        from_blocks(grads, rows, narrow), ("dp", "fsdp"), scatter_dimension=0, tiled=False
    )
    return summed.astype(jnp.float32)


def body(
    tokens,
    frame_counts,
    cotangent,
    w_qkv,
    w_out,
    w_up,
    w_down,
    norm_params,
    first_qkv,
    first_out,
    first_up,
    first_down,
    first_norm,
    second_qkv,
    second_out,
    second_up,
    second_down,
    second_norm,
):
    masters = (w_qkv, w_out, w_up, w_down)
    axes = ("dp", "fsdp")
    shards = lax.axis_size("dp") * lax.axis_size("fsdp")
    rows = w_out.shape[1]
    by_chips = (lax.axis_size("dp"), lax.axis_size("fsdp")) == (4, 8)
    fsdp = lax.axis_index("fsdp")
    place = jnp.stack([lax.axis_index("dp"), fsdp // 2, fsdp % 2]).astype(jnp.int32)
    norm_rows = jnp.pad(
        norm_params.astype(jnp.bfloat16).reshape(1, -1), ((0, rows - 1), (0, WIDTH - 8 * rows))
    )
    shard = pack_weights(w_qkv[0], w_out[0], w_up[0], w_down[0])
    second_shard = pack_weights(w_qkv[1], w_out[1], w_up[1], w_down[1])
    if by_chips:
        early, late_pieces = gather_by_chips(
            [jnp.concatenate([shard[: 4 * rows], norm_rows], axis=0), shard[4 * rows :]]
        )
        early = gather_cores(early, place, "early")
        norm_values = early[:, 4 * rows, : 8 * rows]
    else:
        gathered = lax.all_gather(jnp.concatenate([shard, norm_rows], axis=0), axes, axis=0)
        norm_values = gathered[:, 12 * rows, : 8 * rows]
        early = to_blocks(gathered, rows)
    gains = norm_values.reshape(shards, 2, 4, rows)
    gains = gains.transpose(1, 2, 0, 3).reshape(2, 4, WIDTH).astype(jnp.float32)
    weights_second = to_blocks(lax.all_gather(second_shard, axes, axis=0), rows)

    normed, projected, probs, attended, middle, hidden_in = first_attention(tokens, early, gains[0])
    if by_chips:
        late_pieces = [after(piece, hidden_in) for piece in late_pieces]
        late, late_at = gather_cores(late_pieces, place, "late"), 0
    else:
        late, late_at = early, 1
    hidden, slopes, stream = first_mlp(middle, hidden_in, late, late_at)
    (
        block_out,
        upstream,
        normed_second,
        projected_grad_second,
        attended_second,
        branch_grad_second,
        hidden_in_second,
        up_grad_second,
        hidden_second,
        sums_second,
    ) = second_block(frame_counts, stream, cotangent, weights_second, gains[1])
    core = place[2:] if by_chips else jnp.zeros((1,), jnp.int32)
    up_pair = outer_columns(core, hidden_in_second, up_grad_second, "outer_up")
    down_pair = outer_rows(core, after(hidden_second, *up_pair), cotangent, "outer_down")
    qkv_pair = outer_columns(
        core, after(normed_second, *down_pair), projected_grad_second, "outer_qkv"
    )
    out_pair = outer_columns(
        core, after(attended_second, *qkv_pair), branch_grad_second, "outer_out"
    )
    pairs_second = [up_pair, out_pair, qkv_pair, down_pair]
    out_grad, up_grad, branch_grad, attended_grad, middle_grad, sums_late = first_back(
        after(upstream, *out_pair), slopes, middle, early, late, late_at, gains[0]
    )
    if by_chips:
        second = scatter_cores(pairs_second, place, "second")
        up_grad = after(up_grad, *second)
    up_pair = outer_columns(core, hidden_in, up_grad, "outer_up")
    down_pair = outer_rows(core, after(hidden, *up_pair), out_grad, "outer_down")
    out_pair = outer_columns(core, after(attended, *down_pair), branch_grad, "outer_out")
    pairs_first = [up_pair, out_pair, down_pair]
    if by_chips:
        first = scatter_cores(pairs_first, place, "first")
        attended_grad = after(attended_grad, *first)
    projected_grad = first_attention_back(projected, probs, attended_grad)
    if by_chips:
        second = scatter_chips(second, place, "second", projected_grad)
        normed = after(normed, *second)
    pairs_last = [outer_columns(core, normed, projected_grad, "outer_qkv")]
    if by_chips:
        first = scatter_chips(first, place, "first", *pairs_last[0])
        last = scatter_cores(pairs_last, place, "last")
        projected_grad = after(projected_grad, *last)
    tokens_grad, sums_early = first_input_back(
        projected_grad, tokens, middle_grad, early, gains[0]
    )
    if by_chips:
        last = scatter_chips(last, place, "last")
        reduced_second, reduced_first, reduced_last = (
            scatter_planes(pieces) for pieces in (second, first, last)
        )
    else:
        reduced_second = scatter_whole(pairs_second, rows, 8)
        reduced_first = scatter_whole(pairs_first, rows, 5)
        reduced_last = scatter_whole(pairs_last, rows, 3)

    def columns(packed, first, last):
        return jnp.concatenate(
            [packed[rows * index : rows * index + rows] for index in range(first, last)], axis=1
        )

    reduced_first = (
        columns(reduced_last, 0, 3),
        columns(reduced_first, 4, 5),
        columns(reduced_first, 0, 4),
        reduced_first[5 * rows :],
    )
    reduced_second = (
        columns(reduced_second, 5, 8),
        columns(reduced_second, 4, 5),
        columns(reduced_second, 0, 4),
        reduced_second[8 * rows :],
    )

    norm_parts = jnp.concatenate(
        [jnp.sum(part, axis=1) for part in (sums_early, sums_late, sums_second)]
    )
    norm_parts = norm_parts.reshape(8, shards, rows).transpose(1, 0, 2).reshape(shards, -1)
    stacked = [jnp.stack(pair) for pair in zip(reduced_first, reduced_second)]
    firsts = (first_qkv, first_out, first_up, first_down)
    seconds = (second_qkv, second_out, second_up, second_down)
    updates = [adam_parts(*parts) for parts in zip(stacked, firsts, seconds)]
    directions = [update[2] + DECAY_RATE * master for update, master in zip(updates, masters)]
    local_squares = jnp.stack(
        [
            jnp.stack([jnp.sum(matrix * matrix, axis=(1, 2)) for matrix in group], axis=1)
            for group in (masters, directions)
        ],
        axis=2,
    )
    message = jnp.concatenate(
        [norm_parts, jnp.broadcast_to(local_squares.reshape(1, 16), (shards, 16))], axis=1
    )
    arrived = jnp.sum(lax.all_to_all(message, axes, 0, 0, tiled=True), axis=0)
    matrix_norms = jnp.sqrt(arrived[-16:].reshape(2, 4, 2))
    norm_update = adam_parts(arrived[:-16].reshape(2, 2, 2, rows), first_norm, second_norm)
    updates.append(norm_update)
    updated = [
        masters[index]
        - RATE
        * (matrix_norms[:, index, 0] / matrix_norms[:, index, 1])[:, None, None]
        * directions[index]
        for index in range(4)
    ]
    return (
        block_out,
        tokens_grad,
        *updated,
        norm_params - RATE * norm_update[2],
        *(array.astype(jnp.bfloat16) for array in updated),
        *(update[0] for update in updates),
        *(update[1] for update in updates),
        matrix_norms,
    )


def solution(mesh):
    in_specs = (
        P(("dp", "fsdp"), None),
        P(("dp", "fsdp")),
        P(("dp", "fsdp"), None),
        P(None, ("dp", "fsdp"), None),
        P(None, ("dp", "fsdp"), None),
        P(None, ("dp", "fsdp"), None),
        P(None, ("dp", "fsdp"), None),
        P(None, None, None, ("dp", "fsdp")),
        P(None, ("dp", "fsdp"), None),
        P(None, ("dp", "fsdp"), None),
        P(None, ("dp", "fsdp"), None),
        P(None, ("dp", "fsdp"), None),
        P(None, None, None, ("dp", "fsdp")),
        P(None, ("dp", "fsdp"), None),
        P(None, ("dp", "fsdp"), None),
        P(None, ("dp", "fsdp"), None),
        P(None, ("dp", "fsdp"), None),
        P(None, None, None, ("dp", "fsdp")),
    )
    out_specs = (
        P(("dp", "fsdp"), None),
        P(("dp", "fsdp"), None),
        P(None, ("dp", "fsdp"), None),
        P(None, ("dp", "fsdp"), None),
        P(None, ("dp", "fsdp"), None),
        P(None, ("dp", "fsdp"), None),
        P(None, None, None, ("dp", "fsdp")),
        P(None, ("dp", "fsdp"), None),
        P(None, ("dp", "fsdp"), None),
        P(None, ("dp", "fsdp"), None),
        P(None, ("dp", "fsdp"), None),
        P(None, ("dp", "fsdp"), None),
        P(None, ("dp", "fsdp"), None),
        P(None, ("dp", "fsdp"), None),
        P(None, ("dp", "fsdp"), None),
        P(None, None, None, ("dp", "fsdp")),
        P(None, ("dp", "fsdp"), None),
        P(None, ("dp", "fsdp"), None),
        P(None, ("dp", "fsdp"), None),
        P(None, ("dp", "fsdp"), None),
        P(None, None, None, ("dp", "fsdp")),
        P(),
    )
    return jax.shard_map(body, mesh=mesh, in_specs=in_specs, out_specs=out_specs, check_vma=False)
```

time: 1840 us -> 371 us (0.20)
  waiting for transfers between devices: 1260 us -> 54.2 us
  Pallas kernels: 0 us -> 218 us
  blocking collectives: 206 us -> 10.7 us
  matrix products: 180 us -> 0 us
  local copies, waits for them, and re-layouts: 133 us -> 14.7 us
  starting transfers between devices: 1.04 us -> 43.4 us
  other arithmetic: 33.7 us -> 12.4 us
    reduce_scatter x8 -> x0, waiting for transfers between devices: 1040 us -> none  [the longest x2 284 us: reduce_grads(): lax.psum_scatter(grad_up, ('dp', 'fsdp'), scatter_dimension=0, tiled=True)]
    pallas_call x0 -> x22, Pallas kernels: none -> 218 us  [the longest x1 58 us: second_block(): pl.pallas_call(second_kernel, grid=(WIN // SPOTS,), in_specs=[pl.BlockSpe...]
    dot_general x36 -> x0, matrix products: 180 us -> none  [the longest x2 28 us: block_forward(): upward = jnp.dot(hidden_in, weight_up, preferred_element_type=jnp.float32)]
    all_gather x4 -> x0, blocking collectives: 169 us -> none  [the longest x2 85.9 us: fetch_forward(): lax.all_gather(part_out, ('dp', 'fsdp'), axis=0, tiled=True)]
    unnamed x18 -> x1, waiting for transfers between devices: 166 us -> 0.02 us
    all_gather x6 -> x1, waiting for transfers between devices: 54.9 us -> 0.01 us  [body(): weights_second = to_blocks(lax.all_gather(second_shard, axes, axis=0), rows)]
    ppermute x0 -> x46, waiting for transfers between devices: none -> 54.2 us  [swap(): lax.ppermute(array, ('dp', 'fsdp'), [(device, device ^ mask) for device i...]
    reshape x13 -> x4, local copies, waits for them, and re-layouts: 48.7 us -> 0.32 us  [the longest x2 0.15 us: body(): norm_parts.reshape(8, shards, rows).transpose(1, 0, 2).reshape(shards, -1)]
  transfers between devices with their start and end apart: 16 -> 47, of which waited for: 12 -> 17; matrix products, arithmetic and copies ran while one was open for 12% -> 2% of each run, Pallas kernels for 0% -> 32%
where the time goes in v2:
time: 371 us; the launch traced here: 369 us
  Pallas kernels  218 us (59%)
  waiting for transfers between devices  54.2 us (15%)
  starting transfers between devices  43.4 us (12%)
  between operations  15.5 us (4%)
  local copies, waits for them, and re-layouts  14.7 us (4%)
  other arithmetic  12.4 us (3%)
  blocking collectives  10.7 us (3%)
    pallas_call x1, Pallas kernels, second_block(): pl.pallas_call(second_kernel, grid=(WIN // SPOTS,), in_specs=[pl.BlockSpe...  58 us
    ppermute x46, waiting for transfers between devices, swap(): lax.ppermute(array, ('dp', 'fsdp'), [(device, device ^ mask) for device i...  54.2 us
    pallas_call x8, Pallas kernels, outer_call(): pl.pallas_call(outer_kernel, grid=(parts,), in_specs=[pl.BlockSpec(memory...  44.7 us
    ppermute x46, starting transfers between devices, swap(): lax.ppermute(array, ('dp', 'fsdp'), [(device, device ^ mask) for device i...  43.3 us
    pallas_call x1, Pallas kernels, first_attention_back(): pl.pallas_call(first_attention_back_kernel, out_shape=jax.ShapeDtypeStruc...  25 us
    pallas_call x1, Pallas kernels, first_attention(): pl.pallas_call(first_attention_kernel, grid=(2 * TILES + 1,), in_specs=[p...  24.6 us
    pallas_call x1, Pallas kernels, first_mlp(): pl.pallas_call(first_mlp_kernel, grid=(TILES,), in_specs=[tile(WIDTH), ti...  15.8 us
    pallas_call x3, Pallas kernels, fold_cores(): pl.pallas_call(fold_cores_kernel, grid_spec=pltpu.PrefetchScalarGridSpec(...  15.4 us
  transfers between devices with their start and end apart: 47, of which 17 were waited for; matrix products, arithmetic and copies ran while one was open for 2% of the time, Pallas kernels for 32%

profile of v2, /device:TPU:0, one launch (start us, length us, event | category | flops | bytes accessed | tf_op | source)
XLA Modules:
  0.0 369.4 jit_solution(11789823673027753953)
XLA Ops:
  12.6 5.1 %collective-permute-start.2 = (bf16[80,512]{1,0:T(8,128)(2,1)S(1)}, bf16[80,512]{1,0:T(8,128)(2,1)S(1)}, u32[]{:S(2)}, u32[]{:S(2)}) collective-permute-start(bf16[80,512]{1,0:T(8,128)(2,1)S(1)} %constant_dynamic-update-slice_fusion), channel_id=1, source_target_pairs={{0,6},{1,7},{2,4},{3,5},{4,2},{5,3},{6,0},{7,1},{8,14},{9,15},{10,... | collective-permute-start | bytes 245768 | tf_op jit(solution)/shard_map/ppermute | solution.py:744
  20.8 3.8 %collective-permute-done.1 = bf16[80,512]{1,0:T(8,128)(2,1)S(1)} collective-permute-done((bf16[80,512]{1,0:T(8,128)(2,1)S(1)}, bf16[80,512]{1,0:T(8,128)(2,1)S(1)}, u32[]{:S(2)}, u32[]{:S(2)}) %collective-permute-start.1) | collective-permute-done | bytes 81952 | tf_op jit(solution)/shard_map/ppermute | solution.py:744
  30.9 5.8 %collective-permute-done.12 = bf16[128,512]{1,0:T(8,128)(2,1)S(1)} collective-permute-done((bf16[128,512]{1,0:T(8,128)(2,1)S(1)}, bf16[128,512]{1,0:T(8,128)(2,1)S(1)}, u32[]{:S(2)}, u32[]{:S(2)}) %collective-permute-start.12) | collective-permute-done | bytes 131104 | tf_op jit(solution)/shard_map/ppermute | solution.py:744
  37.3 6.4 %collective-permute-done.11 = bf16[128,512]{1,0:T(8,128)(2,1)S(1)} collective-permute-done((bf16[128,512]{1,0:T(8,128)(2,1)S(1)}, bf16[128,512]{1,0:T(8,128)(2,1)S(1)}, u32[]{:S(2)}, u32[]{:S(2)}) %collective-permute-start.11) | collective-permute-done | bytes 131104 | tf_op jit(solution)/shard_map/ppermute | solution.py:744
  44.3 4.4 %collective-permute-done.10 = bf16[128,512]{1,0:T(8,128)(2,1)S(1)} collective-permute-done((bf16[128,512]{1,0:T(8,128)(2,1)S(1)}, bf16[128,512]{1,0:T(8,128)(2,1)S(1)}, u32[]{:S(2)}, u32[]{:S(2)}) %collective-permute-start.10) | collective-permute-done | bytes 131104 | tf_op jit(solution)/shard_map/ppermute | solution.py:744
  58.0 24.6 %first_attention.1 = (bf16[1088,512]{1,0:T(8,128)(2,1)}, bf16[1088,1536]{1,0:T(8,128)(2,1)}, bf16[17,4,128,64]{3,2,1,0:T(8,128)(2,1)}, bf16[1088,512]{1,0:T(8,12...) custom-call(bf16[1088,512]{1,0:T(8,128)(2,1)} %tokens.3, bf16[32,80,512]{2,1,0:T(8,128)(2,1)} %arrange_early.1.weights, ...), custom_call_target="tpu_custom_call" | custom-call | flops 100000000 | bytes 100000 | tf_op jit(solution)/shard_map/first_attention/pallas_call | solution.py:183
  87.2 4.4 %arrange_late.1.weights_up.weights_down = bf16[32,128,512]{2,1,0:T(8,128)(2,1)} custom-call(s32[3]{0:T(128)} %pad_add_fusion.place, bf16[4,128,512]{2,1,0:T(8,128)(2,1)} %copy-done.1, bf16[4,128,512]{2,1,0:T(8,128)(2,1)} %copy-done.26, bf16[4,128,512]{2,1,0:T(8,128)(2,1)} %copy-done.25, bf16[4,128,512]{2,1,0:T(8,128)(2,1)} %copy-done.24, ...), custom_call_target="tpu_custom_call" | custom-call | flops 100000000 | bytes 100000 | tf_op jit(solution)/shard_map/arrange_late/pallas_call | solution.py:685
  91.6 15.8 %first_mlp.1 = (bf16[1088,2048]{1,0:T(8,128)(2,1)}, bf16[1088,2048]{1,0:T(8,128)(2,1)}, f32[1088,512]{1,0:T(8,128)}) custom-call(f32[1088,512]{1,0:T(8,128)} %get-tuple-element.107.middle, bf16[1088,512]{1,0:T(8,128)(2,1)} %get-tuple-element.108.hidden_in.left, bf16[32,128,512]{2,1,0:T(8,128)(2,1)} %arrange_late.1.weights_up.weights_down, ...), custom_call_target="tpu_custom_call" | custom-call | flops 100000000 | bytes 100000 | tf_op jit(solution)/shard_map/first_mlp/pallas_call | solution.py:234
  107.4 58.0 %second_block.1 = (bf16[17,64,512]{2,1,0:T(8,128)(2,1)}, f32[17,64,512]{2,1,0:T(8,128)}, bf16[17,64,512]{2,1,0:T(8,128)(2,1)}, bf16[17,64,1536]{2,1,0:T(8,128)(2...) custom-call(s32[1]{0:T(128)S(6)} %copy.87.frame_count, ...), custom_call_target="tpu_custom_call" | custom-call | flops 100000000 | bytes 100000 | tf_op jit(solution)/shard_map/second_block/pallas_call | solution.py:375
  165.4 6.7 %outer_up.2 = (bf16[16,64,512]{2,1,0:T(8,128)(2,1)}, bf16[16,64,512]{2,1,0:T(8,128)(2,1)}) custom-call(s32[1]{0:T(128)} %bitcast.2.core, bf16[1088,512]{1,0:T(8,128)(2,1)} %bitcast.126, bf16[1088,2048]{1,0:T(8,128)(2,1)} %bitcast.119), custom_call_target="tpu_custom_call" | custom-call | flops 100000000 | bytes 100000 | tf_op jit(solution)/shard_map/outer_up/pallas_call | solution.py:571
  172.1 6.9 %outer_down.2 = (bf16[16,64,512]{2,1,0:T(8,128)(2,1)}, bf16[16,64,512]{2,1,0:T(8,128)(2,1)}) custom-call(s32[1]{0:T(128)} %bitcast.2.core, bf16[1088,2048]{1,0:T(8,128)(2,1)} %bitcast.118, bf16[1088,512]{1,0:T(8,128)(2,1)} %right.1), custom_call_target="tpu_custom_call" | custom-call | flops 100000000 | bytes 100000 | tf_op jit(solution)/shard_map/outer_down/pallas_call | solution.py:571
  179.5 5.6 %outer_qkv.2 = (bf16[16,48,512]{2,1,0:T(8,128)(2,1)}, bf16[16,48,512]{2,1,0:T(8,128)(2,1)}) custom-call(s32[1]{0:T(128)} %bitcast.2.core, bf16[1088,512]{1,0:T(8,128)(2,1)} %bitcast.125, bf16[1088,1536]{1,0:T(8,128)(2,1)} %bitcast.120), custom_call_target="tpu_custom_call" | custom-call | flops 100000000 | bytes 100000 | tf_op jit(solution)/shard_map/outer_qkv/pallas_call | solution.py:571
  188.8 12.6 %first_back.1 = (bf16[1088,512]{1,0:T(8,128)(2,1)}, bf16[1088,2048]{1,0:T(8,128)(2,1)}, bf16[1088,512]{1,0:T(8,128)(2,1)}, bf16[1088,512]{1,0:T(8,128)(2,1)}, f32[1088,512]{1,0:T(8,128)}, /*index=5*/f32[2,8,512]{2,1,0:T(8,128)}) custom-call(f32[1088,512]{1,0:T(8,128)} %bitcast.121, bf16[1088,2048]{1,0:T(8,128)(2,1)} %get-tuple-element.139.slopes, ...), custom_call_target="tpu_custom_call" | custom-call | flops 100000000 | bytes 100000 | tf_op jit(solution)/shard_map/first_back/pallas_call | solution.py:453
  203.1 6.1 %cores_second.1 = (bf16[4,192,512]{2,1,0:T(8,128)(2,1)}, bf16[4,192,512]{2,1,0:T(8,128)(2,1)}, bf16[4,192,512]{2,1,0:T(8,128)(2,1)}, bf16[4,192,512]{2,1,0:T(8,128)(2,1)}) custom-call(s32[3]{0:T(128)} %pad_add_fusion.place, bf16[4,4,64,512]{3,2,1,0:T(8,128)(2,1)} %bitcast.127, bf16[4,4,64,512]{3,2,1,0:T(8,128)(2,1)} %bitcast.131, ...), custom_call_target="tpu_custom_call" | custom-call | flops 100000000 | bytes 100000 | tf_op jit(solution)/shard_map/cores_second/pallas_call | solution.py:633
  209.2 6.6 %outer_up.3 = (bf16[16,64,512]{2,1,0:T(8,128)(2,1)}, bf16[16,64,512]{2,1,0:T(8,128)(2,1)}) custom-call(s32[1]{0:T(128)} %bitcast.2.core, bf16[1088,512]{1,0:T(8,128)(2,1)} %get-tuple-element.108.hidden_in.left, bf16[1088,2048]{1,0:T(8,128)(2,1)} %get-tuple-element.146.right), custom_call_target="tpu_custom_call" | custom-call | flops 100000000 | bytes 100000 | tf_op jit(solution)/shard_map/outer_up/pallas_call | solution.py:571
  215.8 6.7 %outer_down.3 = (bf16[16,64,512]{2,1,0:T(8,128)(2,1)}, bf16[16,64,512]{2,1,0:T(8,128)(2,1)}) custom-call(s32[1]{0:T(128)} %bitcast.2.core, bf16[1088,2048]{1,0:T(8,128)(2,1)} %get-tuple-element.151.left, bf16[1088,512]{1,0:T(8,128)(2,1)} %get-tuple-element.152.right), custom_call_target="tpu_custom_call" | custom-call | flops 100000000 | bytes 100000 | tf_op jit(solution)/shard_map/outer_down/pallas_call | solution.py:571
  231.4 5.3 %cores_first.1 = (bf16[4,144,512]{2,1,0:T(8,128)(2,1)}, bf16[4,144,512]{2,1,0:T(8,128)(2,1)}, bf16[4,144,512]{2,1,0:T(8,128)(2,1)}, bf16[4,144,512]{2,1,0:T(8,128)(2,1)}) custom-call(s32[3]{0:T(128)} %pad_add_fusion.place, bf16[4,4,64,512]{3,2,1,0:T(8,128)(2,1)} %bitcast.130, bf16[4,4,64,512]{3,2,1,0:T(8,128)(2,1)} %bitcast.134, ...), custom_call_target="tpu_custom_call" | custom-call | flops 100000000 | bytes 100000 | tf_op jit(solution)/shard_map/cores_first/pallas_call | solution.py:633
  236.7 25.0 %first_attention_back.1.right.projected_grad = bf16[1088,1536]{1,0:T(8,128)(2,1)} custom-call(bf16[1088,1536]{1,0:T(8,128)(2,1)} %get-tuple-element.117.projected, bf16[17,4,128,64]{3,2,1,0:T(8,128)(2,1)} %get-tuple-element.118.probs, bf16[1088,512]{1,0:T(8,128)(2,1)} %get-tuple-element.163.attended_grad), custom_call_target="tpu_custom_call" | custom-call | flops 100000000 | bytes 100000 | tf_op jit(solution)/shard_map/first_attention_back/pallas_call | solution.py:502
  279.5 5.7 %outer_qkv.3 = (bf16[16,48,512]{2,1,0:T(8,128)(2,1)}, bf16[16,48,512]{2,1,0:T(8,128)(2,1)}) custom-call(s32[1]{0:T(128)} %bitcast.2.core, bf16[1088,512]{1,0:T(8,128)(2,1)} %get-tuple-element.170.left, bf16[1088,1536]{1,0:T(8,128)(2,1)} %first_attention_back.1.right.projected_grad), custom_call_target="tpu_custom_call" | custom-call | flops 100000000 | bytes 100000 | tf_op jit(solution)/shard_map/outer_qkv/pallas_call | solution.py:571
  285.9 4.1 %collective-permute-done.41.refs_2_ = bf16[4,144,512]{2,1,0:T(8,128)(2,1)S(1)} collective-permute-done((bf16[4,144,512]{2,1,0:T(8,128)(2,1)}, bf16[4,144,512]{2,1,0:T(8,128)(2,1)S(1)}, u32[]{:S(2)}, u32[]{:S(2)}) %collective-permute-start.41) | collective-permute-done | bytes 589856 | tf_op jit(solution)/shard_map/ppermute | solution.py:744
  290.0 10.0 %collective-permute-done.42.refs_3_ = bf16[4,144,512]{2,1,0:T(8,128)(2,1)S(1)} collective-permute-done((bf16[4,144,512]{2,1,0:T(8,128)(2,1)}, bf16[4,144,512]{2,1,0:T(8,128)(2,1)S(1)}, u32[]{:S(2)}, u32[]{:S(2)}) %collective-permute-start.42) | collective-permute-done | bytes 589856 | tf_op jit(solution)/shard_map/ppermute | solution.py:744
  318.2 3.9 %cores_last.1 = (bf16[4,48,512]{2,1,0:T(8,128)(2,1)}, bf16[4,48,512]{2,1,0:T(8,128)(2,1)}, bf16[4,48,512]{2,1,0:T(8,128)(2,1)}, bf16[4,48,512]{2,1,0:T(8,128)(2,1)}) custom-call(s32[3]{0:T(128)} %pad_add_fusion.place, bf16[4,4,48,512]{3,2,1,0:T(8,128)(2,1)} %bitcast.137, bf16[4,4,48,512]{3,2,1,0:T(8,128)(2,1)} %bitcast.138), custom_call_target="tpu_custom_call" | custom-call | flops 100000000 | bytes 100000 | tf_op jit(solution)/shard_map/cores_last/pallas_call | solution.py:633
  325.9 7.0 %first_input_back.1 = (f32[1088,512]{1,0:T(8,128)}, f32[2,8,512]{2,1,0:T(8,128)}) custom-call(bf16[1088,1536]{1,0:T(8,128)(2,1)} %first_attention_back.1.right.projected_grad, bf16[1088,512]{1,0:T(8,128)(2,1)} %tokens.3, f32[1088,512]{1,0:T(8,128)} %get-tuple-element.178.middle_grad, bf16[32,80,512]{2,1,0:T(8,128)(2,1)} %arrange_early.1.weights, ...), custom_call_target="tpu_custom_call" | custom-call | flops 100000000 | bytes 100000 | tf_op jit(solution)/shard_map/first_input_back/pallas_call | solution.py:535
  346.7 10.7 %all_to_all.9 = f32[32,1,144]{2,1,0:T(1,128)S(1)} all-to-all(f32[32,1,144]{2,1,0:T(1,128)S(1)} %all_to_all.6), channel_id=1, replica_groups=mesh['dp'=4,'fsdp'=8] {'dp','fsdp'}, dimensions={0} | all-to-all | bytes 36864 | tf_op jit(solution)/shard_map/all_to_all | solution.py:939
  (290 shorter events, 102.6 us)
Async XLA Ops:
  7.2 100.2 %all-gather.2.cloned.1.call-start = ((), (), s32[]{:S(2)}) async-start(), calls=%async_computation.1 | async-start | bytes 6488064 | tf_op jit(solution)/shard_map/all_gather | solution.py:836
  24.7 12.1 %collective-permute-start.5 = (bf16[4,80,512]{2,1,0:T(8,128)(2,1)S(1)}, bf16[4,80,512]{2,1,0:T(8,128)(2,1)S(1)}, u32[]{:S(2)}, u32[]{:S(2)}) collective-permute-start(bf16[4,80,512]{2,1,0:T(8,128)(2,1)S(1)} %pad_maximum_fusion.1.refs_0_), channel_id=1, source_target_pairs={{0,24},{1,25},{2,26},{3,27},{4,28},{5,29},{6,30},{7,31},{8,16},{9,... | collective-permute-start | bytes 983048 | tf_op jit(solution)/shard_map/ppermute | solution.py:744
  27.2 16.5 %collective-permute-start.4 = (bf16[4,80,512]{2,1,0:T(8,128)(2,1)S(1)}, bf16[4,80,512]{2,1,0:T(8,128)(2,1)S(1)}, u32[]{:S(2)}, u32[]{:S(2)}) collective-permute-start(bf16[4,80,512]{2,1,0:T(8,128)(2,1)S(1)} %pad_maximum_fusion.1.refs_0_), channel_id=1, source_target_pairs={{0,16},{1,17},{2,18},{3,19},{4,20},{5,21},{6,22},{7,23},{8,24},{9,... | collective-permute-start | bytes 983048 | tf_op jit(solution)/shard_map/ppermute | solution.py:744
  27.7 16.1 %collective-permute-start.3 = (bf16[4,80,512]{2,1,0:T(8,128)(2,1)S(1)}, bf16[4,80,512]{2,1,0:T(8,128)(2,1)S(1)}, u32[]{:S(2)}, u32[]{:S(2)}) collective-permute-start(bf16[4,80,512]{2,1,0:T(8,128)(2,1)S(1)} %pad_maximum_fusion.1.refs_0_), channel_id=1, source_target_pairs={{0,8},{1,9},{2,10},{3,11},{4,12},{5,13},{6,14},{7,15},{8,0},{9,1},... | collective-permute-start | bytes 983048 | tf_op jit(solution)/shard_map/ppermute | solution.py:744
  30.9 12.7 %collective-permute-start.11 = (bf16[128,512]{1,0:T(8,128)(2,1)S(1)}, bf16[128,512]{1,0:T(8,128)(2,1)S(1)}, u32[]{:S(2)}, u32[]{:S(2)}) collective-permute-start(bf16[128,512]{1,0:T(8,128)(2,1)S(1)} %fusion.6), channel_id=1, source_target_pairs={{0,4},{1,5},{2,6},{3,7},{4,0},{5,1},{6,2},{7,3},{8,12},{9,13},{10,... | collective-permute-start | bytes 393224 | tf_op jit(solution)/shard_map/ppermute | solution.py:744
  36.8 14.1 %collective-permute-start.6 = (bf16[4,80,512]{2,1,0:T(8,128)(2,1)S(1)}, bf16[4,80,512]{2,1,0:T(8,128)(2,1)}, u32[]{:S(2)}, u32[]{:S(2)}) collective-permute-start(bf16[4,80,512]{2,1,0:T(8,128)(2,1)S(1)} %pad_maximum_fusion.1.refs_0_), channel_id=1, source_target_pairs={{0,1},{1,0},{2,3},{3,2},{4,5},{5,4},{6,7},{7,6},{8,9},{9,8},{10,11... | collective-permute-start | bytes 983048 | tf_op jit(solution)/shard_map/ppermute | solution.py:744
  36.8 14.9 %collective-permute-start.9 = (bf16[4,80,512]{2,1,0:T(8,128)(2,1)S(1)}, bf16[4,80,512]{2,1,0:T(8,128)(2,1)}, u32[]{:S(2)}, u32[]{:S(2)}) collective-permute-start(bf16[4,80,512]{2,1,0:T(8,128)(2,1)S(1)} %collective-permute-done.5.refs_3_), channel_id=1, source_target_pairs={{0,1},{1,0},{2,3},{3,2},{4,5},{5,4},{6,7},{7,6},{8,9},{9,8},{10,11... | collective-permute-start | bytes 983048 | tf_op jit(solution)/shard_map/ppermute | solution.py:744
  48.7 34.0 %collective-permute-start.15 = (bf16[4,128,512]{2,1,0:T(8,128)(2,1)S(1)}, bf16[4,128,512]{2,1,0:T(8,128)(2,1)S(1)}, u32[]{:S(2)}, u32[]{:S(2)}) collective-permute-start(bf16[4,128,512]{2,1,0:T(8,128)(2,1)S(1)} %pad_maximum_fusion.refs_0_), channel_id=1, source_target_pairs={{0,24},{1,25},{2,26},{3,27},{4,28},{5,29},{6,30},{7,31},{8,16},{9,... | collective-permute-start | bytes 1572872 | tf_op jit(solution)/shard_map/ppermute | solution.py:744
  50.9 31.9 %collective-permute-start.14 = (bf16[4,128,512]{2,1,0:T(8,128)(2,1)S(1)}, bf16[4,128,512]{2,1,0:T(8,128)(2,1)S(1)}, u32[]{:S(2)}, u32[]{:S(2)}) collective-permute-start(bf16[4,128,512]{2,1,0:T(8,128)(2,1)S(1)} %pad_maximum_fusion.refs_0_), channel_id=1, source_target_pairs={{0,16},{1,17},{2,18},{3,19},{4,20},{5,21},{6,22},{7,23},{8,24},{9,... | collective-permute-start | bytes 1572872 | tf_op jit(solution)/shard_map/ppermute | solution.py:744
  51.7 31.1 %collective-permute-start.13 = (bf16[4,128,512]{2,1,0:T(8,128)(2,1)S(1)}, bf16[4,128,512]{2,1,0:T(8,128)(2,1)S(1)}, u32[]{:S(2)}, u32[]{:S(2)}) collective-permute-start(bf16[4,128,512]{2,1,0:T(8,128)(2,1)S(1)} %pad_maximum_fusion.refs_0_), channel_id=1, source_target_pairs={{0,8},{1,9},{2,10},{3,11},{4,12},{5,13},{6,14},{7,15},{8,0},{9,1},... | collective-permute-start | bytes 1572872 | tf_op jit(solution)/shard_map/ppermute | solution.py:744
  178.9 22.5 %collective-permute-start.23 = (bf16[16,64,512]{2,1,0:T(8,128)(2,1)}, bf16[16,64,512]{2,1,0:T(8,128)(2,1)S(1)}, u32[]{:S(2)}, u32[]{:S(2)}) collective-permute-start(bf16[16,64,512]{2,1,0:T(8,128)(2,1)} %get-tuple-element.129), channel_id=1, source_target_pairs={{0,1},{1,0},{2,3},{3,2},{4,5},{5,4},{6,7},{7,6},{8,9},{9,8},{10,11... | collective-permute-start | bytes 3145736 | tf_op jit(solution)/shard_map/ppermute | solution.py:744
  179.1 22.4 %collective-permute-start.20 = (bf16[16,64,512]{2,1,0:T(8,128)(2,1)S(1)}, bf16[16,64,512]{2,1,0:T(8,128)(2,1)S(1)}, u32[]{:S(2)}, u32[]{:S(2)}) collective-permute-start(bf16[16,64,512]{2,1,0:T(8,128)(2,1)S(1)} %copy-done.54), channel_id=1, source_target_pairs={{0,1},{1,0},{2,3},{3,2},{4,5},{5,4},{6,7},{7,6},{8,9},{9,8},{10,11... | collective-permute-start | bytes 3145736 | tf_op jit(solution)/shard_map/ppermute | solution.py:744
  185.1 16.3 %collective-permute-start.22 = (bf16[16,48,512]{2,1,0:T(8,128)(2,1)}, bf16[16,48,512]{2,1,0:T(8,128)(2,1)S(1)}, u32[]{:S(2)}, u32[]{:S(2)}) collective-permute-start(bf16[16,48,512]{2,1,0:T(8,128)(2,1)} %get-tuple-element.133), channel_id=1, source_target_pairs={{0,1},{1,0},{2,3},{3,2},{4,5},{5,4},{6,7},{7,6},{8,9},{9,8},{10,11... | collective-permute-start | bytes 2359304 | tf_op jit(solution)/shard_map/ppermute | solution.py:744
  188.5 12.9 %collective-permute-start.21 = (bf16[16,16,512]{2,1,0:T(8,128)(2,1)}, bf16[16,16,512]{2,1,0:T(8,128)(2,1)S(1)}, u32[]{:S(2)}, u32[]{:S(2)}) collective-permute-start(bf16[16,16,512]{2,1,0:T(8,128)(2,1)} %get-tuple-element.137), channel_id=1, source_target_pairs={{0,1},{1,0},{2,3},{3,2},{4,5},{5,4},{6,7},{7,6},{8,9},{9,8},{10,11... | collective-permute-start | bytes 786440 | tf_op jit(solution)/shard_map/ppermute | solution.py:744
  226.5 35.2 %collective-permute-start.28 = (bf16[4,192,512]{2,1,0:T(8,128)(2,1)S(1)}, bf16[4,192,512]{2,1,0:T(8,128)(2,1)S(1)}, u32[]{:S(2)}, u32[]{:S(2)}) collective-permute-start(bf16[4,192,512]{2,1,0:T(8,128)(2,1)S(1)} %copy-done.58), channel_id=1, source_target_pairs={{0,8},{1,9},{2,10},{3,11},{4,12},{5,13},{6,14},{7,15},{8,0},{9,1},... | collective-permute-start | bytes 2359304 | tf_op jit(solution)/shard_map/ppermute | solution.py:744
  228.0 36.3 %collective-permute-start.29 = (bf16[4,192,512]{2,1,0:T(8,128)(2,1)S(1)}, bf16[4,192,512]{2,1,0:T(8,128)(2,1)S(1)}, u32[]{:S(2)}, u32[]{:S(2)}) collective-permute-start(bf16[4,192,512]{2,1,0:T(8,128)(2,1)S(1)} %copy-done.57), channel_id=1, source_target_pairs={{0,16},{1,17},{2,18},{3,19},{4,20},{5,21},{6,22},{7,23},{8,24},{9,... | collective-permute-start | bytes 2359304 | tf_op jit(solution)/shard_map/ppermute | solution.py:744
  229.2 35.1 %collective-permute-start.27 = (bf16[4,192,512]{2,1,0:T(8,128)(2,1)S(1)}, bf16[4,192,512]{2,1,0:T(8,128)(2,1)S(1)}, u32[]{:S(2)}, u32[]{:S(2)}) collective-permute-start(bf16[4,192,512]{2,1,0:T(8,128)(2,1)S(1)} %copy-done.56), channel_id=1, source_target_pairs={{0,24},{1,25},{2,26},{3,27},{4,28},{5,29},{6,30},{7,31},{8,16},{9,... | collective-permute-start | bytes 2359304 | tf_op jit(solution)/shard_map/ppermute | solution.py:744
  269.1 16.6 %collective-permute-start.38 = (bf16[192,512]{1,0:T(8,128)(2,1)}, bf16[192,512]{1,0:T(8,128)(2,1)S(1)}, u32[]{:S(2)}, u32[]{:S(2)}) collective-permute-start(bf16[192,512]{1,0:T(8,128)(2,1)} %get-tuple-element.168), channel_id=1, source_target_pairs={{0,4},{1,5},{2,6},{3,7},{4,0},{5,1},{6,2},{7,3},{8,12},{9,13},{10,... | collective-permute-start | bytes 589832 | tf_op jit(solution)/shard_map/ppermute | solution.py:744
  271.0 14.7 %collective-permute-start.37 = (bf16[192,512]{1,0:T(8,128)(2,1)}, bf16[192,512]{1,0:T(8,128)(2,1)S(1)}, u32[]{:S(2)}, u32[]{:S(2)}) collective-permute-start(bf16[192,512]{1,0:T(8,128)(2,1)} %get-tuple-element.169), channel_id=1, source_target_pairs={{0,6},{1,7},{2,4},{3,5},{4,2},{5,3},{6,0},{7,1},{8,14},{9,15},{10,... | collective-permute-start | bytes 589832 | tf_op jit(solution)/shard_map/ppermute | solution.py:744
  273.5 16.5 %collective-permute-start.41 = (bf16[4,144,512]{2,1,0:T(8,128)(2,1)}, bf16[4,144,512]{2,1,0:T(8,128)(2,1)S(1)}, u32[]{:S(2)}, u32[]{:S(2)}) collective-permute-start(bf16[4,144,512]{2,1,0:T(8,128)(2,1)} %get-tuple-element.160), channel_id=1, source_target_pairs={{0,8},{1,9},{2,10},{3,11},{4,12},{5,13},{6,14},{7,15},{8,0},{9,1},... | collective-permute-start | bytes 1769480 | tf_op jit(solution)/shard_map/ppermute | solution.py:744
  273.5 26.4 %collective-permute-start.42 = (bf16[4,144,512]{2,1,0:T(8,128)(2,1)}, bf16[4,144,512]{2,1,0:T(8,128)(2,1)S(1)}, u32[]{:S(2)}, u32[]{:S(2)}) collective-permute-start(bf16[4,144,512]{2,1,0:T(8,128)(2,1)} %get-tuple-element.161), channel_id=1, source_target_pairs={{0,16},{1,17},{2,18},{3,19},{4,20},{5,21},{6,22},{7,23},{8,24},{9,... | collective-permute-start | bytes 1769480 | tf_op jit(solution)/shard_map/ppermute | solution.py:744
  277.8 22.1 %collective-permute-start.40 = (bf16[4,144,512]{2,1,0:T(8,128)(2,1)}, bf16[4,144,512]{2,1,0:T(8,128)(2,1)S(1)}, u32[]{:S(2)}, u32[]{:S(2)}) collective-permute-start(bf16[4,144,512]{2,1,0:T(8,128)(2,1)} %get-tuple-element.162), channel_id=1, source_target_pairs={{0,24},{1,25},{2,26},{3,27},{4,28},{5,29},{6,30},{7,31},{8,16},{9,... | collective-permute-start | bytes 1769480 | tf_op jit(solution)/shard_map/ppermute | solution.py:744
  285.7 31.6 %collective-permute-start.30 = (bf16[16,48,512]{2,1,0:T(8,128)(2,1)}, bf16[16,48,512]{2,1,0:T(8,128)(2,1)S(1)}, u32[]{:S(2)}, u32[]{:S(2)}) collective-permute-start(bf16[16,48,512]{2,1,0:T(8,128)(2,1)} %get-tuple-element.172), channel_id=1, source_target_pairs={{0,1},{1,0},{2,3},{3,2},{4,5},{5,4},{6,7},{7,6},{8,9},{9,8},{10,11... | collective-permute-start | bytes 2359304 | tf_op jit(solution)/shard_map/ppermute | solution.py:744
  322.2 11.5 %collective-permute-start.32 = (bf16[4,48,512]{2,1,0:T(8,128)(2,1)}, bf16[4,48,512]{2,1,0:T(8,128)(2,1)S(1)}, u32[]{:S(2)}, u32[]{:S(2)}) collective-permute-start(bf16[4,48,512]{2,1,0:T(8,128)(2,1)} %get-tuple-element.174), channel_id=1, source_target_pairs={{0,8},{1,9},{2,10},{3,11},{4,12},{5,13},{6,14},{7,15},{8,0},{9,1},... | collective-permute-start | bytes 589832 | tf_op jit(solution)/shard_map/ppermute | solution.py:744
  (82 other events, 922.1 us)
Sparse Core Ops, SparseCore 0:
  11.9 87.5 all-gather.1

commit v3 on v2

v3 whole, which is shorter than its diff:
```python
import jax
import jax.numpy as jnp
from jax import lax
from jax.experimental import pallas as pl
from jax.experimental.pallas import tpu as pltpu
from jax.sharding import PartitionSpec as P

HEADS = 8
HEAD_DIM = 64
FRAMES = 17
WIN = 64
STEP = 5
WIDTH = 512
BLOCKS = 32
SLAB = WIDTH // BLOCKS
TILES = 4
TILE = FRAMES * WIN // TILES
SPOTS = WIN // TILES
HALF = TILE // 2
GROUP = 9
SCALE = HEAD_DIM ** (-0.5)
VMEM_BYTES = 56 * 2**20
COST = pl.CostEstimate(flops=10**8, bytes_accessed=10**5, transcendentals=0)

NORM_EPS = 1e-05
ADAM_EPS = 1e-06
BETA_FIRST = 0.5
BETA_SECOND = 0.5
RATE = 0.25
DECAY_RATE = 0.01
MASKED = -1e30


def row_norm(inputs):
    center = inputs - jnp.mean(inputs, axis=-1, keepdims=True)
    spread = jnp.mean(center * center, axis=-1, keepdims=True)
    scale = lax.rsqrt(spread + NORM_EPS)
    return center * scale, scale


def row_norm_back(grad, gain_row, normal, scale):
    scaled = grad * gain_row
    first = jnp.mean(scaled, axis=-1, keepdims=True)
    second = jnp.mean(scaled * normal, axis=-1, keepdims=True)
    return scale * (scaled - first - normal * second)


def fold_rows(array):
    return jnp.sum(array.reshape(-1, 8, array.shape[-1]), axis=0)


def gelu_pair(upward):
    bell = jnp.exp(-0.5 * upward * upward)
    place = 1.0 / (1.0 + 0.23164189 * jnp.abs(upward))
    tail = 0.5 * 1.061405429
    for factor in (-1.453152027, 1.421413741, -0.284496736, 0.254829592):
        tail = tail * place + 0.5 * factor
    tail = tail * place * bell
    cumulative = jnp.where(upward >= 0.0, 1.0 - tail, tail)
    return upward * cumulative, cumulative + 0.3989422804014327 * upward * bell


def dot_nn(left, right):
    return lax.dot_general(
        left, right, (((1,), (0,)), ((), ())), preferred_element_type=jnp.float32
    )


def dot_nt(left, right):
    return lax.dot_general(
        left, right, (((1,), (1,)), ((), ())), preferred_element_type=jnp.float32
    )


def dot_tn(left, right):
    return lax.dot_general(
        left, right, (((0,), (0,)), ((), ())), preferred_element_type=jnp.float32
    )


def slab(weights, index):
    return weights[:, SLAB * index : SLAB * index + SLAB, :].reshape(WIDTH, WIDTH)


def down_rows(weights, index):
    part = BLOCKS // 4
    return weights[part * index : part * index + part].reshape(WIDTH, WIDTH)


def weight_spec(array, index):
    return pl.BlockSpec(
        (BLOCKS, 4 * SLAB, WIDTH), lambda i: (0, index, 0), pipeline_mode=pl.Buffered(1)
    )


def stack_heads(pair):
    lane = lax.broadcasted_iota(jnp.int32, pair.shape, 1)
    zero = jnp.zeros_like(pair)
    return jnp.concatenate(
        [jnp.where(lane < HEAD_DIM, pair, zero), jnp.where(lane < HEAD_DIM, zero, pair)], axis=0
    )


def merge_heads(stacked):
    rows = stacked.shape[0] // 2
    lane = lax.broadcasted_iota(jnp.int32, (rows, 2 * HEAD_DIM), 1)
    return jnp.where(lane < HEAD_DIM, stacked[:rows], stacked[rows:])


def soft_weights(scores, axis):
    raised = jnp.exp(scores - jnp.max(scores, axis=axis, keepdims=True))
    return raised * (1.0 / jnp.sum(raised, axis=axis, keepdims=True))


def pair_caps():
    row = lax.broadcasted_iota(jnp.int32, (4 * WIN, 2 * WIN), 0)
    column = lax.broadcasted_iota(jnp.int32, (4 * WIN, 2 * WIN), 1)
    return jnp.where(row // WIN % 2 == column // WIN, 3.0e38, MASKED)


def frame_pairs():
    return [min(2 * index, FRAMES - 2) for index in range((FRAMES + 1) // 2)]


def outer_store(core, left, right, mine, other, block, row, rows):
    first = core[0] == 0
    count = 128 // rows
    for half in range(2):
        part = dot_tn(left[:, 256 * half : 256 * half + 256], right).astype(jnp.bfloat16)
        part = part.reshape(count, 2, rows, WIDTH)
        even, odd = part[:, 0], part[:, 1]
        place = pl.ds(block + count * half, count), pl.ds(row, rows)
        mine[place] = jnp.where(first, even, odd)
        other[place] = jnp.where(first, odd, even)


def slab_row(step, first):
    return pl.multiple_of((step - first) * SLAB, SLAB)


def grad_specs(rows):
    return [pl.BlockSpec((BLOCKS // 2, rows, WIDTH), lambda i: (0, 0, 0))] * 2


def grad_shapes(rows):
    return [jax.ShapeDtypeStruct((BLOCKS // 2, rows, WIDTH), jnp.bfloat16)] * 2


def part_of(step, first):
    return pl.ds(pl.multiple_of((step - first) * WIDTH, WIDTH), WIDTH)


def first_attention_kernel(
    tokens, weights, gains, normed_out, projected_out, probs, attended, middle_out, hidden_in_out,
    projected,
):
    step = pl.program_id(0)

    @pl.when(step < TILES)
    def _():
        normal, _ = row_norm(tokens[...].astype(jnp.float32))
        normed = (normal * gains[0:1, :] + gains[1:2, :]).astype(jnp.bfloat16)
        normed_out[...] = normed
        rows = pl.ds(pl.multiple_of(step * TILE, TILE), TILE)
        for index in range(3):
            part = dot_nn(normed, slab(weights, index)).astype(jnp.bfloat16)
            projected[rows, WIDTH * index : WIDTH * index + WIDTH] = part
            projected_out[:, WIDTH * index : WIDTH * index + WIDTH] = part

    @pl.when(step == TILES)
    def _():
        caps = pair_caps()
        for index, frame in enumerate(frame_pairs()):
            rows = slice(WIN * frame, WIN * frame + 2 * WIN)
            lanes = [slice(128 * pair, 128 * pair + 128) for pair in range(HEADS // 2)]
            queries = [stack_heads(projected[rows, lane] * SCALE) for lane in lanes]
            keys = [projected[rows, WIDTH + 128 * pair : WIDTH + 128 * pair + 128] for pair in range(4)]
            scores = [jnp.minimum(dot_nt(*both), caps) for both in zip(queries, keys)]
            shares = [soft_weights(score, -1).astype(jnp.bfloat16) for score in scores]
            for pair, share in enumerate(shares):
                probs[index, pair] = share
                values = projected[rows, 2 * WIDTH + 128 * pair : 2 * WIDTH + 128 * pair + 128]
                attended[rows, lanes[pair]] = merge_heads(dot_nn(share, values)).astype(jnp.bfloat16)

    @pl.when(step > TILES)
    def _():
        rows = pl.ds(pl.multiple_of((step - TILES - 1) * TILE, TILE), TILE)
        middle = tokens[...].astype(jnp.float32) + dot_nn(attended[rows, :], slab(weights, 3))
        middle_out[...] = middle
        normal, _ = row_norm(middle)
        hidden_in_out[...] = (normal * gains[2:3, :] + gains[3:4, :]).astype(jnp.bfloat16)


def first_attention(tokens, weights, gains):
    count = tokens.shape[0]

    def early(width):
        return pl.BlockSpec((TILE, width), lambda i: (jnp.minimum(i, TILES - 1), 0))

    def late(width):
        return pl.BlockSpec((TILE, width), lambda i: (jnp.maximum(i - TILES - 1, 0), 0))

    def whole_out(*shape):
        return pl.BlockSpec(shape, lambda i: (0,) * len(shape))

    def out(width, kind):
        return jax.ShapeDtypeStruct((count, width), kind)

    return pl.pallas_call(
        first_attention_kernel,
        grid=(2 * TILES + 1,),
        in_specs=[
            pl.BlockSpec(
                (TILE, WIDTH), lambda i: (jnp.where(i < TILES, i, jnp.maximum(i - TILES - 1, 0)), 0)
            ),
            weight_spec(weights, 0),
            whole_out(4, WIDTH),
        ],
        out_specs=[
            early(WIDTH),
            early(3 * WIDTH),
            whole_out((FRAMES + 1) // 2, HEADS // 2, 4 * WIN, 2 * WIN),
            whole_out(count, WIDTH),
            late(WIDTH),
            late(WIDTH),
        ],
        out_shape=[
            out(WIDTH, jnp.bfloat16),
            out(3 * WIDTH, jnp.bfloat16),
            jax.ShapeDtypeStruct(((FRAMES + 1) // 2, HEADS // 2, 4 * WIN, 2 * WIN), jnp.bfloat16),
            out(WIDTH, jnp.bfloat16),
            out(WIDTH, jnp.float32),
            out(WIDTH, jnp.bfloat16),
        ],
        scratch_shapes=[pltpu.VMEM((count, 3 * WIDTH), jnp.bfloat16)],
        compiler_params=pltpu.CompilerParams(vmem_limit_bytes=VMEM_BYTES),
        cost_estimate=COST,
        name="first_attention",
    )(tokens, weights, gains)


def first_mlp_kernel(middle, hidden_in, weights_up, weights_down, hidden_out, slope_out, result_out):
    result = middle[...]
    for index in range(4):
        columns = slice(WIDTH * index, WIDTH * index + WIDTH)
        value, slope = gelu_pair(dot_nn(hidden_in[...], slab(weights_up, index)))
        hidden = value.astype(jnp.bfloat16)
        hidden_out[:, columns] = hidden
        slope_out[:, columns] = slope.astype(jnp.bfloat16)
        result = result + dot_nn(hidden, down_rows(weights_down, index))
    result_out[...] = result


def first_mlp(middle, hidden_in, weights, weights_at):
    count = middle.shape[0]

    def tile(width):
        return pl.BlockSpec((TILE, width), lambda i: (i, 0))

    return pl.pallas_call(
        first_mlp_kernel,
        grid=(TILES,),
        in_specs=[
            tile(WIDTH),
            tile(WIDTH),
            weight_spec(weights, weights_at),
            weight_spec(weights, weights_at + 1),
        ],
        out_specs=[tile(4 * WIDTH), tile(4 * WIDTH), tile(WIDTH)],
        out_shape=[
            jax.ShapeDtypeStruct((count, 4 * WIDTH), jnp.bfloat16),
            jax.ShapeDtypeStruct((count, 4 * WIDTH), jnp.bfloat16),
            jax.ShapeDtypeStruct((count, WIDTH), jnp.float32),
        ],
        compiler_params=pltpu.CompilerParams(vmem_limit_bytes=VMEM_BYTES),
        cost_estimate=COST,
        name="first_mlp",
    )(middle, hidden_in, weights, weights)


def second_kernel(
    frame_count, core, inputs, cotangent, weights, weights_up, weights_down, gains, result_out,
    grad_out, sums, mine, other,
    caps, query_rows, key_rows, value_rows, probs, slopes, normed, projected_grads, attended,
    branch_grads, hidden_in, up_grads, hidden, out_grads,
):
    step = pl.program_id(0)

    @pl.when(step == 0)
    def _():
        row = lax.broadcasted_iota(jnp.int32, caps.shape, 0)
        column = lax.broadcasted_iota(jnp.int32, caps.shape, 1) % HALF
        soon, late = row // 8, column // 8
        video = (late < frame_count[0]) & (soon < frame_count[0])
        allowed = (row % 8 == column % 8) & ((soon == late) | ((soon < late) & video))
        caps[...] = jnp.where(allowed, 3.0e38, MASKED)
        sums[...] = jnp.zeros_like(sums)

    def flat(ref):
        array = ref[...].astype(jnp.float32)
        return jnp.concatenate(
            [array[:, :8].reshape(HALF, WIDTH), array[:, 8:].reshape(HALF, WIDTH)], axis=0
        )

    def keep(ref, value):
        halves = [value[HALF * half : HALF * half + HALF] for half in range(2)]
        ref[...] = jnp.concatenate(
            [half.reshape(FRAMES, 8, WIDTH) for half in halves], axis=1
        ).astype(ref.dtype)

    @pl.when(step < TILES)
    def _():
        rows = pl.ds(pl.multiple_of(step * TILE, TILE), TILE)
        inside = lax.broadcasted_iota(jnp.int32, (TILE, 1), 0) % HALF // 8 < frame_count[0]
        gate = jnp.where(inside, 1.0, 0.0)
        stream = flat(inputs)
        normal_first, scale_first = row_norm(stream)
        normed_tile = (normal_first * gains[0:1, :] + gains[1:2, :]).astype(jnp.bfloat16)
        normed[rows, :] = normed_tile
        for index, ref in enumerate((query_rows, key_rows, value_rows)):
            part = dot_nn(normed_tile, slab(weights, index))
            for half in range(2):
                piece = part[HALF * half : HALF * half + HALF]
                if index == 0:
                    for pair in range(HEADS // 2):
                        stacked = stack_heads(piece[:, 128 * pair : 128 * pair + 128] * SCALE)
                        ref[half, pair] = stacked.astype(jnp.bfloat16)
                else:
                    ref[half] = piece.astype(jnp.bfloat16)
        units = [
            (half, pair, slice(128 * pair, 128 * pair + 128))
            for half in range(2)
            for pair in range(HEADS // 2)
        ]
        scores = [
            dot_nt(key_rows[half, :, lanes], query_rows[half, pair]) for half, pair, lanes in units
        ]
        shares = [
            soft_weights(jnp.minimum(score, caps[...]), 0).astype(jnp.bfloat16) for score in scores
        ]
        for share, (half, pair, _) in zip(shares, units):
            probs[half, pair] = share
        parts = [
            merge_heads(dot_tn(share, value_rows[half, :, lanes]))
            for share, (half, _, lanes) in zip(shares, units)
        ]
        halves = [jnp.concatenate(parts[4 * half : 4 * half + 4], axis=1) for half in range(2)]
        attended_tile = jnp.concatenate(halves, axis=0).astype(jnp.bfloat16)
        attended[rows, :] = attended_tile
        middle = stream + gate * dot_nn(attended_tile, slab(weights, 3))
        normal_second, scale_second = row_norm(middle)
        hidden_in_tile = (normal_second * gains[2:3, :] + gains[3:4, :]).astype(jnp.bfloat16)
        hidden_in[rows, :] = hidden_in_tile
        result = middle
        for index in range(4):
            columns = slice(WIDTH * index, WIDTH * index + WIDTH)
            value, slope = gelu_pair(dot_nn(hidden_in_tile, slab(weights_up, index)))
            hidden_tile = value.astype(jnp.bfloat16)
            hidden[rows, columns] = hidden_tile
            slopes[:, columns] = slope
            result = result + dot_nn(hidden_tile, down_rows(weights_down, index))
        keep(result_out, result)

        upstream = flat(cotangent)
        out_grad = upstream.astype(jnp.bfloat16)
        out_grads[rows, :] = out_grad
        hidden_in_grad = jnp.zeros((TILE, WIDTH), jnp.float32)
        for index in range(4):
            columns = slice(WIDTH * index, WIDTH * index + WIDTH)
            up_grad = (dot_nt(out_grad, down_rows(weights_down, index)) * slopes[:, columns]).astype(
                jnp.bfloat16
            )
            up_grads[rows, columns] = up_grad
            hidden_in_grad = hidden_in_grad + dot_nt(up_grad, slab(weights_up, index))
        sums[2] += fold_rows(hidden_in_grad * normal_second)
        sums[3] += fold_rows(hidden_in_grad)
        middle_grad = upstream + row_norm_back(
            hidden_in_grad, gains[2:3, :], normal_second, scale_second
        )
        branch_grad = (middle_grad * gate).astype(jnp.bfloat16)
        branch_grads[rows, :] = branch_grad
        attended_grad = dot_nt(branch_grad, slab(weights, 3))
        grads = [
            stack_heads(attended_grad[HALF * half : HALF * half + HALF, lanes]).astype(jnp.bfloat16)
            for half, _, lanes in units
        ]
        share_grads = [
            dot_nt(value_rows[half, :, lanes], grad) for grad, (half, _, lanes) in zip(grads, units)
        ]
        value_grads = [
            dot_nn(probs[half, pair], grad) for grad, (half, pair, _) in zip(grads, units)
        ]
        score_grads = []
        for share_grad, (half, pair, _) in zip(share_grads, units):
            share = probs[half, pair].astype(jnp.float32)
            total = jnp.sum(share_grad * share, axis=0, keepdims=True)
            score_grads.append((share * (share_grad - total)).astype(jnp.bfloat16))
        query_grads = [
            dot_tn(grad, key_rows[half, :, lanes])
            for grad, (half, _, lanes) in zip(score_grads, units)
        ]
        key_grads = [
            dot_nn(grad, query_rows[half, pair]) for grad, (half, pair, _) in zip(score_grads, units)
        ]
        query_grads = [merge_heads(grad) * SCALE for grad in query_grads]
        halves = [
            jnp.concatenate(
                [
                    part
                    for parts in (query_grads, key_grads, value_grads)
                    for part in parts[4 * half : 4 * half + 4]
                ],
                axis=1,
            )
            for half in range(2)
        ]
        projected_grad = jnp.concatenate(halves, axis=0).astype(jnp.bfloat16)
        projected_grads[rows, :] = projected_grad
        normed_grad = jnp.zeros((TILE, WIDTH), jnp.float32)
        for index in range(3):
            part = projected_grad[:, WIDTH * index : WIDTH * index + WIDTH]
            normed_grad = normed_grad + dot_nt(part, slab(weights, index))
        sums[0] += fold_rows(normed_grad * normal_first)
        sums[1] += fold_rows(normed_grad)
        keep(
            grad_out,
            middle_grad + row_norm_back(normed_grad, gains[0:1, :], normal_first, scale_first),
        )

    @pl.when((step >= TILES) & (step < TILES + 4))
    def _():
        right = up_grads[:, part_of(step, TILES)]
        outer_store(core, hidden_in, right, mine, other, 0, slab_row(step, TILES), SLAB)

    @pl.when((step >= TILES + 4) & (step < TILES + 7))
    def _():
        right = projected_grads[:, part_of(step, TILES + 4)]
        outer_store(core, normed, right, mine, other, 0, slab_row(step, TILES - 1), SLAB)

    @pl.when((step >= TILES + 7) & (step < TILES + 11))
    def _():
        left = hidden[:, part_of(step, TILES + 7)]
        block = (step - TILES - 7) * 4
        outer_store(core, left, out_grads[...], mine, other, block, 8 * SLAB, 4 * SLAB)

    @pl.when(step == TILES + 11)
    def _():
        outer_store(core, attended, branch_grads[...], mine, other, 0, 4 * SLAB, SLAB)


def second_block(frame_counts, core, inputs, cotangent, weights, gains):
    def tile(width):
        return pl.BlockSpec((FRAMES, SPOTS, width), lambda i: (0, jnp.minimum(i, TILES - 1), 0))

    def held(width):
        return pltpu.VMEM((FRAMES * WIN, width * WIDTH), jnp.bfloat16)

    whole = (FRAMES, WIN, WIDTH)
    outs = pl.pallas_call(
        second_kernel,
        grid=(TILES + 12,),
        in_specs=[
            pl.BlockSpec(memory_space=pltpu.SMEM),
            pl.BlockSpec(memory_space=pltpu.SMEM),
            tile(WIDTH),
            tile(WIDTH),
            weight_spec(weights, 0),
            weight_spec(weights, 1),
            weight_spec(weights, 2),
            pl.BlockSpec((4, WIDTH), lambda i: (0, 0)),
        ],
        out_specs=[
            tile(WIDTH),
            tile(WIDTH),
            pl.BlockSpec((4, 8, WIDTH), lambda i: (0, 0, 0)),
            *grad_specs(12 * SLAB),
        ],
        out_shape=[
            jax.ShapeDtypeStruct(whole, jnp.bfloat16),
            jax.ShapeDtypeStruct(whole, jnp.float32),
            jax.ShapeDtypeStruct((4, 8, WIDTH), jnp.float32),
            *grad_shapes(12 * SLAB),
        ],
        scratch_shapes=[
            pltpu.VMEM((HALF, 2 * HALF), jnp.float32),
            pltpu.VMEM((2, HEADS // 2, 2 * HALF, 128), jnp.bfloat16),
            pltpu.VMEM((2, HALF, WIDTH), jnp.bfloat16),
            pltpu.VMEM((2, HALF, WIDTH), jnp.bfloat16),
            pltpu.VMEM((2, HEADS // 2, HALF, 2 * HALF), jnp.bfloat16),
            pltpu.VMEM((TILE, 4 * WIDTH), jnp.float32),
            held(1),
            held(3),
            held(1),
            held(1),
            held(1),
            held(4),
            held(4),
            held(1),
        ],
        compiler_params=pltpu.CompilerParams(vmem_limit_bytes=VMEM_BYTES),
        cost_estimate=COST,
        name="second_block",
    )(
        frame_counts,
        core,
        inputs.reshape(whole),
        cotangent.reshape(whole),
        weights,
        weights,
        weights,
        gains,
    )
    return (
        outs[0].reshape(-1, WIDTH),
        outs[1].reshape(-1, WIDTH),
        outs[2],
        tuple(outs[3:]),
    )


def first_back_kernel(
    core, upstream, slopes, middle, weights, weights_up, weights_down, gains, hidden, hidden_in,
    attended, attended_grad_out, middle_grad_out, sums, mine, other, up_grads, out_grads, branch_grads,
):
    step = pl.program_id(0)

    @pl.when(step == 0)
    def _():
        sums[...] = jnp.zeros_like(sums)

    @pl.when(step < TILES)
    def _():
        rows = pl.ds(pl.multiple_of(step * TILE, TILE), TILE)
        out_grad = upstream[...].astype(jnp.bfloat16)
        out_grads[rows, :] = out_grad
        hidden_in_grad = jnp.zeros((TILE, WIDTH), jnp.float32)
        for index in range(4):
            columns = slice(WIDTH * index, WIDTH * index + WIDTH)
            up_grad = (dot_nt(out_grad, down_rows(weights_down, index)) * slopes[:, columns]).astype(
                jnp.bfloat16
            )
            up_grads[rows, columns] = up_grad
            hidden_in_grad = hidden_in_grad + dot_nt(up_grad, slab(weights_up, index))
        normal, scale = row_norm(middle[...])
        sums[0] += fold_rows(hidden_in_grad * normal)
        sums[1] += fold_rows(hidden_in_grad)
        middle_grad = upstream[...] + row_norm_back(hidden_in_grad, gains[2:3, :], normal, scale)
        middle_grad_out[...] = middle_grad
        branch_grad = middle_grad.astype(jnp.bfloat16)
        branch_grads[rows, :] = branch_grad
        attended_grad_out[...] = dot_nt(branch_grad, slab(weights, 3)).astype(jnp.bfloat16)

    @pl.when((step >= TILES) & (step < TILES + 4))
    def _():
        right = up_grads[:, part_of(step, TILES)]
        outer_store(core, hidden_in, right, mine, other, 0, slab_row(step, TILES), SLAB)

    @pl.when((step >= TILES + 4) & (step < TILES + 8))
    def _():
        block = (step - TILES - 4) * 4
        outer_store(core, hidden, out_grads[...], mine, other, block, 5 * SLAB, 4 * SLAB)

    @pl.when(step == TILES + 8)
    def _():
        outer_store(core, attended, branch_grads[...], mine, other, 0, 4 * SLAB, SLAB)


def first_back(
    core, upstream, slopes, middle, weights, late_weights, late_at, gains, hidden, hidden_in, attended
):
    count = upstream.shape[0]

    def tile(width):
        return pl.BlockSpec((TILE, width), lambda i: (jnp.minimum(i, TILES - 1), 0))

    def whole(*shape):
        return pl.BlockSpec(shape, lambda i: (0,) * len(shape))

    outs = pl.pallas_call(
        first_back_kernel,
        grid=(TILES + 9,),
        in_specs=[
            pl.BlockSpec(memory_space=pltpu.SMEM),
            tile(WIDTH),
            tile(4 * WIDTH),
            tile(WIDTH),
            weight_spec(weights, 0),
            weight_spec(late_weights, late_at),
            weight_spec(late_weights, late_at + 1),
            whole(4, WIDTH),
            pl.BlockSpec((count, WIDTH), lambda i: (0, jnp.clip(i - TILES - 4, 0, 3))),
            whole(count, WIDTH),
            whole(count, WIDTH),
        ],
        out_specs=[
            tile(WIDTH),
            tile(WIDTH),
            whole(2, 8, WIDTH),
            *grad_specs(9 * SLAB),
        ],
        out_shape=[
            jax.ShapeDtypeStruct((count, WIDTH), jnp.bfloat16),
            jax.ShapeDtypeStruct((count, WIDTH), jnp.float32),
            jax.ShapeDtypeStruct((2, 8, WIDTH), jnp.float32),
            *grad_shapes(9 * SLAB),
        ],
        scratch_shapes=[
            pltpu.VMEM((count, 4 * WIDTH), jnp.bfloat16),
            pltpu.VMEM((count, WIDTH), jnp.bfloat16),
            pltpu.VMEM((count, WIDTH), jnp.bfloat16),
        ],
        compiler_params=pltpu.CompilerParams(vmem_limit_bytes=VMEM_BYTES),
        cost_estimate=COST,
        name="first_back",
    )(
        core, upstream, slopes, middle, weights, late_weights, late_weights, gains, hidden, hidden_in,
        attended,
    )
    return (*outs[:3], tuple(outs[3:]))


def first_attention_back_kernel(
    core, queries_in, keys_in, values_in, probs, attended_grad, normed, projected_grad_out, mine,
    other, projected_grads,
):
    step = pl.program_id(0)

    @pl.when(step < HEADS // 2)
    def _():
        frames = list(enumerate(frame_pairs()))
        for some in (frames[at : at + GROUP] for at in range(0, len(frames), GROUP)):
            rows = [slice(WIN * frame, WIN * frame + 2 * WIN) for _, frame in some]
            out_grads = [stack_heads(attended_grad[row, :]) for row in rows]
            share_grads = [dot_nt(grad, values_in[row, :]) for grad, row in zip(out_grads, rows)]
            shares = [probs[index, 0] for index, _ in some]
            value_grads = [dot_tn(share, grad) for share, grad in zip(shares, out_grads)]
            score_grads = []
            for share, share_grad in zip(shares, share_grads):
                weights = share.astype(jnp.float32)
                total = jnp.sum(share_grad * weights, axis=-1, keepdims=True)
                score_grads.append((weights * (share_grad - total)).astype(jnp.bfloat16))
            query_grads = [dot_nn(grad, keys_in[row, :]) for grad, row in zip(score_grads, rows)]
            key_grads = [
                dot_tn(grad, stack_heads(queries_in[row, :] * SCALE))
                for grad, row in zip(score_grads, rows)
            ]
            query_grads = [merge_heads(grad) * SCALE for grad in query_grads]
            for index, grads in enumerate((query_grads, key_grads, value_grads)):
                lanes = pl.ds(pl.multiple_of(step * 128 + WIDTH * index, 128), 128)
                for row, grad in zip(rows, grads):
                    projected_grads[row, lanes] = grad.astype(jnp.bfloat16)

    @pl.when(step >= HEADS // 2)
    def _():
        right = projected_grads[:, part_of(step, HEADS // 2)]
        projected_grad_out[...] = right
        outer_store(core, normed, right, mine, other, 0, slab_row(step, HEADS // 2), SLAB)


def first_attention_back(core, projected, probs, attended_grad, normed):
    count = projected.shape[0]
    pairs = HEADS // 2

    def lanes(first):
        return pl.BlockSpec((count, 128), lambda i: (0, first + jnp.minimum(i, pairs - 1)))

    outs = pl.pallas_call(
        first_attention_back_kernel,
        grid=(pairs + 3,),
        in_specs=[
            pl.BlockSpec(memory_space=pltpu.SMEM),
            lanes(0),
            lanes(pairs),
            lanes(2 * pairs),
            pl.BlockSpec(
                ((FRAMES + 1) // 2, 1, 4 * WIN, 2 * WIN),
                lambda i: (0, jnp.minimum(i, pairs - 1), 0, 0),
            ),
            lanes(0),
            pl.BlockSpec((count, WIDTH), lambda i: (0, 0)),
        ],
        out_specs=[
            pl.BlockSpec((count, WIDTH), lambda i: (0, jnp.clip(i - pairs, 0, 2))),
            *grad_specs(3 * SLAB),
        ],
        out_shape=[
            jax.ShapeDtypeStruct((count, 3 * WIDTH), jnp.bfloat16),
            *grad_shapes(3 * SLAB),
        ],
        scratch_shapes=[pltpu.VMEM((count, 3 * WIDTH), jnp.bfloat16)],
        compiler_params=pltpu.CompilerParams(vmem_limit_bytes=VMEM_BYTES),
        cost_estimate=COST,
        name="first_attention_back",
    )(core, projected, projected, projected, probs, attended_grad, normed)
    return outs[0], tuple(outs[1:])


def first_input_back_kernel(projected_grad, tokens, middle_grad, weights, gains, grad_out, sums):
    @pl.when(pl.program_id(0) == 0)
    def _():
        sums[...] = jnp.zeros_like(sums)

    normed_grad = jnp.zeros((TILE, WIDTH), jnp.float32)
    for index in range(3):
        part = projected_grad[:, WIDTH * index : WIDTH * index + WIDTH]
        normed_grad = normed_grad + dot_nt(part, slab(weights, index))
    normal, scale = row_norm(tokens[...].astype(jnp.float32))
    sums[0] += fold_rows(normed_grad * normal)
    sums[1] += fold_rows(normed_grad)
    grad_out[...] = middle_grad[...] + row_norm_back(normed_grad, gains[0:1, :], normal, scale)


def first_input_back(projected_grad, tokens, middle_grad, weights, gains):
    count = tokens.shape[0]

    def tile(width):
        return pl.BlockSpec((TILE, width), lambda i: (i, 0))

    def whole(*shape):
        return pl.BlockSpec(shape, lambda i: (0,) * len(shape), pipeline_mode=pl.Buffered(1))

    return pl.pallas_call(
        first_input_back_kernel,
        grid=(TILES,),
        in_specs=[
            tile(3 * WIDTH),
            tile(WIDTH),
            tile(WIDTH),
            whole(BLOCKS, 3 * SLAB, WIDTH),
            whole(4, WIDTH),
        ],
        out_specs=[tile(WIDTH), pl.BlockSpec((2, 8, WIDTH), lambda i: (0, 0, 0))],
        out_shape=[
            jax.ShapeDtypeStruct((count, WIDTH), jnp.float32),
            jax.ShapeDtypeStruct((2, 8, WIDTH), jnp.float32),
        ],
        compiler_params=pltpu.CompilerParams(vmem_limit_bytes=VMEM_BYTES),
        cost_estimate=COST,
        name="first_input_back",
    )(projected_grad, tokens, middle_grad, weights, gains)


def arrange_kernel(place, *refs):
    ins, out = refs[:-1], refs[-1]
    across, plane, core = place[0], place[1], place[2]
    for index, ref in enumerate(ins):
        column = (across ^ (index % 4)) * 8 + (core ^ (index // 4))
        for way in range(4):
            out[column + (plane ^ way) * 2] = ref[way]


def arrange(place, pieces, name):
    rows = pieces[0].shape[1]
    return pl.pallas_call(
        arrange_kernel,
        in_specs=[pl.BlockSpec(memory_space=pltpu.SMEM)]
        + [pl.BlockSpec(memory_space=pltpu.VMEM)] * 8,
        out_shape=jax.ShapeDtypeStruct((BLOCKS, rows, WIDTH), jnp.bfloat16),
        compiler_params=pltpu.CompilerParams(vmem_limit_bytes=VMEM_BYTES),
        cost_estimate=COST,
        name=name,
    )(place, *pieces)


def adam_parts(gradient, first_moment, second_moment):
    first_next = BETA_FIRST * first_moment + (1.0 - BETA_FIRST) * gradient
    second_next = BETA_SECOND * second_moment + (1.0 - BETA_SECOND) * gradient * gradient
    direction = (
        first_next
        / (1.0 - BETA_FIRST**STEP)
        / (jnp.sqrt(second_next / (1.0 - BETA_SECOND**STEP)) + ADAM_EPS)
    )
    return (first_next, second_next, direction)


def pack_weights(part_qkv, part_out, part_up, part_down):
    return jnp.concatenate(
        [part_qkv[:, WIDTH * i : WIDTH * i + WIDTH] for i in range(3)]
        + [part_out]
        + [part_up[:, WIDTH * i : WIDTH * i + WIDTH] for i in range(4)]
        + [part_down],
        axis=0,
    ).astype(jnp.bfloat16)


def to_blocks(packed, rows):
    if rows == SLAB:
        return packed
    packed = packed[:, : 12 * rows]
    slabs = packed[:, : 8 * rows].reshape(BLOCKS, -1, 8, rows, WIDTH).transpose(0, 2, 1, 3, 4)
    return jnp.concatenate(
        [
            slabs.reshape(BLOCKS, 8 * SLAB, WIDTH),
            packed[:, 8 * rows :].reshape(BLOCKS, 4 * SLAB, WIDTH),
        ],
        axis=1,
    )


def from_blocks(grads, rows, narrow):
    if rows == SLAB:
        return grads
    slabs = grads[:, : narrow * SLAB].reshape(BLOCKS, narrow, -1, rows, WIDTH)
    slabs = slabs.transpose(0, 2, 1, 3, 4).reshape(-1, narrow * rows, WIDTH)
    if grads.shape[1] == narrow * SLAB:
        return slabs
    wide = grads[:, narrow * SLAB :].reshape(slabs.shape[0], -1, WIDTH)
    return jnp.concatenate([slabs, wide], axis=1)


def swap(array, mask):
    count = lax.axis_size("dp") * lax.axis_size("fsdp")
    return lax.ppermute(array, ("dp", "fsdp"), [(device, device ^ mask) for device in range(count)])


def after(value, *others):
    return lax.optimization_barrier((value, *others))[0]


def gather_by_chips(shards):
    results = []
    steps = [(), ()]
    for shard in shards:
        shard = after(shard, *steps[0])
        steps[0] = [swap(shard, 2 * way) for way in (1, 2, 3)]
        pieces = after(jnp.stack([shard] + steps[0]), *steps[1])
        steps[1] = [swap(pieces, 8 * way) for way in (1, 2, 3)]
        results.append([pieces] + steps[1])
    return results


def gather_cores(pieces, place, name):
    return arrange(place, pieces + [swap(piece, 1) for piece in pieces], "arrange_" + name)


def sum_at(arrays, index):
    total = sum(
        lax.dynamic_index_in_dim(array, index, 0, keepdims=False).astype(jnp.float32)
        for array in arrays
    )
    return total.astype(jnp.bfloat16)


def scatter_cores(pair, place):
    both = [array.reshape(4, 4, -1, WIDTH) for array in (pair[0], swap(pair[1], 1))]
    return [sum_at(both, place[0] ^ way) for way in (0, 3, 1, 2)]


def swap_chips(pieces):
    return [pieces[0]] + [swap(piece, 8 * way) for piece, way in zip(pieces[1:], (3, 1, 2))]


def fold_planes(pieces, place):
    return [sum_at(pieces, place[1] ^ way) for way in (0, 3, 2, 1)]


def scatter_planes(pieces, *others):
    pieces = [pieces[0]] + [swap(piece, 2 * way) for piece, way in zip(pieces[1:], (3, 2, 1))]
    pieces[0] = after(pieces[0], *others)
    return sum(piece.astype(jnp.float32) for piece in pieces)


def scatter_whole(pair, rows, narrow):
    grads = jnp.stack(pair, axis=1).reshape(BLOCKS, -1, WIDTH)
    summed = lax.psum_scatter(
        from_blocks(grads, rows, narrow), ("dp", "fsdp"), scatter_dimension=0, tiled=False
    )
    return summed.astype(jnp.float32)


def body(
    tokens,
    frame_counts,
    cotangent,
    w_qkv,
    w_out,
    w_up,
    w_down,
    norm_params,
    first_qkv,
    first_out,
    first_up,
    first_down,
    first_norm,
    second_qkv,
    second_out,
    second_up,
    second_down,
    second_norm,
):
    masters = (w_qkv, w_out, w_up, w_down)
    axes = ("dp", "fsdp")
    shards = lax.axis_size("dp") * lax.axis_size("fsdp")
    rows = w_out.shape[1]
    by_chips = (lax.axis_size("dp"), lax.axis_size("fsdp")) == (4, 8)
    fsdp = lax.axis_index("fsdp")
    place = jnp.stack([lax.axis_index("dp"), fsdp // 2, fsdp % 2]).astype(jnp.int32)
    norm_rows = jnp.pad(
        norm_params.astype(jnp.bfloat16).reshape(1, -1), ((0, rows - 1), (0, WIDTH - 8 * rows))
    )
    shard = pack_weights(w_qkv[0], w_out[0], w_up[0], w_down[0])
    second_shard = pack_weights(w_qkv[1], w_out[1], w_up[1], w_down[1])
    if by_chips:
        early, late_pieces = gather_by_chips(
            [jnp.concatenate([shard[: 4 * rows], norm_rows], axis=0), shard[4 * rows :]]
        )
        early = gather_cores(early, place, "early")
        norm_values = early[:, 4 * rows, : 8 * rows]
    else:
        gathered = lax.all_gather(jnp.concatenate([shard, norm_rows], axis=0), axes, axis=0)
        norm_values = gathered[:, 12 * rows, : 8 * rows]
        early = to_blocks(gathered, rows)
    gains = norm_values.reshape(shards, 2, 4, rows)
    gains = gains.transpose(1, 2, 0, 3).reshape(2, 4, WIDTH).astype(jnp.float32)
    weights_second = to_blocks(lax.all_gather(second_shard, axes, axis=0), rows)

    normed, projected, probs, attended, middle, hidden_in = first_attention(tokens, early, gains[0])
    if by_chips:
        late_pieces = [after(piece, hidden_in) for piece in late_pieces]
        late, late_at = gather_cores(late_pieces, place, "late"), 0
    else:
        late, late_at = early, 1
    hidden, slopes, stream = first_mlp(middle, hidden_in, late, late_at)
    core = place[2:] if by_chips else jnp.zeros((1,), jnp.int32)
    block_out, upstream, sums_second, pair_second = second_block(
        frame_counts, core, stream, cotangent, weights_second, gains[1]
    )
    if by_chips:
        second = scatter_cores(pair_second, place)
        upstream = after(upstream, *second)
        second = swap_chips(second)
    attended_grad, middle_grad, sums_late, pair_first = first_back(
        core, upstream, slopes, middle, early, late, late_at, gains[0], hidden, hidden_in, attended
    )
    if by_chips:
        second[0], *pair_first = lax.optimization_barrier((second[0], *pair_first, *second[1:]))[:3]
        first = scatter_cores(pair_first, place)
        reduced_second = scatter_planes(fold_planes(second, place))
        attended_grad = after(attended_grad, reduced_second, *first)
        first = swap_chips(first)
    projected_grad, pair_last = first_attention_back(core, projected, probs, attended_grad, normed)
    if by_chips:
        first[0], *pair_last = lax.optimization_barrier((first[0], *pair_last, *first[1:]))[:3]
        last = scatter_cores(pair_last, place)
        first[0] = after(first[0], *last)
        last = swap_chips(last)
        first = fold_planes(first, place)
        projected_grad = after(projected_grad, *first)
    tokens_grad, sums_early = first_input_back(
        projected_grad, tokens, middle_grad, early, gains[0]
    )
    if by_chips:
        last[0] = after(last[0], tokens_grad)
        last = fold_planes(last, place)
        reduced_first = scatter_planes(first, *last)
        reduced_last = scatter_planes(last)
    else:
        reduced_second = scatter_whole(pair_second, rows, 8)
        reduced_first = scatter_whole(pair_first, rows, 5)
        reduced_last = scatter_whole(pair_last, rows, 3)

    def columns(packed, first, last):
        return jnp.concatenate(
            [packed[rows * index : rows * index + rows] for index in range(first, last)], axis=1
        )

    reduced_first = (
        columns(reduced_last, 0, 3),
        columns(reduced_first, 4, 5),
        columns(reduced_first, 0, 4),
        reduced_first[5 * rows :],
    )
    reduced_second = (
        columns(reduced_second, 5, 8),
        columns(reduced_second, 4, 5),
        columns(reduced_second, 0, 4),
        reduced_second[8 * rows :],
    )

    norm_parts = jnp.concatenate(
        [jnp.sum(part, axis=1) for part in (sums_early, sums_late, sums_second)]
    )
    norm_parts = norm_parts.reshape(8, shards, rows).transpose(1, 0, 2).reshape(shards, -1)
    stacked = [jnp.stack(pair) for pair in zip(reduced_first, reduced_second)]
    firsts = (first_qkv, first_out, first_up, first_down)
    seconds = (second_qkv, second_out, second_up, second_down)
    updates = [adam_parts(*parts) for parts in zip(stacked, firsts, seconds)]
    directions = [update[2] + DECAY_RATE * master for update, master in zip(updates, masters)]
    local_squares = jnp.stack(
        [
            jnp.stack([jnp.sum(matrix * matrix, axis=(1, 2)) for matrix in group], axis=1)
            for group in (masters, directions)
        ],
        axis=2,
    )
    message = jnp.concatenate(
        [norm_parts, jnp.broadcast_to(local_squares.reshape(1, 16), (shards, 16))], axis=1
    )
    arrived = jnp.sum(lax.all_to_all(message, axes, 0, 0, tiled=True), axis=0)
    matrix_norms = jnp.sqrt(arrived[-16:].reshape(2, 4, 2))
    norm_update = adam_parts(arrived[:-16].reshape(2, 2, 2, rows), first_norm, second_norm)
    updates.append(norm_update)
    updated = [
        masters[index]
        - RATE
        * (matrix_norms[:, index, 0] / matrix_norms[:, index, 1])[:, None, None]
        * directions[index]
        for index in range(4)
    ]
    return (
        block_out,
        tokens_grad,
        *updated,
        norm_params - RATE * norm_update[2],
        *(array.astype(jnp.bfloat16) for array in updated),
        *(update[0] for update in updates),
        *(update[1] for update in updates),
        matrix_norms,
    )


def solution(mesh):
    in_specs = (
        P(("dp", "fsdp"), None),
        P(("dp", "fsdp")),
        P(("dp", "fsdp"), None),
        P(None, ("dp", "fsdp"), None),
        P(None, ("dp", "fsdp"), None),
        P(None, ("dp", "fsdp"), None),
        P(None, ("dp", "fsdp"), None),
        P(None, None, None, ("dp", "fsdp")),
        P(None, ("dp", "fsdp"), None),
        P(None, ("dp", "fsdp"), None),
        P(None, ("dp", "fsdp"), None),
        P(None, ("dp", "fsdp"), None),
        P(None, None, None, ("dp", "fsdp")),
        P(None, ("dp", "fsdp"), None),
        P(None, ("dp", "fsdp"), None),
        P(None, ("dp", "fsdp"), None),
        P(None, ("dp", "fsdp"), None),
        P(None, None, None, ("dp", "fsdp")),
    )
    out_specs = (
        P(("dp", "fsdp"), None),
        P(("dp", "fsdp"), None),
        P(None, ("dp", "fsdp"), None),
        P(None, ("dp", "fsdp"), None),
        P(None, ("dp", "fsdp"), None),
        P(None, ("dp", "fsdp"), None),
        P(None, None, None, ("dp", "fsdp")),
        P(None, ("dp", "fsdp"), None),
        P(None, ("dp", "fsdp"), None),
        P(None, ("dp", "fsdp"), None),
        P(None, ("dp", "fsdp"), None),
        P(None, ("dp", "fsdp"), None),
        P(None, ("dp", "fsdp"), None),
        P(None, ("dp", "fsdp"), None),
        P(None, ("dp", "fsdp"), None),
        P(None, None, None, ("dp", "fsdp")),
        P(None, ("dp", "fsdp"), None),
        P(None, ("dp", "fsdp"), None),
        P(None, ("dp", "fsdp"), None),
        P(None, ("dp", "fsdp"), None),
        P(None, None, None, ("dp", "fsdp")),
        P(),
    )
    return jax.shard_map(body, mesh=mesh, in_specs=in_specs, out_specs=out_specs, check_vma=False)
```

time: 371 us -> 303 us (0.82)
  Pallas kernels: 218 us -> 136 us
  starting transfers between devices: 43.4 us -> 52.5 us
  other arithmetic: 12.4 us -> 20.6 us
  local copies, waits for them, and re-layouts: 14.7 us -> 8.05 us
  waiting for transfers between devices: 54.2 us -> 59.6 us
    pallas_call x17 -> x3, Pallas kernels: 163 us -> 88.9 us  [the longest x1 53.2 us: second_block(): pl.pallas_call(second_kernel, grid=(TILES + 12,), in_specs=[pl.BlockSpec(...]
    ppermute x46 -> x41, starting transfers between devices: 43.3 us -> 52.5 us  [swap(): lax.ppermute(array, ('dp', 'fsdp'), [(device, device ^ mask) for device i...]
    pallas_call x1, Pallas kernels: 24.6 us -> 16 us  [first_attention(): pl.pallas_call(first_attention_kernel, grid=(2 * TILES + 1,), in_specs=[p...]
    unnamed x135 -> x105, local copies, waits for them, and re-layouts: 10.2 us -> 2.83 us
    convert_element_type x0 -> x3, other arithmetic: none -> 6.6 us  [sum_at(): return total.astype(jnp.bfloat16)]
    ppermute x46 -> x41, waiting for transfers between devices: 54.2 us -> 59.6 us  [swap(): lax.ppermute(array, ('dp', 'fsdp'), [(device, device ^ mask) for device i...]
  transfers between devices with their start and end apart: 47 -> 42, of which waited for: 17 -> 18; matrix products, arithmetic and copies ran while one was open for 2% -> 4% of each run, Pallas kernels for 32% -> 27%
where the time goes in v3:
time: 303 us; the launch traced here: 302 us
  Pallas kernels  136 us (45%)
  waiting for transfers between devices  59.6 us (20%)
  starting transfers between devices  52.5 us (17%)
  other arithmetic  20.6 us (7%)
  between operations  15.5 us (5%)
  blocking collectives  9.93 us (3%)
  local copies, waits for them, and re-layouts  8.05 us (3%)
    ppermute x41, waiting for transfers between devices, swap(): lax.ppermute(array, ('dp', 'fsdp'), [(device, device ^ mask) for device i...  59.6 us
    pallas_call x1, Pallas kernels, second_block(): pl.pallas_call(second_kernel, grid=(TILES + 12,), in_specs=[pl.BlockSpec(...  53.2 us
    ppermute x41, starting transfers between devices, swap(): lax.ppermute(array, ('dp', 'fsdp'), [(device, device ^ mask) for device i...  52.5 us
    pallas_call x1, Pallas kernels, first_back(): pl.pallas_call(first_back_kernel, grid=(TILES + 9,), in_specs=[pl.BlockSp...  25 us
    pallas_call x1, Pallas kernels, first_attention(): pl.pallas_call(first_attention_kernel, grid=(2 * TILES + 1,), in_specs=[p...  16 us
    pallas_call x1, Pallas kernels, first_mlp(): pl.pallas_call(first_mlp_kernel, grid=(TILES,), in_specs=[tile(WIDTH), ti...  15.9 us
    pallas_call x1, Pallas kernels, first_attention_back(): pl.pallas_call(first_attention_back_kernel, grid=(pairs + 3,), in_specs=[...  10.8 us
    all_to_all x1, blocking collectives, body(): arrived = jnp.sum(lax.all_to_all(message, axes, 0, 0, tiled=True), axis=0)  9.93 us
  transfers between devices with their start and end apart: 42, of which 18 were waited for; matrix products, arithmetic and copies ran while one was open for 4% of the time, Pallas kernels for 27%

profile of v3, /device:TPU:0, one launch (start us, length us, event | category | flops | bytes accessed | tf_op | source)
XLA Modules:
  0.0 301.8 jit_solution(592810106069816425)
XLA Ops:
  12.6 3.1 %collective-permute-start = (bf16[80,512]{1,0:T(8,128)(2,1)S(1)}, bf16[80,512]{1,0:T(8,128)(2,1)S(1)}, u32[]{:S(2)}, u32[]{:S(2)}) collective-permute-start(bf16[80,512]{1,0:T(8,128)(2,1)S(1)} %constant_dynamic-update-slice_fusion), channel_id=1, source_target_pairs={{0,2},{1,3},{2,0},{3,1},{4,6},{5,7},{6,4},{7,5},{8,10},{9,11},{10,... | collective-permute-start | bytes 245768 | tf_op jit(solution)/shard_map/ppermute | solution.py:813
  15.7 2.6 collective-permute-start.1
  18.4 6.6 %collective-permute-done.1 = bf16[80,512]{1,0:T(8,128)(2,1)S(1)} collective-permute-done((bf16[80,512]{1,0:T(8,128)(2,1)S(1)}, bf16[80,512]{1,0:T(8,128)(2,1)S(1)}, u32[]{:S(2)}, u32[]{:S(2)}) %collective-permute-start.1) | collective-permute-done | bytes 81952 | tf_op jit(solution)/shard_map/ppermute | solution.py:813
  31.6 5.2 %collective-permute-done.10 = bf16[128,512]{1,0:T(8,128)(2,1)S(1)} collective-permute-done((bf16[128,512]{1,0:T(8,128)(2,1)S(1)}, bf16[128,512]{1,0:T(8,128)(2,1)S(1)}, u32[]{:S(2)}, u32[]{:S(2)}) %collective-permute-start.10) | collective-permute-done | bytes 131104 | tf_op jit(solution)/shard_map/ppermute | solution.py:813
  42.0 5.3 %collective-permute-done.12 = bf16[128,512]{1,0:T(8,128)(2,1)S(1)} collective-permute-done((bf16[128,512]{1,0:T(8,128)(2,1)S(1)}, bf16[128,512]{1,0:T(8,128)(2,1)S(1)}, u32[]{:S(2)}, u32[]{:S(2)}) %collective-permute-start.12) | collective-permute-done | bytes 131104 | tf_op jit(solution)/shard_map/ppermute | solution.py:813
  51.5 3.3 %arrange_early.1.weights = bf16[32,80,512]{2,1,0:T(8,128)(2,1)} custom-call(s32[3]{0:T(128)} %pad_add_fusion.place, bf16[4,80,512]{2,1,0:T(8,128)(2,1)} %copy-done.5, bf16[4,80,512]{2,1,0:T(8,128)(2,1)} %copy-done.21, bf16[4,80,512]{2,1,0:T(8,128)(2,1)} %copy-done.22, bf16[4,80,512]{2,1,0:T(8,128)(2,1)} %copy-done.23, ...), custom_call_target="tpu_custom_call" | custom-call | flops 100000000 | bytes 100000 | tf_op jit(solution)/shard_map/arrange_early/pallas_call | solution.py:754
  56.6 16.0 %first_attention.1 = (bf16[1088,512]{1,0:T(8,128)(2,1)}, bf16[1088,1536]{1,0:T(8,128)(2,1)}, bf16[9,4,256,128]{3,2,1,0:T(8,128)(2,1)}, bf16[1088,512]{1,0:T(8,12...) custom-call(bf16[1088,512]{1,0:T(8,128)(2,1)} %tokens.3, bf16[32,80,512]{2,1,0:T(8,128)(2,1)} %arrange_early.1.weights, ...), custom_call_target="tpu_custom_call" | custom-call | flops 100000000 | bytes 100000 | tf_op jit(solution)/shard_map/first_attention/pallas_call | solution.py:209
  73.2 5.1 %collective-permute-done.14.refs_2_ = bf16[4,128,512]{2,1,0:T(8,128)(2,1)S(1)} collective-permute-done((bf16[4,128,512]{2,1,0:T(8,128)(2,1)S(1)}, bf16[4,128,512]{2,1,0:T(8,128)(2,1)S(1)}, u32[]{:S(2)}, u32[]{:S(2)}) %collective-permute-start.14) | collective-permute-done | bytes 524320 | tf_op jit(solution)/shard_map/ppermute | solution.py:813
  78.3 2.7 collective-permute-done.13.refs_1_
  83.4 4.5 %arrange_late.1.weights_up.weights_down = bf16[32,128,512]{2,1,0:T(8,128)(2,1)} custom-call(s32[3]{0:T(128)} %pad_add_fusion.place, bf16[4,128,512]{2,1,0:T(8,128)(2,1)} %copy-done.3, bf16[4,128,512]{2,1,0:T(8,128)(2,1)} %copy-done.18, bf16[4,128,512]{2,1,0:T(8,128)(2,1)} %copy-done.17, bf16[4,128,512]{2,1,0:T(8,128)(2,1)} %copy-done.16, ...), custom_call_target="tpu_custom_call" | custom-call | flops 100000000 | bytes 100000 | tf_op jit(solution)/shard_map/arrange_late/pallas_call | solution.py:754
  87.9 15.9 %first_mlp.1 = (bf16[1088,2048]{1,0:T(8,128)(2,1)}, bf16[1088,2048]{1,0:T(8,128)(2,1)}, f32[1088,512]{1,0:T(8,128)}) custom-call(f32[1088,512]{1,0:T(8,128)} %get-tuple-element.64.middle, bf16[1088,512]{1,0:T(8,128)(2,1)} %get-tuple-element.65.hidden_in, bf16[32,128,512]{2,1,0:T(8,128)(2,1)} %arrange_late.1.weights_up.weights_down, ...), custom_call_target="tpu_custom_call" | custom-call | flops 100000000 | bytes 100000 | tf_op jit(solution)/shard_map/first_mlp/pallas_call | solution.py:260
  103.8 53.2 %second_block.1 = (bf16[17,64,512]{2,1,0:T(8,128)(2,1)}, f32[17,64,512]{2,1,0:T(8,128)}, f32[4,8,512]{2,1,0:T(8,128)}, bf16[16,192,512]{2,1,0:T(8,128)(2,1)}, bf16[16,192,512]{2,1,0:T(8,128)(2,1)}) custom-call(s32[1]{0:T(128)S(6)} %copy.87.frame_count, s32[1]{0:T(128)} %bitcast.core, f32[17,64,512]{2,1,0:T(8,128)} %bitcast.153, ...), custom_call_target="tpu_custom_call" | custom-call | flops 100000000 | bytes 100000 | tf_op jit(solution)/shard_map/second_block/pallas_call | solution.py:459
  157.6 5.5 %collective-permute-done.20 = bf16[16,192,512]{2,1,0:T(8,128)(2,1)S(1)} collective-permute-done((bf16[16,192,512]{2,1,0:T(8,128)(2,1)}, bf16[16,192,512]{2,1,0:T(8,128)(2,1)S(1)}, u32[]{:S(2)}, u32[]{:S(2)}) %collective-permute-start.20) | collective-permute-done | bytes 3145760 | tf_op jit(solution)/shard_map/ppermute | solution.py:813
  163.1 3.7 %fusion.3 = (bf16[4,192,512]{2,1,0:T(8,128)(2,1)S(1)}, bf16[4,192,512]{2,1,0:T(8,128)(2,1)S(1)}, bf16[4,192,512]{2,1,0:T(8,128)(2,1)S(1)}, bf16[4,192,512]{2,1,0:T(8,128)(2,1)}) fusion(bf16[4,4,192,512]{3,2,1,0:T(8,128)(2,1)S(1)} %bitcast.149, s32[]{:T(128)S(6)} %select_n.110, bf16[4,4,192,512]{3,2,1,0:T(8,128)(2,1)} %bitcast.148, s32[]{:T(128)S(6)} %select_n.109, ...), kind=kLoop, calls=%fused_computation.11 | loop fusion | flops 6291456 | bytes 9437200 | tf_op jit(solution)/shard_map/convert_element_type | solution.py:841
  170.3 25.0 %first_back.1 = (bf16[1088,512]{1,0:T(8,128)(2,1)}, f32[1088,512]{1,0:T(8,128)}, f32[2,8,512]{2,1,0:T(8,128)}, bf16[16,144,512]{2,1,0:T(8,128)(2,1)}, bf16[16,144,512]{2,1,0:T(8,128)(2,1)}) custom-call(s32[1]{0:T(128)} %bitcast.core, f32[1088,512]{1,0:T(8,128)} %bitcast.152, bf16[1088,2048]{1,0:T(8,128)(2,1)} %get-tuple-element.80.slopes, ...), custom_call_target="tpu_custom_call" | custom-call | flops 100000000 | bytes 100000 | tf_op jit(solution)/shard_map/first_back/pallas_call | solution.py:579
  195.3 8.3 %collective-permute-done.22 = bf16[4,192,512]{2,1,0:T(8,128)(2,1)} collective-permute-done((bf16[4,192,512]{2,1,0:T(8,128)(2,1)S(1)}, bf16[4,192,512]{2,1,0:T(8,128)(2,1)}, u32[]{:S(2)}, u32[]{:S(2)}) %collective-permute-start.22) | collective-permute-done | bytes 786464 | tf_op jit(solution)/shard_map/ppermute | solution.py:813
  206.8 3.0 collective-permute-start.24
  216.2 8.8 %collective-permute-start.26 = (bf16[192,512]{1,0:T(8,128)(2,1)S(1)}, bf16[192,512]{1,0:T(8,128)(2,1)S(1)}, u32[]{:S(2)}, u32[]{:S(2)}) collective-permute-start(bf16[192,512]{1,0:T(8,128)(2,1)S(1)} %get-tuple-element.234), channel_id=1, source_target_pairs={{0,2},{1,3},{2,0},{3,1},{4,6},{5,7},{6,4},{7,5},{8,10},{9,11},{10,... | collective-permute-start | bytes 589832 | tf_op jit(solution)/shard_map/ppermute | solution.py:813
  225.0 3.5 %collective-permute-done.25 = bf16[192,512]{1,0:T(8,128)(2,1)S(1)} collective-permute-done((bf16[192,512]{1,0:T(8,128)(2,1)S(1)}, bf16[192,512]{1,0:T(8,128)(2,1)S(1)}, u32[]{:S(2)}, u32[]{:S(2)}) %collective-permute-start.25) | collective-permute-done | bytes 196640 | tf_op jit(solution)/shard_map/ppermute | solution.py:813
  228.5 4.1 %collective-permute-done.26 = bf16[192,512]{1,0:T(8,128)(2,1)S(1)} collective-permute-done((bf16[192,512]{1,0:T(8,128)(2,1)S(1)}, bf16[192,512]{1,0:T(8,128)(2,1)S(1)}, u32[]{:S(2)}, u32[]{:S(2)}) %collective-permute-start.26) | collective-permute-done | bytes 196640 | tf_op jit(solution)/shard_map/ppermute | solution.py:813
  232.8 10.8 %first_attention_back.1 = (bf16[1088,1536]{1,0:T(8,128)(2,1)}, bf16[16,48,512]{2,1,0:T(8,128)(2,1)}, bf16[16,48,512]{2,1,0:T(8,128)(2,1)}) custom-call(s32[1]{0:T(128)} %bitcast.core, bf16[1088,1536]{1,0:T(8,128)(2,1)} %get-tuple-element.74.queries_in.keys_in.values_in, bf16[1088,1536]{1,0:T(8,128)(2,1)} %get-tuple-element.74.queries_in.keys_in.values_in, ...), custom_call_target="tpu_custom_call" | custom-call | flops 100000000 | bytes 100000 | tf_op jit(solution)/shard_map/first_attention_back/pallas_call | solution.py:667
  256.1 6.9 %first_input_back.1 = (f32[1088,512]{1,0:T(8,128)}, f32[2,8,512]{2,1,0:T(8,128)}) custom-call(bf16[1088,1536]{1,0:T(8,128)(2,1)} %get-tuple-element.98.projected_grad, bf16[1088,512]{1,0:T(8,128)(2,1)} %tokens.3, f32[1088,512]{1,0:T(8,128)} %get-tuple-element.99.middle_grad, bf16[32,80,512]{2,1,0:T(8,128)(2,1)} %arrange_early.1.weights, f32[4,512]{1,0:T(4,128)} %squeeze.118.gains), custom_call_target="tpu_custom_call" | custom-call | flops 100000000 | bytes 100000 | tf_op jit(solution)/shard_map/first_input_back/pallas_call | solution.py:722
  268.1 3.1 %collective-permute-done.40 = bf16[144,512]{1,0:T(8,128)(2,1)S(1)} collective-permute-done((bf16[144,512]{1,0:T(8,128)(2,1)}, bf16[144,512]{1,0:T(8,128)(2,1)S(1)}, u32[]{:S(2)}, u32[]{:S(2)}) %collective-permute-start.40) | collective-permute-done | bytes 147488 | tf_op jit(solution)/shard_map/ppermute | solution.py:813
  279.8 9.9 %all_to_all.9 = f32[32,1,144]{2,1,0:T(1,128)S(1)} all-to-all(f32[32,1,144]{2,1,0:T(1,128)S(1)} %all_to_all.6), channel_id=1, replica_groups=mesh['dp'=4,'fsdp'=8] {'dp','fsdp'}, dimensions={0} | all-to-all | bytes 36864 | tf_op jit(solution)/shard_map/all_to_all | solution.py:999
  (242 shorter events, 70.3 us)
Async XLA Ops:
  7.2 96.6 %all-gather.2.cloned.1.call-start = ((), (), s32[]{:S(2)}) async-start(), calls=%async_computation.1 | async-start | bytes 6488064 | tf_op jit(solution)/shard_map/all_gather | solution.py:915
  25.0 11.8 %collective-permute-start.3 = (bf16[4,80,512]{2,1,0:T(8,128)(2,1)S(1)}, bf16[4,80,512]{2,1,0:T(8,128)(2,1)S(1)}, u32[]{:S(2)}, u32[]{:S(2)}) collective-permute-start(bf16[4,80,512]{2,1,0:T(8,128)(2,1)S(1)} %pad_maximum_fusion.1.refs_0_), channel_id=1, source_target_pairs={{0,8},{1,9},{2,10},{3,11},{4,12},{5,13},{6,14},{7,15},{8,0},{9,1},... | collective-permute-start | bytes 983048 | tf_op jit(solution)/shard_map/ppermute | solution.py:813
  26.5 14.4 %collective-permute-start.4 = (bf16[4,80,512]{2,1,0:T(8,128)(2,1)S(1)}, bf16[4,80,512]{2,1,0:T(8,128)(2,1)S(1)}, u32[]{:S(2)}, u32[]{:S(2)}) collective-permute-start(bf16[4,80,512]{2,1,0:T(8,128)(2,1)S(1)} %pad_maximum_fusion.1.refs_0_), channel_id=1, source_target_pairs={{0,16},{1,17},{2,18},{3,19},{4,20},{5,21},{6,22},{7,23},{8,24},{9,... | collective-permute-start | bytes 983048 | tf_op jit(solution)/shard_map/ppermute | solution.py:813
  28.1 13.9 %collective-permute-start.5 = (bf16[4,80,512]{2,1,0:T(8,128)(2,1)S(1)}, bf16[4,80,512]{2,1,0:T(8,128)(2,1)S(1)}, u32[]{:S(2)}, u32[]{:S(2)}) collective-permute-start(bf16[4,80,512]{2,1,0:T(8,128)(2,1)S(1)} %pad_maximum_fusion.1.refs_0_), channel_id=1, source_target_pairs={{0,24},{1,25},{2,26},{3,27},{4,28},{5,29},{6,30},{7,31},{8,16},{9,... | collective-permute-start | bytes 983048 | tf_op jit(solution)/shard_map/ppermute | solution.py:813
  36.8 11.8 %collective-permute-start.6 = (bf16[4,80,512]{2,1,0:T(8,128)(2,1)S(1)}, bf16[4,80,512]{2,1,0:T(8,128)(2,1)}, u32[]{:S(2)}, u32[]{:S(2)}) collective-permute-start(bf16[4,80,512]{2,1,0:T(8,128)(2,1)S(1)} %pad_maximum_fusion.1.refs_0_), channel_id=1, source_target_pairs={{0,1},{1,0},{2,3},{3,2},{4,5},{5,4},{6,7},{7,6},{8,9},{9,8},{10,11... | collective-permute-start | bytes 983048 | tf_op jit(solution)/shard_map/ppermute | solution.py:813
  36.8 13.9 %collective-permute-start.7 = (bf16[4,80,512]{2,1,0:T(8,128)(2,1)S(1)}, bf16[4,80,512]{2,1,0:T(8,128)(2,1)}, u32[]{:S(2)}, u32[]{:S(2)}) collective-permute-start(bf16[4,80,512]{2,1,0:T(8,128)(2,1)S(1)} %collective-permute-done.3.refs_1_), channel_id=1, source_target_pairs={{0,1},{1,0},{2,3},{3,2},{4,5},{5,4},{6,7},{7,6},{8,9},{9,8},{10,11... | collective-permute-start | bytes 983048 | tf_op jit(solution)/shard_map/ppermute | solution.py:813
  41.0 10.5 %collective-permute-start.8 = (bf16[4,80,512]{2,1,0:T(8,128)(2,1)S(1)}, bf16[4,80,512]{2,1,0:T(8,128)(2,1)}, u32[]{:S(2)}, u32[]{:S(2)}) collective-permute-start(bf16[4,80,512]{2,1,0:T(8,128)(2,1)S(1)} %collective-permute-done.4.refs_2_), channel_id=1, source_target_pairs={{0,1},{1,0},{2,3},{3,2},{4,5},{5,4},{6,7},{7,6},{8,9},{9,8},{10,11... | collective-permute-start | bytes 983048 | tf_op jit(solution)/shard_map/ppermute | solution.py:813
  47.4 25.3 %collective-permute-start.15 = (bf16[4,128,512]{2,1,0:T(8,128)(2,1)S(1)}, bf16[4,128,512]{2,1,0:T(8,128)(2,1)S(1)}, u32[]{:S(2)}, u32[]{:S(2)}) collective-permute-start(bf16[4,128,512]{2,1,0:T(8,128)(2,1)S(1)} %pad_maximum_fusion.refs_0_), channel_id=1, source_target_pairs={{0,24},{1,25},{2,26},{3,27},{4,28},{5,29},{6,30},{7,31},{8,16},{9,... | collective-permute-start | bytes 1572872 | tf_op jit(solution)/shard_map/ppermute | solution.py:813
  48.6 29.7 %collective-permute-start.14 = (bf16[4,128,512]{2,1,0:T(8,128)(2,1)S(1)}, bf16[4,128,512]{2,1,0:T(8,128)(2,1)S(1)}, u32[]{:S(2)}, u32[]{:S(2)}) collective-permute-start(bf16[4,128,512]{2,1,0:T(8,128)(2,1)S(1)} %pad_maximum_fusion.refs_0_), channel_id=1, source_target_pairs={{0,16},{1,17},{2,18},{3,19},{4,20},{5,21},{6,22},{7,23},{8,24},{9,... | collective-permute-start | bytes 1572872 | tf_op jit(solution)/shard_map/ppermute | solution.py:813
  50.7 30.3 %collective-permute-start.13 = (bf16[4,128,512]{2,1,0:T(8,128)(2,1)S(1)}, bf16[4,128,512]{2,1,0:T(8,128)(2,1)S(1)}, u32[]{:S(2)}, u32[]{:S(2)}) collective-permute-start(bf16[4,128,512]{2,1,0:T(8,128)(2,1)S(1)} %pad_maximum_fusion.refs_0_), channel_id=1, source_target_pairs={{0,8},{1,9},{2,10},{3,11},{4,12},{5,13},{6,14},{7,15},{8,0},{9,1},... | collective-permute-start | bytes 1572872 | tf_op jit(solution)/shard_map/ppermute | solution.py:813
  72.6 9.8 %collective-permute-start.16 = (bf16[4,128,512]{2,1,0:T(8,128)(2,1)S(1)}, bf16[4,128,512]{2,1,0:T(8,128)(2,1)S(1)}, u32[]{:S(2)}, u32[]{:S(2)}) collective-permute-start(bf16[4,128,512]{2,1,0:T(8,128)(2,1)S(1)} %pad_maximum_fusion.refs_0_), channel_id=1, source_target_pairs={{0,1},{1,0},{2,3},{3,2},{4,5},{5,4},{6,7},{7,6},{8,9},{9,8},{10,11... | collective-permute-start | bytes 1572872 | tf_op jit(solution)/shard_map/ppermute | solution.py:813
  166.8 28.5 %collective-permute-start.21 = (bf16[4,192,512]{2,1,0:T(8,128)(2,1)S(1)}, bf16[4,192,512]{2,1,0:T(8,128)(2,1)}, u32[]{:S(2)}, u32[]{:S(2)}) collective-permute-start(bf16[4,192,512]{2,1,0:T(8,128)(2,1)S(1)} %get-tuple-element.227), channel_id=1, source_target_pairs={{0,24},{1,25},{2,26},{3,27},{4,28},{5,29},{6,30},{7,31},{8,16},{9,... | collective-permute-start | bytes 2359304 | tf_op jit(solution)/shard_map/ppermute | solution.py:813
  168.5 35.1 %collective-permute-start.22 = (bf16[4,192,512]{2,1,0:T(8,128)(2,1)S(1)}, bf16[4,192,512]{2,1,0:T(8,128)(2,1)}, u32[]{:S(2)}, u32[]{:S(2)}) collective-permute-start(bf16[4,192,512]{2,1,0:T(8,128)(2,1)S(1)} %get-tuple-element.226), channel_id=1, source_target_pairs={{0,8},{1,9},{2,10},{3,11},{4,12},{5,13},{6,14},{7,15},{8,0},{9,1},... | collective-permute-start | bytes 2359304 | tf_op jit(solution)/shard_map/ppermute | solution.py:813
  168.8 35.7 %collective-permute-start.23 = (bf16[4,192,512]{2,1,0:T(8,128)(2,1)S(1)}, bf16[4,192,512]{2,1,0:T(8,128)(2,1)}, u32[]{:S(2)}, u32[]{:S(2)}) collective-permute-start(bf16[4,192,512]{2,1,0:T(8,128)(2,1)S(1)} %get-tuple-element.225), channel_id=1, source_target_pairs={{0,16},{1,17},{2,18},{3,19},{4,20},{5,21},{6,22},{7,23},{8,24},{9,... | collective-permute-start | bytes 2359304 | tf_op jit(solution)/shard_map/ppermute | solution.py:813
  210.5 33.0 %collective-permute-start.28 = (bf16[4,144,512]{2,1,0:T(8,128)(2,1)S(1)}, bf16[4,144,512]{2,1,0:T(8,128)(2,1)S(1)}, u32[]{:S(2)}, u32[]{:S(2)}) collective-permute-start(bf16[4,144,512]{2,1,0:T(8,128)(2,1)S(1)} %get-tuple-element.231), channel_id=1, source_target_pairs={{0,24},{1,25},{2,26},{3,27},{4,28},{5,29},{6,30},{7,31},{8,16},{9,... | collective-permute-start | bytes 1769480 | tf_op jit(solution)/shard_map/ppermute | solution.py:813
  212.1 31.4 %collective-permute-start.29 = (bf16[4,144,512]{2,1,0:T(8,128)(2,1)S(1)}, bf16[4,144,512]{2,1,0:T(8,128)(2,1)S(1)}, u32[]{:S(2)}, u32[]{:S(2)}) collective-permute-start(bf16[4,144,512]{2,1,0:T(8,128)(2,1)S(1)} %get-tuple-element.230), channel_id=1, source_target_pairs={{0,8},{1,9},{2,10},{3,11},{4,12},{5,13},{6,14},{7,15},{8,0},{9,1},... | collective-permute-start | bytes 1769480 | tf_op jit(solution)/shard_map/ppermute | solution.py:813
  213.4 30.2 %collective-permute-start.30 = (bf16[4,144,512]{2,1,0:T(8,128)(2,1)S(1)}, bf16[4,144,512]{2,1,0:T(8,128)(2,1)S(1)}, u32[]{:S(2)}, u32[]{:S(2)}) collective-permute-start(bf16[4,144,512]{2,1,0:T(8,128)(2,1)S(1)} %get-tuple-element.229), channel_id=1, source_target_pairs={{0,16},{1,17},{2,18},{3,19},{4,20},{5,21},{6,22},{7,23},{8,24},{9,... | collective-permute-start | bytes 1769480 | tf_op jit(solution)/shard_map/ppermute | solution.py:813
  214.1 14.5 %collective-permute-start.25 = (bf16[192,512]{1,0:T(8,128)(2,1)S(1)}, bf16[192,512]{1,0:T(8,128)(2,1)S(1)}, u32[]{:S(2)}, u32[]{:S(2)}) collective-permute-start(bf16[192,512]{1,0:T(8,128)(2,1)S(1)} %get-tuple-element.235), channel_id=1, source_target_pairs={{0,4},{1,5},{2,6},{3,7},{4,0},{5,1},{6,2},{7,3},{8,12},{9,13},{10,... | collective-permute-start | bytes 589832 | tf_op jit(solution)/shard_map/ppermute | solution.py:813
  216.2 16.4 %collective-permute-start.26 = (bf16[192,512]{1,0:T(8,128)(2,1)S(1)}, bf16[192,512]{1,0:T(8,128)(2,1)S(1)}, u32[]{:S(2)}, u32[]{:S(2)}) collective-permute-start(bf16[192,512]{1,0:T(8,128)(2,1)S(1)} %get-tuple-element.234), channel_id=1, source_target_pairs={{0,2},{1,3},{2,0},{3,1},{4,6},{5,7},{6,4},{7,5},{8,10},{9,11},{10,... | collective-permute-start | bytes 589832 | tf_op jit(solution)/shard_map/ppermute | solution.py:813
  249.0 14.8 %collective-permute-start.32 = (bf16[4,48,512]{2,1,0:T(8,128)(2,1)}, bf16[4,48,512]{2,1,0:T(8,128)(2,1)S(1)}, u32[]{:S(2)}, u32[]{:S(2)}) collective-permute-start(bf16[4,48,512]{2,1,0:T(8,128)(2,1)} %get-tuple-element.243), channel_id=1, source_target_pairs={{0,24},{1,25},{2,26},{3,27},{4,28},{5,29},{6,30},{7,31},{8,16},{9,... | collective-permute-start | bytes 589832 | tf_op jit(solution)/shard_map/ppermute | solution.py:813
  251.5 15.2 %collective-permute-start.33 = (bf16[4,48,512]{2,1,0:T(8,128)(2,1)}, bf16[4,48,512]{2,1,0:T(8,128)(2,1)S(1)}, u32[]{:S(2)}, u32[]{:S(2)}) collective-permute-start(bf16[4,48,512]{2,1,0:T(8,128)(2,1)} %get-tuple-element.242), channel_id=1, source_target_pairs={{0,8},{1,9},{2,10},{3,11},{4,12},{5,13},{6,14},{7,15},{8,0},{9,1},... | collective-permute-start | bytes 589832 | tf_op jit(solution)/shard_map/ppermute | solution.py:813
  252.0 14.7 %collective-permute-start.34 = (bf16[4,48,512]{2,1,0:T(8,128)(2,1)}, bf16[4,48,512]{2,1,0:T(8,128)(2,1)S(1)}, u32[]{:S(2)}, u32[]{:S(2)}) collective-permute-start(bf16[4,48,512]{2,1,0:T(8,128)(2,1)} %get-tuple-element.241), channel_id=1, source_target_pairs={{0,16},{1,17},{2,18},{3,19},{4,20},{5,21},{6,22},{7,23},{8,24},{9,... | collective-permute-start | bytes 589832 | tf_op jit(solution)/shard_map/ppermute | solution.py:813
  254.2 12.6 %collective-permute-start.38 = (bf16[144,512]{1,0:T(8,128)(2,1)}, bf16[144,512]{1,0:T(8,128)(2,1)S(1)}, u32[]{:S(2)}, u32[]{:S(2)}) collective-permute-start(bf16[144,512]{1,0:T(8,128)(2,1)} %get-tuple-element.239), channel_id=1, source_target_pairs={{0,6},{1,7},{2,4},{3,5},{4,2},{5,3},{6,0},{7,1},{8,14},{9,15},{10,... | collective-permute-start | bytes 442376 | tf_op jit(solution)/shard_map/ppermute | solution.py:813
  256.1 12.0 %collective-permute-start.39 = (bf16[144,512]{1,0:T(8,128)(2,1)}, bf16[144,512]{1,0:T(8,128)(2,1)S(1)}, u32[]{:S(2)}, u32[]{:S(2)}) collective-permute-start(bf16[144,512]{1,0:T(8,128)(2,1)} %get-tuple-element.238), channel_id=1, source_target_pairs={{0,4},{1,5},{2,6},{3,7},{4,0},{5,1},{6,2},{7,3},{8,12},{9,13},{10,... | collective-permute-start | bytes 442376 | tf_op jit(solution)/shard_map/ppermute | solution.py:813
  (62 other events, 514.5 us)
Sparse Core Ops, SparseCore 0:
  11.9 82.0 all-gather.1

commit v4 on v3

--- a/solution.py
+++ b/solution.py
@@ -17,7 +17,6 @@
 TILE = FRAMES * WIN // TILES
 SPOTS = WIN // TILES
 HALF = TILE // 2
-GROUP = 9
 SCALE = HEAD_DIM ** (-0.5)
 VMEM_BYTES = 56 * 2**20
 COST = pl.CostEstimate(flops=10**8, bytes_accessed=10**5, transcendentals=0)
@@ -241,13 +240,16 @@
 
 def first_mlp_kernel(middle, hidden_in, weights_up, weights_down, hidden_out, slope_out, result_out):
     result = middle[...]
+    upward = dot_nn(hidden_in[...], slab(weights_up, 0))
     for index in range(4):
         columns = slice(WIDTH * index, WIDTH * index + WIDTH)
-        value, slope = gelu_pair(dot_nn(hidden_in[...], slab(weights_up, index)))
+        following = dot_nn(hidden_in[...], slab(weights_up, index + 1)) if index < 3 else None
+        value, slope = gelu_pair(upward)
         hidden = value.astype(jnp.bfloat16)
         hidden_out[:, columns] = hidden
         slope_out[:, columns] = slope.astype(jnp.bfloat16)
         result = result + dot_nn(hidden, down_rows(weights_down, index))
+        upward = following
     result_out[...] = result
 
 
@@ -352,13 +354,16 @@
         hidden_in_tile = (normal_second * gains[2:3, :] + gains[3:4, :]).astype(jnp.bfloat16)
         hidden_in[rows, :] = hidden_in_tile
         result = middle
+        upward = dot_nn(hidden_in_tile, slab(weights_up, 0))
         for index in range(4):
             columns = slice(WIDTH * index, WIDTH * index + WIDTH)
-            value, slope = gelu_pair(dot_nn(hidden_in_tile, slab(weights_up, index)))
+            following = dot_nn(hidden_in_tile, slab(weights_up, index + 1)) if index < 3 else None
+            value, slope = gelu_pair(upward)
             hidden_tile = value.astype(jnp.bfloat16)
             hidden[rows, columns] = hidden_tile
             slopes[:, columns] = slope
             result = result + dot_nn(hidden_tile, down_rows(weights_down, index))
+            upward = following
         keep(result_out, result)
 
         upstream = flat(cotangent)
@@ -520,9 +525,12 @@
 
 def first_back_kernel(
     core, upstream, slopes, middle, weights, weights_up, weights_down, gains, hidden, hidden_in,
-    attended, attended_grad_out, middle_grad_out, sums, mine, other, up_grads, out_grads, branch_grads,
+    attended, queries_in, keys_in, values_in, probs, normed, middle_grad_out, sums, projected_grad_out,
+    mine, other, up_grads, out_grads, branch_grads, attended_grads, projected_grads,
 ):
     step = pl.program_id(0)
+    heads_at = TILES + 9
+    last_at = heads_at + HEADS // 2
 
     @pl.when(step == 0)
     def _():
@@ -548,7 +556,9 @@
         middle_grad_out[...] = middle_grad
         branch_grad = middle_grad.astype(jnp.bfloat16)
         branch_grads[rows, :] = branch_grad
-        attended_grad_out[...] = dot_nt(branch_grad, slab(weights, 3)).astype(jnp.bfloat16)
+        attended_grad = dot_nt(branch_grad, slab(weights, 3)).astype(jnp.bfloat16)
+        for pair in range(HEADS // 2):
+            attended_grads[pair, rows, :] = attended_grad[:, 128 * pair : 128 * pair + 128]
 
     @pl.when((step >= TILES) & (step < TILES + 4))
     def _():
@@ -558,27 +568,71 @@
     @pl.when((step >= TILES + 4) & (step < TILES + 8))
     def _():
         block = (step - TILES - 4) * 4
-        outer_store(core, hidden, out_grads[...], mine, other, block, 5 * SLAB, 4 * SLAB)
+        outer_store(core, hidden, out_grads[...], mine, other, block, 8 * SLAB, 4 * SLAB)
 
     @pl.when(step == TILES + 8)
     def _():
         outer_store(core, attended, branch_grads[...], mine, other, 0, 4 * SLAB, SLAB)
 
+    @pl.when((step >= heads_at) & (step < last_at))
+    def _():
+        pair = step - heads_at
+        frames = list(enumerate(frame_pairs()))
+        rows = [slice(WIN * frame, WIN * frame + 2 * WIN) for _, frame in frames]
+        grads = [stack_heads(attended_grads[pair, row, :]) for row in rows]
+        share_grads = [dot_nt(grad, values_in[row, :]) for grad, row in zip(grads, rows)]
+        shares = [probs[index, 0] for index, _ in frames]
+        value_grads = [dot_tn(share, grad) for share, grad in zip(shares, grads)]
+        score_grads = []
+        for share, share_grad in zip(shares, share_grads):
+            share = share.astype(jnp.float32)
+            total = jnp.sum(share_grad * share, axis=-1, keepdims=True)
+            score_grads.append((share * (share_grad - total)).astype(jnp.bfloat16))
+        query_grads = [dot_nn(grad, keys_in[row, :]) for grad, row in zip(score_grads, rows)]
+        key_grads = [
+            dot_tn(grad, stack_heads(queries_in[row, :] * SCALE))
+            for grad, row in zip(score_grads, rows)
+        ]
+        query_grads = [merge_heads(grad) * SCALE for grad in query_grads]
+        for index, parts in enumerate((query_grads, key_grads, value_grads)):
+            lanes = pl.ds(pl.multiple_of(pair * 128 + WIDTH * index, 128), 128)
+            for row, part in zip(rows, parts):
+                projected_grads[row, lanes] = part.astype(jnp.bfloat16)
+
+    @pl.when(step >= last_at)
+    def _():
+        right = projected_grads[:, part_of(step, last_at)]
+        projected_grad_out[...] = right
+        outer_store(core, normed, right, mine, other, 0, slab_row(step, last_at - 5), SLAB)
+
 
 def first_back(
-    core, upstream, slopes, middle, weights, late_weights, late_at, gains, hidden, hidden_in, attended
+    core, upstream, slopes, middle, weights, late_weights, late_at, gains, hidden, hidden_in, attended,
+    projected, probs, normed,
 ):
     count = upstream.shape[0]
+    pairs = HEADS // 2
+    heads_at = TILES + 9
+    last_at = heads_at + pairs
 
     def tile(width):
         return pl.BlockSpec((TILE, width), lambda i: (jnp.minimum(i, TILES - 1), 0))
 
     def whole(*shape):
-        return pl.BlockSpec(shape, lambda i: (0,) * len(shape))
+        return pl.BlockSpec(shape, lambda i: (0,) * len(shape), pipeline_mode=pl.Buffered(1))
+
+    def pair_of(step):
+        return jnp.clip(step - heads_at, 0, pairs - 1)
+
+    def lanes(first):
+        return pl.BlockSpec((count, 128), lambda i: (0, first + pair_of(i)))
+
+    def held(width):
+        return pltpu.VMEM((count, width * WIDTH), jnp.bfloat16)
 
     outs = pl.pallas_call(
         first_back_kernel,
-        grid=(TILES + 9,),
+        grid=(last_at + 3,),
         in_specs=[
             pl.BlockSpec(memory_space=pltpu.SMEM),
             tile(WIDTH),
@@ -591,108 +645,41 @@
             pl.BlockSpec((count, WIDTH), lambda i: (0, jnp.clip(i - TILES - 4, 0, 3))),
             whole(count, WIDTH),
             whole(count, WIDTH),
+            lanes(0),
+            lanes(pairs),
+            lanes(2 * pairs),
+            pl.BlockSpec(
+                ((FRAMES + 1) // 2, 1, 4 * WIN, 2 * WIN), lambda i: (0, pair_of(i), 0, 0)
+            ),
+            whole(count, WIDTH),
         ],
         out_specs=[
             tile(WIDTH),
-            tile(WIDTH),
-            whole(2, 8, WIDTH),
-            *grad_specs(9 * SLAB),
+            pl.BlockSpec((2, 8, WIDTH), lambda i: (0, 0, 0)),
+            pl.BlockSpec((count, WIDTH), lambda i: (0, jnp.clip(i - last_at, 0, 2))),
+            *grad_specs(12 * SLAB),
         ],
         out_shape=[
-            jax.ShapeDtypeStruct((count, WIDTH), jnp.bfloat16),
             jax.ShapeDtypeStruct((count, WIDTH), jnp.float32),
             jax.ShapeDtypeStruct((2, 8, WIDTH), jnp.float32),
-            *grad_shapes(9 * SLAB),
+            jax.ShapeDtypeStruct((count, 3 * WIDTH), jnp.bfloat16),
+            *grad_shapes(12 * SLAB),
         ],
         scratch_shapes=[
-            pltpu.VMEM((count, 4 * WIDTH), jnp.bfloat16),
-            pltpu.VMEM((count, WIDTH), jnp.bfloat16),
-            pltpu.VMEM((count, WIDTH), jnp.bfloat16),
+            held(4),
+            held(1),
+            held(1),
+            pltpu.VMEM((pairs, count, 128), jnp.bfloat16),
+            held(3),
         ],
         compiler_params=pltpu.CompilerParams(vmem_limit_bytes=VMEM_BYTES),
         cost_estimate=COST,
         name="first_back",
     )(
         core, upstream, slopes, middle, weights, late_weights, late_weights, gains, hidden, hidden_in,
-        attended,
+        attended, projected, projected, projected, probs, normed,
     )
     return (*outs[:3], tuple(outs[3:]))
-
-
-def first_attention_back_kernel(
-    core, queries_in, keys_in, values_in, probs, attended_grad, normed, projected_grad_out, mine,
-    other, projected_grads,
-):
-    step = pl.program_id(0)
-
-    @pl.when(step < HEADS // 2)
-    def _():
-        frames = list(enumerate(frame_pairs()))
-        for some in (frames[at : at + GROUP] for at in range(0, len(frames), GROUP)):
-            rows = [slice(WIN * frame, WIN * frame + 2 * WIN) for _, frame in some]
-            out_grads = [stack_heads(attended_grad[row, :]) for row in rows]
-            share_grads = [dot_nt(grad, values_in[row, :]) for grad, row in zip(out_grads, rows)]
-            shares = [probs[index, 0] for index, _ in some]
-            value_grads = [dot_tn(share, grad) for share, grad in zip(shares, out_grads)]
-            score_grads = []
-            for share, share_grad in zip(shares, share_grads):
-                weights = share.astype(jnp.float32)
-                total = jnp.sum(share_grad * weights, axis=-1, keepdims=True)
-                score_grads.append((weights * (share_grad - total)).astype(jnp.bfloat16))
-            query_grads = [dot_nn(grad, keys_in[row, :]) for grad, row in zip(score_grads, rows)]
-            key_grads = [
-                dot_tn(grad, stack_heads(queries_in[row, :] * SCALE))
-                for grad, row in zip(score_grads, rows)
-            ]
-            query_grads = [merge_heads(grad) * SCALE for grad in query_grads]
-            for index, grads in enumerate((query_grads, key_grads, value_grads)):
-                lanes = pl.ds(pl.multiple_of(step * 128 + WIDTH * index, 128), 128)
-                for row, grad in zip(rows, grads):
-                    projected_grads[row, lanes] = grad.astype(jnp.bfloat16)
-
-    @pl.when(step >= HEADS // 2)
-    def _():
-        right = projected_grads[:, part_of(step, HEADS // 2)]
-        projected_grad_out[...] = right
-        outer_store(core, normed, right, mine, other, 0, slab_row(step, HEADS // 2), SLAB)
-
-
-def first_attention_back(core, projected, probs, attended_grad, normed):
-    count = projected.shape[0]
-    pairs = HEADS // 2
-
-    def lanes(first):
-        return pl.BlockSpec((count, 128), lambda i: (0, first + jnp.minimum(i, pairs - 1)))
-
-    outs = pl.pallas_call(
-        first_attention_back_kernel,
-        grid=(pairs + 3,),
-        in_specs=[
-            pl.BlockSpec(memory_space=pltpu.SMEM),
-            lanes(0),
-            lanes(pairs),
-            lanes(2 * pairs),
-            pl.BlockSpec(
-                ((FRAMES + 1) // 2, 1, 4 * WIN, 2 * WIN),
-                lambda i: (0, jnp.minimum(i, pairs - 1), 0, 0),
-            ),
-            lanes(0),
-            pl.BlockSpec((count, WIDTH), lambda i: (0, 0)),
-        ],
-        out_specs=[
-            pl.BlockSpec((count, WIDTH), lambda i: (0, jnp.clip(i - pairs, 0, 2))),
-            *grad_specs(3 * SLAB),
-        ],
-        out_shape=[
-            jax.ShapeDtypeStruct((count, 3 * WIDTH), jnp.bfloat16),
-            *grad_shapes(3 * SLAB),
-        ],
-        scratch_shapes=[pltpu.VMEM((count, 3 * WIDTH), jnp.bfloat16)],
-        compiler_params=pltpu.CompilerParams(vmem_limit_bytes=VMEM_BYTES),
-        cost_estimate=COST,
-        name="first_attention_back",
-    )(core, projected, projected, projected, probs, attended_grad, normed)
-    return outs[0], tuple(outs[1:])
 
 
 def first_input_back_kernel(projected_grad, tokens, middle_grad, weights, gains, grad_out, sums):
@@ -760,6 +747,37 @@
         cost_estimate=COST,
         name=name,
     )(place, *pieces)
+
+
+def pack_kernel(w_qkv, w_out, w_up, w_down, norm, early, late, second):
+    def narrow(array):
+        return array.astype(jnp.bfloat16)
+
+    for block, (start, rest) in enumerate(((early, late), (second, second))):
+        for index in range(3):
+            columns = slice(WIDTH * index, WIDTH * index + WIDTH)
+            start[SLAB * index : SLAB * index + SLAB, :] = narrow(w_qkv[block, :, columns])
+        start[3 * SLAB : 4 * SLAB, :] = narrow(w_out[block])
+        first = 4 * SLAB * block
+        for index in range(4):
+            columns = slice(WIDTH * index, WIDTH * index + WIDTH)
+            row = first + SLAB * index
+            rest[row : row + SLAB, :] = narrow(w_up[block, :, columns])
+        rest[first + 4 * SLAB : first + 8 * SLAB, :] = narrow(w_down[block])
+    early[4 * SLAB :, :] = narrow(norm[...])
+
+
+def pack_all(w_qkv, w_out, w_up, w_down, norm_rows):
+    return pl.pallas_call(
+        pack_kernel,
+        out_shape=[
+            jax.ShapeDtypeStruct((rows, WIDTH), jnp.bfloat16)
+            for rows in (5 * SLAB, 8 * SLAB, 12 * SLAB)
+        ],
+        compiler_params=pltpu.CompilerParams(vmem_limit_bytes=VMEM_BYTES),
+        cost_estimate=COST,
+        name="pack",
+    )(w_qkv, w_out, w_up, w_down, norm_rows)
 
 
 def adam_parts(gradient, first_moment, second_moment):
@@ -896,18 +914,18 @@
     fsdp = lax.axis_index("fsdp")
     place = jnp.stack([lax.axis_index("dp"), fsdp // 2, fsdp % 2]).astype(jnp.int32)
     norm_rows = jnp.pad(
-        norm_params.astype(jnp.bfloat16).reshape(1, -1), ((0, rows - 1), (0, WIDTH - 8 * rows))
-    )
-    shard = pack_weights(w_qkv[0], w_out[0], w_up[0], w_down[0])
-    second_shard = pack_weights(w_qkv[1], w_out[1], w_up[1], w_down[1])
+        norm_params.reshape(1, -1), ((0, rows - 1), (0, WIDTH - 8 * rows))
+    )
     if by_chips:
-        early, late_pieces = gather_by_chips(
-            [jnp.concatenate([shard[: 4 * rows], norm_rows], axis=0), shard[4 * rows :]]
-        )
+        *shard, second_shard = pack_all(w_qkv, w_out, w_up, w_down, norm_rows)
+        early, late_pieces = gather_by_chips(shard)
         early = gather_cores(early, place, "early")
         norm_values = early[:, 4 * rows, : 8 * rows]
     else:
-        gathered = lax.all_gather(jnp.concatenate([shard, norm_rows], axis=0), axes, axis=0)
+        shard = pack_weights(w_qkv[0], w_out[0], w_up[0], w_down[0])
+        second_shard = pack_weights(w_qkv[1], w_out[1], w_up[1], w_down[1])
+        shard = jnp.concatenate([shard, norm_rows.astype(jnp.bfloat16)], axis=0)
+        gathered = lax.all_gather(shard, axes, axis=0)
         norm_values = gathered[:, 12 * rows, : 8 * rows]
         early = to_blocks(gathered, rows)
     gains = norm_values.reshape(shards, 2, 4, rows)
@@ -929,52 +947,34 @@
         second = scatter_cores(pair_second, place)
         upstream = after(upstream, *second)
         second = swap_chips(second)
-    attended_grad, middle_grad, sums_late, pair_first = first_back(
-        core, upstream, slopes, middle, early, late, late_at, gains[0], hidden, hidden_in, attended
+    middle_grad, sums_late, projected_grad, pair_first = first_back(
+        core, upstream, slopes, middle, early, late, late_at, gains[0], hidden, hidden_in, attended,
+        projected, probs, normed,
     )
     if by_chips:
         second[0], *pair_first = lax.optimization_barrier((second[0], *pair_first, *second[1:]))[:3]
         first = scatter_cores(pair_first, place)
+        projected_grad = after(projected_grad, *first)
+        first = swap_chips(first)
         reduced_second = scatter_planes(fold_planes(second, place))
-        attended_grad = after(attended_grad, reduced_second, *first)
-        first = swap_chips(first)
-    projected_grad, pair_last = first_attention_back(core, projected, probs, attended_grad, normed)
-    if by_chips:
-        first[0], *pair_last = lax.optimization_barrier((first[0], *pair_last, *first[1:]))[:3]
-        last = scatter_cores(pair_last, place)
-        first[0] = after(first[0], *last)
-        last = swap_chips(last)
-        first = fold_planes(first, place)
-        projected_grad = after(projected_grad, *first)
     tokens_grad, sums_early = first_input_back(
         projected_grad, tokens, middle_grad, early, gains[0]
     )
     if by_chips:
-        last[0] = after(last[0], tokens_grad)
-        last = fold_planes(last, place)
-        reduced_first = scatter_planes(first, *last)
-        reduced_last = scatter_planes(last)
+        first[0] = after(first[0], tokens_grad)
+        reduced_first = scatter_planes(fold_planes(first, place))
     else:
         reduced_second = scatter_whole(pair_second, rows, 8)
-        reduced_first = scatter_whole(pair_first, rows, 5)
-        reduced_last = scatter_whole(pair_last, rows, 3)
+        reduced_first = scatter_whole(pair_first, rows, 8)
 
     def columns(packed, first, last):
         return jnp.concatenate(
             [packed[rows * index : rows * index + rows] for index in range(first, last)], axis=1
         )
 
-    reduced_first = (
-        columns(reduced_last, 0, 3),
-        columns(reduced_first, 4, 5),
-        columns(reduced_first, 0, 4),
-        reduced_first[5 * rows :],
-    )
-    reduced_second = (
-        columns(reduced_second, 5, 8),
-        columns(reduced_second, 4, 5),
-        columns(reduced_second, 0, 4),
-        reduced_second[8 * rows :],
+    reduced_first, reduced_second = (
+        (columns(both, 5, 8), columns(both, 4, 5), columns(both, 0, 4), both[8 * rows :])
+        for both in (reduced_first, reduced_second)
     )
 
     norm_parts = jnp.concatenate(

time: 303 us -> 297 us (0.980)
  starting transfers between devices: 52.5 us -> 32.8 us
  waiting for transfers between devices: 59.6 us -> 74.8 us
    ppermute x41 -> x34, starting transfers between devices: 52.5 us -> 32.8 us  [swap(): lax.ppermute(array, ('dp', 'fsdp'), [(device, device ^ mask) for device i...]
    ppermute x41 -> x34, waiting for transfers between devices: 59.6 us -> 74.8 us  [swap(): lax.ppermute(array, ('dp', 'fsdp'), [(device, device ^ mask) for device i...]
    convert_element_type x3 -> x2, other arithmetic: 6.6 us -> 6.19 us  [sum_at(): return total.astype(jnp.bfloat16)]
  transfers between devices with their start and end apart: 42 -> 35, of which waited for: 18 -> 17; matrix products, arithmetic and copies ran while one was open for 4% -> 5% of each run, Pallas kernels for 27% -> 27%
where the time goes in v4:
time: 297 us; the launch traced here: 296 us
  Pallas kernels  134 us (45%)
  waiting for transfers between devices  74.8 us (25%)
  starting transfers between devices  32.8 us (11%)
  other arithmetic  21.4 us (7%)
  between operations  15.3 us (5%)
  blocking collectives  11.4 us (4%)
  local copies, waits for them, and re-layouts  6.63 us (2%)
    ppermute x34, waiting for transfers between devices, swap(): lax.ppermute(array, ('dp', 'fsdp'), [(device, device ^ mask) for device i...  74.8 us
    pallas_call x1, Pallas kernels, second_block(): pl.pallas_call(second_kernel, grid=(TILES + 12,), in_specs=[pl.BlockSpec(...  51.5 us
    pallas_call x1, Pallas kernels, first_back(): pl.pallas_call(first_back_kernel, grid=(last_at + 3,), in_specs=[pl.Block...  35.7 us
    ppermute x34, starting transfers between devices, swap(): lax.ppermute(array, ('dp', 'fsdp'), [(device, device ^ mask) for device i...  32.8 us
    pallas_call x1, Pallas kernels, first_attention(): pl.pallas_call(first_attention_kernel, grid=(2 * TILES + 1,), in_specs=[p...  15.9 us
    pallas_call x1, Pallas kernels, first_mlp(): pl.pallas_call(first_mlp_kernel, grid=(TILES,), in_specs=[tile(WIDTH), ti...  14 us
    all_to_all x1, blocking collectives, body(): arrived = jnp.sum(lax.all_to_all(message, axes, 0, 0, tiled=True), axis=0)  11.4 us
    pallas_call x2, Pallas kernels, arrange(): pl.pallas_call(arrange_kernel, in_specs=[pl.BlockSpec(memory_space=pltpu....  7.76 us
  transfers between devices with their start and end apart: 35, of which 17 were waited for; matrix products, arithmetic and copies ran while one was open for 5% of the time, Pallas kernels for 27%

profile of v4, /device:TPU:0, one launch (start us, length us, event | category | flops | bytes accessed | tf_op | source)
XLA Modules:
  0.0 296.1 jit_solution(578713334241364570)
XLA Ops:
  10.6 5.1 %collective-permute-start.2 = (bf16[80,512]{1,0:T(8,128)(2,1)}, bf16[80,512]{1,0:T(8,128)(2,1)S(1)}, u32[]{:S(2)}, u32[]{:S(2)}) collective-permute-start(bf16[80,512]{1,0:T(8,128)(2,1)} %get-tuple-element.58), channel_id=1, source_target_pairs={{0,6},{1,7},{2,4},{3,5},{4,2},{5,3},{6,0},{7,1},{8,14},{9,15},{10,... | collective-permute-start | bytes 245768 | tf_op jit(solution)/shard_map/ppermute | solution.py:831
  16.3 2.6 collective-permute-done.2
  18.9 3.8 %collective-permute-done.1 = bf16[80,512]{1,0:T(8,128)(2,1)S(1)} collective-permute-done((bf16[80,512]{1,0:T(8,128)(2,1)}, bf16[80,512]{1,0:T(8,128)(2,1)S(1)}, u32[]{:S(2)}, u32[]{:S(2)}) %collective-permute-start.1) | collective-permute-done | bytes 81952 | tf_op jit(solution)/shard_map/ppermute | solution.py:831
  23.7 2.5 collective-permute-start.5
  27.3 2.7 collective-permute-start.12
  30.0 5.3 %collective-permute-done.12 = bf16[128,512]{1,0:T(8,128)(2,1)S(1)} collective-permute-done((bf16[128,512]{1,0:T(8,128)(2,1)}, bf16[128,512]{1,0:T(8,128)(2,1)S(1)}, u32[]{:S(2)}, u32[]{:S(2)}) %collective-permute-start.12) | collective-permute-done | bytes 131104 | tf_op jit(solution)/shard_map/ppermute | solution.py:831
  35.8 7.3 %collective-permute-done.11 = bf16[128,512]{1,0:T(8,128)(2,1)S(1)} collective-permute-done((bf16[128,512]{1,0:T(8,128)(2,1)}, bf16[128,512]{1,0:T(8,128)(2,1)S(1)}, u32[]{:S(2)}, u32[]{:S(2)}) %collective-permute-start.11) | collective-permute-done | bytes 131104 | tf_op jit(solution)/shard_map/ppermute | solution.py:831
  43.7 4.6 %collective-permute-done.10 = bf16[128,512]{1,0:T(8,128)(2,1)S(1)} collective-permute-done((bf16[128,512]{1,0:T(8,128)(2,1)}, bf16[128,512]{1,0:T(8,128)(2,1)S(1)}, u32[]{:S(2)}, u32[]{:S(2)}) %collective-permute-start.10) | collective-permute-done | bytes 131104 | tf_op jit(solution)/shard_map/ppermute | solution.py:831
  53.4 3.3 %arrange_early.1.weights = bf16[32,80,512]{2,1,0:T(8,128)(2,1)} custom-call(s32[3]{0:T(128)} %pad_add_fusion.place, bf16[4,80,512]{2,1,0:T(8,128)(2,1)} %copy-done.6, bf16[4,80,512]{2,1,0:T(8,128)(2,1)} %copy-done.24, bf16[4,80,512]{2,1,0:T(8,128)(2,1)} %copy-done.23, bf16[4,80,512]{2,1,0:T(8,128)(2,1)} %copy-done.22, ...), custom_call_target="tpu_custom_call" | custom-call | flops 100000000 | bytes 100000 | tf_op jit(solution)/shard_map/arrange_early/pallas_call | solution.py:741
  58.5 15.9 %first_attention.1 = (bf16[1088,512]{1,0:T(8,128)(2,1)}, bf16[1088,1536]{1,0:T(8,128)(2,1)}, bf16[9,4,256,128]{3,2,1,0:T(8,128)(2,1)}, bf16[1088,512]{1,0:T(8,12...) custom-call(bf16[1088,512]{1,0:T(8,128)(2,1)} %tokens.3, bf16[32,80,512]{2,1,0:T(8,128)(2,1)} %arrange_early.1.weights, ...), custom_call_target="tpu_custom_call" | custom-call | flops 100000000 | bytes 100000 | tf_op jit(solution)/shard_map/first_attention/pallas_call | solution.py:208
  75.5 6.6 %collective-permute-done.13.refs_1_ = bf16[4,128,512]{2,1,0:T(8,128)(2,1)S(1)} collective-permute-done((bf16[4,128,512]{2,1,0:T(8,128)(2,1)S(1)}, bf16[4,128,512]{2,1,0:T(8,128)(2,1)S(1)}, u32[]{:S(2)}, u32[]{:S(2)}) %collective-permute-start.13) | collective-permute-done | bytes 524320 | tf_op jit(solution)/shard_map/ppermute | solution.py:831
  85.8 4.4 %arrange_late.1.weights_up.weights_down = bf16[32,128,512]{2,1,0:T(8,128)(2,1)} custom-call(s32[3]{0:T(128)} %pad_add_fusion.place, bf16[4,128,512]{2,1,0:T(8,128)(2,1)} %copy-done.4, bf16[4,128,512]{2,1,0:T(8,128)(2,1)} %copy-done.19, bf16[4,128,512]{2,1,0:T(8,128)(2,1)} %copy-done.18, bf16[4,128,512]{2,1,0:T(8,128)(2,1)} %copy-done.17, ...), custom_call_target="tpu_custom_call" | custom-call | flops 100000000 | bytes 100000 | tf_op jit(solution)/shard_map/arrange_late/pallas_call | solution.py:741
  90.2 14.0 %first_mlp.1 = (bf16[1088,2048]{1,0:T(8,128)(2,1)}, bf16[1088,2048]{1,0:T(8,128)(2,1)}, f32[1088,512]{1,0:T(8,128)}) custom-call(f32[1088,512]{1,0:T(8,128)} %get-tuple-element.59.middle, bf16[1088,512]{1,0:T(8,128)(2,1)} %get-tuple-element.60.hidden_in, bf16[32,128,512]{2,1,0:T(8,128)(2,1)} %arrange_late.1.weights_up.weights_down, ...), custom_call_target="tpu_custom_call" | custom-call | flops 100000000 | bytes 100000 | tf_op jit(solution)/shard_map/first_mlp/pallas_call | solution.py:262
  104.2 51.5 %second_block.1 = (bf16[17,64,512]{2,1,0:T(8,128)(2,1)}, f32[17,64,512]{2,1,0:T(8,128)}, f32[4,8,512]{2,1,0:T(8,128)}, bf16[16,192,512]{2,1,0:T(8,128)(2,1)}, bf16[16,192,512]{2,1,0:T(8,128)(2,1)}) custom-call(s32[1]{0:T(128)S(6)} %copy.71.frame_count, s32[1]{0:T(128)} %bitcast.core, f32[17,64,512]{2,1,0:T(8,128)} %bitcast.95, ...), custom_call_target="tpu_custom_call" | custom-call | flops 100000000 | bytes 100000 | tf_op jit(solution)/shard_map/second_block/pallas_call | solution.py:464
  155.8 5.8 %collective-permute-done.20 = bf16[16,192,512]{2,1,0:T(8,128)(2,1)S(1)} collective-permute-done((bf16[16,192,512]{2,1,0:T(8,128)(2,1)}, bf16[16,192,512]{2,1,0:T(8,128)(2,1)S(1)}, u32[]{:S(2)}, u32[]{:S(2)}) %collective-permute-start.20) | collective-permute-done | bytes 3145760 | tf_op jit(solution)/shard_map/ppermute | solution.py:831
  161.6 3.7 %fusion.3 = (bf16[4,192,512]{2,1,0:T(8,128)(2,1)S(1)}, bf16[4,192,512]{2,1,0:T(8,128)(2,1)S(1)}, bf16[4,192,512]{2,1,0:T(8,128)(2,1)S(1)}, bf16[4,192,512]{2,1,0:T(8,128)(2,1)}) fusion(bf16[4,4,192,512]{3,2,1,0:T(8,128)(2,1)S(1)} %bitcast.93, s32[]{:T(128)S(6)} %select_n.82, bf16[4,4,192,512]{3,2,1,0:T(8,128)(2,1)} %bitcast.92, s32[]{:T(128)S(6)} %select_n.81, ...), kind=kLoop, calls=%fused_computation.11 | loop fusion | flops 6291456 | bytes 9437200 | tf_op jit(solution)/shard_map/convert_element_type | solution.py:859
  168.8 35.7 %first_back.1 = (f32[1088,512]{1,0:T(8,128)}, f32[2,8,512]{2,1,0:T(8,128)}, bf16[1088,1536]{1,0:T(8,128)(2,1)}, bf16[16,192,512]{2,1,0:T(8,128)(2,1)}, bf16[16,192,512]{2,1,0:T(8,128)(2,1)}) custom-call(s32[1]{0:T(128)} %bitcast.core, f32[1088,512]{1,0:T(8,128)} %bitcast.94, bf16[1088,2048]{1,0:T(8,128)(2,1)} %get-tuple-element.75.slopes, ...), custom_call_target="tpu_custom_call" | custom-call | flops 100000000 | bytes 100000 | tf_op jit(solution)/shard_map/first_back/pallas_call | solution.py:633
  206.0 3.2 %fusion.15 = (bf16[192,512]{1,0:T(8,128)(2,1)S(1)}, bf16[192,512]{1,0:T(8,128)(2,1)S(1)}, bf16[192,512]{1,0:T(8,128)(2,1)}, bf16[192,512]{1,0:T(8,128)(2,1)S(1)}) fusion(bf16[4,192,512]{2,1,0:T(8,128)(2,1)} %copy-done.11, s32[]{:T(128)S(6)} %select_n.83, bf16[4,192,512]{2,1,0:T(8,128)(2,1)} %copy-done.12, bf16[4,192,512]{2,1,0:T(8,128)(2,1)} %copy-done.13, ...), kind=kLoop, calls=%fused_computation.51 | loop fusion | flops 3145728 | bytes 3932176 | tf_op jit(solution)/shard_map/add | solution.py:855
  222.7 11.2 %collective-permute-done.32 = bf16[192,512]{1,0:T(8,128)(2,1)S(1)} collective-permute-done((bf16[192,512]{1,0:T(8,128)(2,1)}, bf16[192,512]{1,0:T(8,128)(2,1)S(1)}, u32[]{:S(2)}, u32[]{:S(2)}) %collective-permute-start.32) | collective-permute-done | bytes 196640 | tf_op jit(solution)/shard_map/ppermute | solution.py:831
  235.0 7.0 %first_input_back.1 = (f32[1088,512]{1,0:T(8,128)}, f32[2,8,512]{2,1,0:T(8,128)}) custom-call(bf16[1088,1536]{1,0:T(8,128)(2,1)} %get-tuple-element.86.projected_grad, bf16[1088,512]{1,0:T(8,128)(2,1)} %tokens.3, f32[1088,512]{1,0:T(8,128)} %get-tuple-element.87.middle_grad, bf16[32,80,512]{2,1,0:T(8,128)(2,1)} %arrange_early.1.weights, f32[4,512]{1,0:T(4,128)} %squeeze.66.gains), custom_call_target="tpu_custom_call" | custom-call | flops 100000000 | bytes 100000 | tf_op jit(solution)/shard_map/first_input_back/pallas_call | solution.py:709
  242.0 10.1 %collective-permute-done.25 = bf16[4,192,512]{2,1,0:T(8,128)(2,1)S(1)} collective-permute-done((bf16[4,192,512]{2,1,0:T(8,128)(2,1)}, bf16[4,192,512]{2,1,0:T(8,128)(2,1)S(1)}, u32[]{:S(2)}, u32[]{:S(2)}) %collective-permute-start.25) | collective-permute-done | bytes 786464 | tf_op jit(solution)/shard_map/ppermute | solution.py:831
  257.4 4.0 %collective-permute-done.30 = bf16[192,512]{1,0:T(8,128)(2,1)S(1)} collective-permute-done((bf16[192,512]{1,0:T(8,128)(2,1)S(1)}, bf16[192,512]{1,0:T(8,128)(2,1)S(1)}, u32[]{:S(2)}, u32[]{:S(2)}) %collective-permute-start.30) | collective-permute-done | bytes 196640 | tf_op jit(solution)/shard_map/ppermute | solution.py:831
  261.5 8.7 %collective-permute-done.29 = bf16[192,512]{1,0:T(8,128)(2,1)S(1)} collective-permute-done((bf16[192,512]{1,0:T(8,128)(2,1)S(1)}, bf16[192,512]{1,0:T(8,128)(2,1)S(1)}, u32[]{:S(2)}, u32[]{:S(2)}) %collective-permute-start.29) | collective-permute-done | bytes 196640 | tf_op jit(solution)/shard_map/ppermute | solution.py:831
  272.7 11.4 %all_to_all.9 = f32[32,1,144]{2,1,0:T(1,128)S(1)} all-to-all(f32[32,1,144]{2,1,0:T(1,128)S(1)} %all_to_all.6), channel_id=1, replica_groups=mesh['dp'=4,'fsdp'=8] {'dp','fsdp'}, dimensions={0} | all-to-all | bytes 36864 | tf_op jit(solution)/shard_map/all_to_all | solution.py:999
  (193 shorter events, 50.2 us)
Async XLA Ops:
  7.2 97.0 %all-gather.3.cloned.1.call-start = ((), (), s32[]{:S(2)}) async-start(), calls=%async_computation.1 | async-start | bytes 6488064 | tf_op jit(solution)/shard_map/all_gather | solution.py:933
  23.7 11.7 %collective-permute-start.5 = (bf16[4,80,512]{2,1,0:T(8,128)(2,1)S(1)}, bf16[4,80,512]{2,1,0:T(8,128)(2,1)S(1)}, u32[]{:S(2)}, u32[]{:S(2)}) collective-permute-start(bf16[4,80,512]{2,1,0:T(8,128)(2,1)S(1)} %pad_maximum_fusion.1.refs_0_), channel_id=1, source_target_pairs={{0,24},{1,25},{2,26},{3,27},{4,28},{5,29},{6,30},{7,31},{8,16},{9,... | collective-permute-start | bytes 983048 | tf_op jit(solution)/shard_map/ppermute | solution.py:831
  26.2 16.8 %collective-permute-start.4 = (bf16[4,80,512]{2,1,0:T(8,128)(2,1)S(1)}, bf16[4,80,512]{2,1,0:T(8,128)(2,1)S(1)}, u32[]{:S(2)}, u32[]{:S(2)}) collective-permute-start(bf16[4,80,512]{2,1,0:T(8,128)(2,1)S(1)} %pad_maximum_fusion.1.refs_0_), channel_id=1, source_target_pairs={{0,16},{1,17},{2,18},{3,19},{4,20},{5,21},{6,22},{7,23},{8,24},{9,... | collective-permute-start | bytes 983048 | tf_op jit(solution)/shard_map/ppermute | solution.py:831
  26.7 16.4 %collective-permute-start.3 = (bf16[4,80,512]{2,1,0:T(8,128)(2,1)S(1)}, bf16[4,80,512]{2,1,0:T(8,128)(2,1)S(1)}, u32[]{:S(2)}, u32[]{:S(2)}) collective-permute-start(bf16[4,80,512]{2,1,0:T(8,128)(2,1)S(1)} %pad_maximum_fusion.1.refs_0_), channel_id=1, source_target_pairs={{0,8},{1,9},{2,10},{3,11},{4,12},{5,13},{6,14},{7,15},{8,0},{9,1},... | collective-permute-start | bytes 983048 | tf_op jit(solution)/shard_map/ppermute | solution.py:831
  30.0 13.1 %collective-permute-start.11 = (bf16[128,512]{1,0:T(8,128)(2,1)}, bf16[128,512]{1,0:T(8,128)(2,1)S(1)}, u32[]{:S(2)}, u32[]{:S(2)}) collective-permute-start(bf16[128,512]{1,0:T(8,128)(2,1)} %get-tuple-element.62), channel_id=1, source_target_pairs={{0,4},{1,5},{2,6},{3,7},{4,0},{5,1},{6,2},{7,3},{8,12},{9,13},{10,... | collective-permute-start | bytes 393224 | tf_op jit(solution)/shard_map/ppermute | solution.py:831
  35.3 16.3 %collective-permute-start.6 = (bf16[4,80,512]{2,1,0:T(8,128)(2,1)S(1)}, bf16[4,80,512]{2,1,0:T(8,128)(2,1)}, u32[]{:S(2)}, u32[]{:S(2)}) collective-permute-start(bf16[4,80,512]{2,1,0:T(8,128)(2,1)S(1)} %pad_maximum_fusion.1.refs_0_), channel_id=1, source_target_pairs={{0,1},{1,0},{2,3},{3,2},{4,5},{5,4},{6,7},{7,6},{8,9},{9,8},{10,11... | collective-permute-start | bytes 983048 | tf_op jit(solution)/shard_map/ppermute | solution.py:831
  35.4 16.8 %collective-permute-start.9 = (bf16[4,80,512]{2,1,0:T(8,128)(2,1)S(1)}, bf16[4,80,512]{2,1,0:T(8,128)(2,1)}, u32[]{:S(2)}, u32[]{:S(2)}) collective-permute-start(bf16[4,80,512]{2,1,0:T(8,128)(2,1)S(1)} %collective-permute-done.5.refs_3_), channel_id=1, source_target_pairs={{0,1},{1,0},{2,3},{3,2},{4,5},{5,4},{6,7},{7,6},{8,9},{9,8},{10,11... | collective-permute-start | bytes 983048 | tf_op jit(solution)/shard_map/ppermute | solution.py:831
  43.1 10.3 %collective-permute-start.8 = (bf16[4,80,512]{2,1,0:T(8,128)(2,1)S(1)}, bf16[4,80,512]{2,1,0:T(8,128)(2,1)}, u32[]{:S(2)}, u32[]{:S(2)}) collective-permute-start(bf16[4,80,512]{2,1,0:T(8,128)(2,1)S(1)} %collective-permute-done.4.refs_2_), channel_id=1, source_target_pairs={{0,1},{1,0},{2,3},{3,2},{4,5},{5,4},{6,7},{7,6},{8,9},{9,8},{10,11... | collective-permute-start | bytes 983048 | tf_op jit(solution)/shard_map/ppermute | solution.py:831
  43.2 10.2 %collective-permute-start.7 = (bf16[4,80,512]{2,1,0:T(8,128)(2,1)S(1)}, bf16[4,80,512]{2,1,0:T(8,128)(2,1)}, u32[]{:S(2)}, u32[]{:S(2)}) collective-permute-start(bf16[4,80,512]{2,1,0:T(8,128)(2,1)S(1)} %collective-permute-done.3.refs_1_), channel_id=1, source_target_pairs={{0,1},{1,0},{2,3},{3,2},{4,5},{5,4},{6,7},{7,6},{8,9},{9,8},{10,11... | collective-permute-start | bytes 983048 | tf_op jit(solution)/shard_map/ppermute | solution.py:831
  49.2 25.3 %collective-permute-start.15 = (bf16[4,128,512]{2,1,0:T(8,128)(2,1)S(1)}, bf16[4,128,512]{2,1,0:T(8,128)(2,1)S(1)}, u32[]{:S(2)}, u32[]{:S(2)}) collective-permute-start(bf16[4,128,512]{2,1,0:T(8,128)(2,1)S(1)} %pad_maximum_fusion.refs_0_), channel_id=1, source_target_pairs={{0,24},{1,25},{2,26},{3,27},{4,28},{5,29},{6,30},{7,31},{8,16},{9,... | collective-permute-start | bytes 1572872 | tf_op jit(solution)/shard_map/ppermute | solution.py:831
  51.5 24.0 %collective-permute-start.14 = (bf16[4,128,512]{2,1,0:T(8,128)(2,1)S(1)}, bf16[4,128,512]{2,1,0:T(8,128)(2,1)S(1)}, u32[]{:S(2)}, u32[]{:S(2)}) collective-permute-start(bf16[4,128,512]{2,1,0:T(8,128)(2,1)S(1)} %pad_maximum_fusion.refs_0_), channel_id=1, source_target_pairs={{0,16},{1,17},{2,18},{3,19},{4,20},{5,21},{6,22},{7,23},{8,24},{9,... | collective-permute-start | bytes 1572872 | tf_op jit(solution)/shard_map/ppermute | solution.py:831
  52.3 29.8 %collective-permute-start.13 = (bf16[4,128,512]{2,1,0:T(8,128)(2,1)S(1)}, bf16[4,128,512]{2,1,0:T(8,128)(2,1)S(1)}, u32[]{:S(2)}, u32[]{:S(2)}) collective-permute-start(bf16[4,128,512]{2,1,0:T(8,128)(2,1)S(1)} %pad_maximum_fusion.refs_0_), channel_id=1, source_target_pairs={{0,8},{1,9},{2,10},{3,11},{4,12},{5,13},{6,14},{7,15},{8,0},{9,1},... | collective-permute-start | bytes 1572872 | tf_op jit(solution)/shard_map/ppermute | solution.py:831
  74.4 9.7 %collective-permute-start.16 = (bf16[4,128,512]{2,1,0:T(8,128)(2,1)S(1)}, bf16[4,128,512]{2,1,0:T(8,128)(2,1)S(1)}, u32[]{:S(2)}, u32[]{:S(2)}) collective-permute-start(bf16[4,128,512]{2,1,0:T(8,128)(2,1)S(1)} %pad_maximum_fusion.refs_0_), channel_id=1, source_target_pairs={{0,1},{1,0},{2,3},{3,2},{4,5},{5,4},{6,7},{7,6},{8,9},{9,8},{10,11... | collective-permute-start | bytes 1572872 | tf_op jit(solution)/shard_map/ppermute | solution.py:831
  165.4 39.2 %collective-permute-start.23 = (bf16[4,192,512]{2,1,0:T(8,128)(2,1)S(1)}, bf16[4,192,512]{2,1,0:T(8,128)(2,1)S(1)}, u32[]{:S(2)}, u32[]{:S(2)}) collective-permute-start(bf16[4,192,512]{2,1,0:T(8,128)(2,1)S(1)} %get-tuple-element.217), channel_id=1, source_target_pairs={{0,16},{1,17},{2,18},{3,19},{4,20},{5,21},{6,22},{7,23},{8,24},{9,... | collective-permute-start | bytes 2359304 | tf_op jit(solution)/shard_map/ppermute | solution.py:831
  166.1 38.5 %collective-permute-start.22 = (bf16[4,192,512]{2,1,0:T(8,128)(2,1)S(1)}, bf16[4,192,512]{2,1,0:T(8,128)(2,1)S(1)}, u32[]{:S(2)}, u32[]{:S(2)}) collective-permute-start(bf16[4,192,512]{2,1,0:T(8,128)(2,1)S(1)} %get-tuple-element.218), channel_id=1, source_target_pairs={{0,8},{1,9},{2,10},{3,11},{4,12},{5,13},{6,14},{7,15},{8,0},{9,1},... | collective-permute-start | bytes 2359304 | tf_op jit(solution)/shard_map/ppermute | solution.py:831
  167.3 37.3 %collective-permute-start.21 = (bf16[4,192,512]{2,1,0:T(8,128)(2,1)S(1)}, bf16[4,192,512]{2,1,0:T(8,128)(2,1)S(1)}, u32[]{:S(2)}, u32[]{:S(2)}) collective-permute-start(bf16[4,192,512]{2,1,0:T(8,128)(2,1)S(1)} %get-tuple-element.219), channel_id=1, source_target_pairs={{0,24},{1,25},{2,26},{3,27},{4,28},{5,29},{6,30},{7,31},{8,16},{9,... | collective-permute-start | bytes 2359304 | tf_op jit(solution)/shard_map/ppermute | solution.py:831
  209.2 9.7 %collective-permute-start.33 = (bf16[192,512]{1,0:T(8,128)(2,1)S(1)}, bf16[192,512]{1,0:T(8,128)(2,1)S(1)}, u32[]{:S(2)}, u32[]{:S(2)}) collective-permute-start(bf16[192,512]{1,0:T(8,128)(2,1)S(1)} %get-tuple-element.226), channel_id=1, source_target_pairs={{0,2},{1,3},{2,0},{3,1},{4,6},{5,7},{6,4},{7,5},{8,10},{9,11},{10,... | collective-permute-start | bytes 589832 | tf_op jit(solution)/shard_map/ppermute | solution.py:831
  214.3 27.7 %collective-permute-start.27 = (bf16[4,192,512]{2,1,0:T(8,128)(2,1)}, bf16[4,192,512]{2,1,0:T(8,128)(2,1)S(1)}, u32[]{:S(2)}, u32[]{:S(2)}) collective-permute-start(bf16[4,192,512]{2,1,0:T(8,128)(2,1)} %get-tuple-element.213), channel_id=1, source_target_pairs={{0,16},{1,17},{2,18},{3,19},{4,20},{5,21},{6,22},{7,23},{8,24},{9,... | collective-permute-start | bytes 2359304 | tf_op jit(solution)/shard_map/ppermute | solution.py:831
  215.1 27.0 %collective-permute-start.26 = (bf16[4,192,512]{2,1,0:T(8,128)(2,1)}, bf16[4,192,512]{2,1,0:T(8,128)(2,1)S(1)}, u32[]{:S(2)}, u32[]{:S(2)}) collective-permute-start(bf16[4,192,512]{2,1,0:T(8,128)(2,1)} %get-tuple-element.214), channel_id=1, source_target_pairs={{0,8},{1,9},{2,10},{3,11},{4,12},{5,13},{6,14},{7,15},{8,0},{9,1},... | collective-permute-start | bytes 2359304 | tf_op jit(solution)/shard_map/ppermute | solution.py:831
  216.3 35.9 %collective-permute-start.25 = (bf16[4,192,512]{2,1,0:T(8,128)(2,1)}, bf16[4,192,512]{2,1,0:T(8,128)(2,1)S(1)}, u32[]{:S(2)}, u32[]{:S(2)}) collective-permute-start(bf16[4,192,512]{2,1,0:T(8,128)(2,1)} %get-tuple-element.215), channel_id=1, source_target_pairs={{0,24},{1,25},{2,26},{3,27},{4,28},{5,29},{6,30},{7,31},{8,16},{9,... | collective-permute-start | bytes 2359304 | tf_op jit(solution)/shard_map/ppermute | solution.py:831
  217.8 16.1 %collective-permute-start.32 = (bf16[192,512]{1,0:T(8,128)(2,1)}, bf16[192,512]{1,0:T(8,128)(2,1)S(1)}, u32[]{:S(2)}, u32[]{:S(2)}) collective-permute-start(bf16[192,512]{1,0:T(8,128)(2,1)} %get-tuple-element.227), channel_id=1, source_target_pairs={{0,4},{1,5},{2,6},{3,7},{4,0},{5,1},{6,2},{7,3},{8,12},{9,13},{10,... | collective-permute-start | bytes 589832 | tf_op jit(solution)/shard_map/ppermute | solution.py:831
  218.8 15.1 %collective-permute-start.31 = (bf16[192,512]{1,0:T(8,128)(2,1)S(1)}, bf16[192,512]{1,0:T(8,128)(2,1)S(1)}, u32[]{:S(2)}, u32[]{:S(2)}) collective-permute-start(bf16[192,512]{1,0:T(8,128)(2,1)S(1)} %get-tuple-element.228), channel_id=1, source_target_pairs={{0,6},{1,7},{2,4},{3,5},{4,2},{5,3},{6,0},{7,1},{8,14},{9,15},{10,... | collective-permute-start | bytes 589832 | tf_op jit(solution)/shard_map/ppermute | solution.py:831
  253.6 16.6 %collective-permute-start.29 = (bf16[192,512]{1,0:T(8,128)(2,1)S(1)}, bf16[192,512]{1,0:T(8,128)(2,1)S(1)}, u32[]{:S(2)}, u32[]{:S(2)}) collective-permute-start(bf16[192,512]{1,0:T(8,128)(2,1)S(1)} %get-tuple-element.223), channel_id=1, source_target_pairs={{0,4},{1,5},{2,6},{3,7},{4,0},{5,1},{6,2},{7,3},{8,12},{9,13},{10,... | collective-permute-start | bytes 589832 | tf_op jit(solution)/shard_map/ppermute | solution.py:831
  254.6 15.5 %collective-permute-start.28 = (bf16[192,512]{1,0:T(8,128)(2,1)S(1)}, bf16[192,512]{1,0:T(8,128)(2,1)S(1)}, u32[]{:S(2)}, u32[]{:S(2)}) collective-permute-start(bf16[192,512]{1,0:T(8,128)(2,1)S(1)} %get-tuple-element.224), channel_id=1, source_target_pairs={{0,6},{1,7},{2,4},{3,5},{4,2},{5,3},{6,0},{7,1},{8,14},{9,15},{10,... | collective-permute-start | bytes 589832 | tf_op jit(solution)/shard_map/ppermute | solution.py:831
  (51 other events, 500.5 us)
Sparse Core Ops, SparseCore 0:
  11.6 88.0 all-gather.2

commit v5 on v4

--- a/solution.py
+++ b/solution.py
@@ -238,7 +238,21 @@
     )(tokens, weights, gains)
 
 
-def first_mlp_kernel(middle, hidden_in, weights_up, weights_down, hidden_out, slope_out, result_out):
+def first_mlp_kernel(place, middle, hidden_in, *refs):
+    pieces = refs[:-6]
+    hidden_out, slope_out, result_out, weights_out, weights, store_sem = refs[-6:]
+    store = pltpu.make_async_copy(weights, weights_out, store_sem)
+
+    @pl.when(pl.program_id(0) == 0)
+    def _():
+        if len(pieces) == 1:
+            weights[...] = pieces[0][...]
+        else:
+            place_pieces(place, pieces, weights)
+        store.start()
+
+    weights_up = weights.at[:, : 4 * SLAB]
+    weights_down = weights.at[:, 4 * SLAB :]
     result = middle[...]
     upward = dot_nn(hidden_in[...], slab(weights_up, 0))
     for index in range(4):
@@ -252,8 +266,12 @@
         upward = following
     result_out[...] = result
 
-
-def first_mlp(middle, hidden_in, weights, weights_at):
+    @pl.when(pl.program_id(0) == TILES - 1)
+    def _():
+        store.wait()
+
+
+def first_mlp(place, middle, hidden_in, pieces):
     count = middle.shape[0]
 
     def tile(width):
@@ -263,33 +281,66 @@
         first_mlp_kernel,
         grid=(TILES,),
         in_specs=[
+            pl.BlockSpec(memory_space=pltpu.SMEM),
             tile(WIDTH),
             tile(WIDTH),
-            weight_spec(weights, weights_at),
-            weight_spec(weights, weights_at + 1),
-        ],
-        out_specs=[tile(4 * WIDTH), tile(4 * WIDTH), tile(WIDTH)],
+        ]
+        + [
+            pl.BlockSpec(piece.shape, lambda i: (0, 0, 0), pipeline_mode=pl.Buffered(1))
+            for piece in pieces
+        ],
+        out_specs=[tile(4 * WIDTH), tile(4 * WIDTH), tile(WIDTH), pl.BlockSpec(memory_space=pl.ANY)],
         out_shape=[
             jax.ShapeDtypeStruct((count, 4 * WIDTH), jnp.bfloat16),
             jax.ShapeDtypeStruct((count, 4 * WIDTH), jnp.bfloat16),
             jax.ShapeDtypeStruct((count, WIDTH), jnp.float32),
+            jax.ShapeDtypeStruct((BLOCKS, 8 * SLAB, WIDTH), jnp.bfloat16),
+        ],
+        scratch_shapes=[
+            pltpu.VMEM((BLOCKS, 8 * SLAB, WIDTH), jnp.bfloat16),
+            pltpu.SemaphoreType.DMA,
         ],
         compiler_params=pltpu.CompilerParams(vmem_limit_bytes=VMEM_BYTES),
         cost_estimate=COST,
         name="first_mlp",
-    )(middle, hidden_in, weights, weights)
+    )(place, middle, hidden_in, *pieces)
 
 
 def second_kernel(
-    frame_count, core, inputs, cotangent, weights, weights_up, weights_down, gains, result_out,
-    grad_out, sums, mine, other,
+    frame_count, core, inputs, cotangent, weights, late_weights, gains, result_out, grad_out, sums,
+    mine_out, other_out,
     caps, query_rows, key_rows, value_rows, probs, slopes, normed, projected_grads, attended,
     branch_grads, hidden_in, up_grads, hidden, out_grads,
+    weights_up, weights_down, mine, other, load_sems, store_sems,
 ):
     step = pl.program_id(0)
 
+    def loads():
+        return [
+            pltpu.make_async_copy(
+                late_weights.at[:, 4 * SLAB * index : 4 * SLAB * index + 4 * SLAB, :],
+                ref,
+                load_sems.at[index - 1],
+            )
+            for index, ref in ((1, weights_up), (2, weights_down))
+        ]
+
+    def stores(unit, place):
+        return [
+            pltpu.make_async_copy(ref.at[place], out.at[place], store_sems.at[index, unit])
+            for index, (ref, out) in enumerate(((mine, mine_out), (other, other_out)))
+        ]
+
+    def slab_place(row):
+        return slice(None), pl.ds(row, SLAB)
+
+    def down_place(block):
+        return pl.ds(block, 4), pl.ds(8 * SLAB, 4 * SLAB)
+
     @pl.when(step == 0)
     def _():
+        for copy in loads():
+            copy.start()
         row = lax.broadcasted_iota(jnp.int32, caps.shape, 0)
         column = lax.broadcasted_iota(jnp.int32, caps.shape, 1) % HALF
         soon, late = row // 8, column // 8
@@ -353,6 +404,12 @@
         normal_second, scale_second = row_norm(middle)
         hidden_in_tile = (normal_second * gains[2:3, :] + gains[3:4, :]).astype(jnp.bfloat16)
         hidden_in[rows, :] = hidden_in_tile
+
+        @pl.when(step == 0)
+        def _():
+            for copy in loads():
+                copy.wait()
+
         result = middle
         upward = dot_nn(hidden_in_tile, slab(weights_up, 0))
         for index in range(4):
@@ -435,22 +492,37 @@
     @pl.when((step >= TILES) & (step < TILES + 4))
     def _():
         right = up_grads[:, part_of(step, TILES)]
-        outer_store(core, hidden_in, right, mine, other, 0, slab_row(step, TILES), SLAB)
+        row = slab_row(step, TILES)
+        outer_store(core, hidden_in, right, mine, other, 0, row, SLAB)
+        for copy in stores(step - TILES, slab_place(row)):
+            copy.start()
 
     @pl.when((step >= TILES + 4) & (step < TILES + 7))
     def _():
         right = projected_grads[:, part_of(step, TILES + 4)]
-        outer_store(core, normed, right, mine, other, 0, slab_row(step, TILES - 1), SLAB)
+        row = slab_row(step, TILES - 1)
+        outer_store(core, normed, right, mine, other, 0, row, SLAB)
+        for copy in stores(step - TILES, slab_place(row)):
+            copy.start()
 
     @pl.when((step >= TILES + 7) & (step < TILES + 11))
     def _():
         left = hidden[:, part_of(step, TILES + 7)]
         block = (step - TILES - 7) * 4
         outer_store(core, left, out_grads[...], mine, other, block, 8 * SLAB, 4 * SLAB)
+        for copy in stores(step - TILES, down_place(block)):
+            copy.start()
 
     @pl.when(step == TILES + 11)
     def _():
         outer_store(core, attended, branch_grads[...], mine, other, 0, 4 * SLAB, SLAB)
+        for copy in stores(11, slab_place(4 * SLAB)):
+            copy.start()
+        places = [slab_place(SLAB * index) for index in (0, 1, 2, 3, 5, 6, 7)]
+        places += [down_place(4 * index) for index in range(4)] + [slab_place(4 * SLAB)]
+        for unit, place in enumerate(places):
+            for copy in stores(unit, place):
+                copy.wait()
 
 
 def second_block(frame_counts, core, inputs, cotangent, weights, gains):
@@ -470,15 +542,15 @@
             tile(WIDTH),
             tile(WIDTH),
             weight_spec(weights, 0),
-            weight_spec(weights, 1),
-            weight_spec(weights, 2),
+            pl.BlockSpec(memory_space=pl.ANY),
             pl.BlockSpec((4, WIDTH), lambda i: (0, 0)),
         ],
         out_specs=[
             tile(WIDTH),
             tile(WIDTH),
             pl.BlockSpec((4, 8, WIDTH), lambda i: (0, 0, 0)),
-            *grad_specs(12 * SLAB),
+            pl.BlockSpec(memory_space=pl.ANY),
+            pl.BlockSpec(memory_space=pl.ANY),
         ],
         out_shape=[
             jax.ShapeDtypeStruct(whole, jnp.bfloat16),
@@ -501,6 +573,12 @@
             held(4),
             held(4),
             held(1),
+            pltpu.VMEM((BLOCKS, 4 * SLAB, WIDTH), jnp.bfloat16),
+            pltpu.VMEM((BLOCKS, 4 * SLAB, WIDTH), jnp.bfloat16),
+            pltpu.VMEM((BLOCKS // 2, 12 * SLAB, WIDTH), jnp.bfloat16),
+            pltpu.VMEM((BLOCKS // 2, 12 * SLAB, WIDTH), jnp.bfloat16),
+            pltpu.SemaphoreType.DMA((2,)),
+            pltpu.SemaphoreType.DMA((2, 12)),
         ],
         compiler_params=pltpu.CompilerParams(vmem_limit_bytes=VMEM_BYTES),
         cost_estimate=COST,
@@ -510,7 +588,6 @@
         core,
         inputs.reshape(whole),
         cotangent.reshape(whole),
-        weights,
         weights,
         weights,
         gains,
@@ -727,13 +804,16 @@
     )(projected_grad, tokens, middle_grad, weights, gains)
 
 
-def arrange_kernel(place, *refs):
-    ins, out = refs[:-1], refs[-1]
+def place_pieces(place, pieces, out):
     across, plane, core = place[0], place[1], place[2]
-    for index, ref in enumerate(ins):
+    for index, piece in enumerate(pieces):
         column = (across ^ (index % 4)) * 8 + (core ^ (index // 4))
         for way in range(4):
-            out[column + (plane ^ way) * 2] = ref[way]
+            out[column + (plane ^ way) * 2] = piece[way]
+
+
+def arrange_kernel(place, *refs):
+    place_pieces(place, refs[:-1], refs[-1])
 
 
 def arrange(place, pieces, name):
@@ -847,8 +927,8 @@
     return results
 
 
-def gather_cores(pieces, place, name):
-    return arrange(place, pieces + [swap(piece, 1) for piece in pieces], "arrange_" + name)
+def gather_cores(pieces):
+    return pieces + [swap(piece, 1) for piece in pieces]
 
 
 def sum_at(arrays, index):
@@ -919,7 +999,7 @@
     if by_chips:
         *shard, second_shard = pack_all(w_qkv, w_out, w_up, w_down, norm_rows)
         early, late_pieces = gather_by_chips(shard)
-        early = gather_cores(early, place, "early")
+        early = arrange(place, gather_cores(early), "arrange_early")
         norm_values = early[:, 4 * rows, : 8 * rows]
     else:
         shard = pack_weights(w_qkv[0], w_out[0], w_up[0], w_down[0])
@@ -934,11 +1014,10 @@
 
     normed, projected, probs, attended, middle, hidden_in = first_attention(tokens, early, gains[0])
     if by_chips:
-        late_pieces = [after(piece, hidden_in) for piece in late_pieces]
-        late, late_at = gather_cores(late_pieces, place, "late"), 0
+        late_pieces = gather_cores([after(piece, hidden_in) for piece in late_pieces])
     else:
-        late, late_at = early, 1
-    hidden, slopes, stream = first_mlp(middle, hidden_in, late, late_at)
+        late_pieces = [early[:, 4 * SLAB : 12 * SLAB]]
+    hidden, slopes, stream, late = first_mlp(place, middle, hidden_in, late_pieces)
     core = place[2:] if by_chips else jnp.zeros((1,), jnp.int32)
     block_out, upstream, sums_second, pair_second = second_block(
         frame_counts, core, stream, cotangent, weights_second, gains[1]
@@ -948,7 +1027,7 @@
         upstream = after(upstream, *second)
         second = swap_chips(second)
     middle_grad, sums_late, projected_grad, pair_first = first_back(
-        core, upstream, slopes, middle, early, late, late_at, gains[0], hidden, hidden_in, attended,
+        core, upstream, slopes, middle, early, late, 0, gains[0], hidden, hidden_in, attended,
         projected, probs, normed,
     )
     if by_chips:

time: 297 us -> 291 us (0.980)
  Pallas kernels: 134 us -> 127 us
    pallas_call x2 -> x1, Pallas kernels: 7.76 us -> 3.32 us  [arrange(): pl.pallas_call(arrange_kernel, in_specs=[pl.BlockSpec(memory_space=pltpu....]
  transfers between devices with their start and end apart: 35 -> 35, of which waited for: 17 -> 17; matrix products, arithmetic and copies ran while one was open for 5% -> 5% of each run, Pallas kernels for 27% -> 26%
where the time goes in v5:
time: 291 us; the launch traced here: 290 us
  Pallas kernels  127 us (44%)
  waiting for transfers between devices  74.7 us (26%)
  starting transfers between devices  32.9 us (11%)
  other arithmetic  21.4 us (7%)
  between operations  15.3 us (5%)
  blocking collectives  11.5 us (4%)
  local copies, waits for them, and re-layouts  6.63 us (2%)
    ppermute x34, waiting for transfers between devices, swap(): lax.ppermute(array, ('dp', 'fsdp'), [(device, device ^ mask) for device i...  74.6 us
    pallas_call x1, Pallas kernels, second_block(): pl.pallas_call(second_kernel, grid=(TILES + 12,), in_specs=[pl.BlockSpec(...  49 us
    pallas_call x1, Pallas kernels, first_back(): pl.pallas_call(first_back_kernel, grid=(last_at + 3,), in_specs=[pl.Block...  35.7 us
    ppermute x34, starting transfers between devices, swap(): lax.ppermute(array, ('dp', 'fsdp'), [(device, device ^ mask) for device i...  32.9 us
    pallas_call x1, Pallas kernels, first_attention(): pl.pallas_call(first_attention_kernel, grid=(2 * TILES + 1,), in_specs=[p...  15.9 us
    pallas_call x1, Pallas kernels, first_mlp(): pl.pallas_call(first_mlp_kernel, grid=(TILES,), in_specs=[pl.BlockSpec(me...  14.4 us
    all_to_all x1, blocking collectives, body(): arrived = jnp.sum(lax.all_to_all(message, axes, 0, 0, tiled=True), axis=0)  11.5 us
    pallas_call x1, Pallas kernels, first_input_back(): pl.pallas_call(first_input_back_kernel, grid=(TILES,), in_specs=[tile(3 *...  6.99 us
  transfers between devices with their start and end apart: 35, of which 17 were waited for; matrix products, arithmetic and copies ran while one was open for 5% of the time, Pallas kernels for 26%

profile of v5, /device:TPU:0, one launch (start us, length us, event | category | flops | bytes accessed | tf_op | source)
XLA Modules:
  0.0 289.7 jit_solution(2538508420876500922)
XLA Ops:
  10.6 5.1 %collective-permute-start.2 = (bf16[80,512]{1,0:T(8,128)(2,1)}, bf16[80,512]{1,0:T(8,128)(2,1)S(1)}, u32[]{:S(2)}, u32[]{:S(2)}) collective-permute-start(bf16[80,512]{1,0:T(8,128)(2,1)} %get-tuple-element.59), channel_id=1, source_target_pairs={{0,6},{1,7},{2,4},{3,5},{4,2},{5,3},{6,0},{7,1},{8,14},{9,15},{10,... | collective-permute-start | bytes 245768 | tf_op jit(solution)/shard_map/ppermute | solution.py:911
  16.3 2.6 collective-permute-done.2
  18.9 3.8 %collective-permute-done.1 = bf16[80,512]{1,0:T(8,128)(2,1)S(1)} collective-permute-done((bf16[80,512]{1,0:T(8,128)(2,1)}, bf16[80,512]{1,0:T(8,128)(2,1)S(1)}, u32[]{:S(2)}, u32[]{:S(2)}) %collective-permute-start.1) | collective-permute-done | bytes 81952 | tf_op jit(solution)/shard_map/ppermute | solution.py:911
  23.7 2.5 collective-permute-start.5
  27.3 2.7 collective-permute-start.12
  30.0 5.3 %collective-permute-done.12 = bf16[128,512]{1,0:T(8,128)(2,1)S(1)} collective-permute-done((bf16[128,512]{1,0:T(8,128)(2,1)}, bf16[128,512]{1,0:T(8,128)(2,1)S(1)}, u32[]{:S(2)}, u32[]{:S(2)}) %collective-permute-start.12) | collective-permute-done | bytes 131104 | tf_op jit(solution)/shard_map/ppermute | solution.py:911
  35.8 7.3 %collective-permute-done.11 = bf16[128,512]{1,0:T(8,128)(2,1)S(1)} collective-permute-done((bf16[128,512]{1,0:T(8,128)(2,1)}, bf16[128,512]{1,0:T(8,128)(2,1)S(1)}, u32[]{:S(2)}, u32[]{:S(2)}) %collective-permute-start.11) | collective-permute-done | bytes 131104 | tf_op jit(solution)/shard_map/ppermute | solution.py:911
  43.7 4.6 %collective-permute-done.10 = bf16[128,512]{1,0:T(8,128)(2,1)S(1)} collective-permute-done((bf16[128,512]{1,0:T(8,128)(2,1)}, bf16[128,512]{1,0:T(8,128)(2,1)S(1)}, u32[]{:S(2)}, u32[]{:S(2)}) %collective-permute-start.10) | collective-permute-done | bytes 131104 | tf_op jit(solution)/shard_map/ppermute | solution.py:911
  53.4 3.3 %arrange_early.1.weights = bf16[32,80,512]{2,1,0:T(8,128)(2,1)} custom-call(s32[3]{0:T(128)} %pad_add_fusion.place, bf16[4,80,512]{2,1,0:T(8,128)(2,1)} %copy-done.6, bf16[4,80,512]{2,1,0:T(8,128)(2,1)} %copy-done.24, bf16[4,80,512]{2,1,0:T(8,128)(2,1)} %copy-done.23, bf16[4,80,512]{2,1,0:T(8,128)(2,1)} %copy-done.22, ...), custom_call_target="tpu_custom_call" | custom-call | flops 100000000 | bytes 100000 | tf_op jit(solution)/shard_map/arrange_early/pallas_call | solution.py:821
  58.5 15.9 %first_attention.1 = (bf16[1088,512]{1,0:T(8,128)(2,1)}, bf16[1088,1536]{1,0:T(8,128)(2,1)}, bf16[9,4,256,128]{3,2,1,0:T(8,128)(2,1)}, bf16[1088,512]{1,0:T(8,12...) custom-call(bf16[1088,512]{1,0:T(8,128)(2,1)} %tokens.3, bf16[32,80,512]{2,1,0:T(8,128)(2,1)} %arrange_early.1.weights, ...), custom_call_target="tpu_custom_call" | custom-call | flops 100000000 | bytes 100000 | tf_op jit(solution)/shard_map/first_attention/pallas_call | solution.py:208
  75.5 6.6 %collective-permute-done.13.refs_1_ = bf16[4,128,512]{2,1,0:T(8,128)(2,1)S(1)} collective-permute-done((bf16[4,128,512]{2,1,0:T(8,128)(2,1)S(1)}, bf16[4,128,512]{2,1,0:T(8,128)(2,1)S(1)}, u32[]{:S(2)}, u32[]{:S(2)}) %collective-permute-start.13) | collective-permute-done | bytes 524320 | tf_op jit(solution)/shard_map/ppermute | solution.py:911
  85.8 14.4 %first_mlp.1 = (bf16[1088,2048]{1,0:T(8,128)(2,1)}, bf16[1088,2048]{1,0:T(8,128)(2,1)}, f32[1088,512]{1,0:T(8,128)}, bf16[32,128,512]{2,1,0:T(8,128)(2,1)}) custom-call(s32[3]{0:T(128)} %pad_add_fusion.place, f32[1088,512]{1,0:T(8,128)} %get-tuple-element.60.middle, bf16[1088,512]{1,0:T(8,128)(2,1)} %get-tuple-element.61.hidden_in, ...), custom_call_target="tpu_custom_call" | custom-call | flops 100000000 | bytes 100000 | tf_op jit(solution)/shard_map/first_mlp/pallas_call | solution.py:280
  100.3 49.0 %second_block.1 = (bf16[17,64,512]{2,1,0:T(8,128)(2,1)}, f32[17,64,512]{2,1,0:T(8,128)}, f32[4,8,512]{2,1,0:T(8,128)}, bf16[16,192,512]{2,1,0:T(8,128)(2,1)}, bf16[16,192,512]{2,1,0:T(8,128)(2,1)}) custom-call(s32[1]{0:T(128)S(6)} %copy.71.frame_count, s32[1]{0:T(128)} %bitcast.core, f32[17,64,512]{2,1,0:T(8,128)} %bitcast.94, ...), custom_call_target="tpu_custom_call" | custom-call | flops 100000000 | bytes 100000 | tf_op jit(solution)/shard_map/second_block/pallas_call | solution.py:536
  149.5 5.7 %collective-permute-done.20 = bf16[16,192,512]{2,1,0:T(8,128)(2,1)S(1)} collective-permute-done((bf16[16,192,512]{2,1,0:T(8,128)(2,1)}, bf16[16,192,512]{2,1,0:T(8,128)(2,1)S(1)}, u32[]{:S(2)}, u32[]{:S(2)}) %collective-permute-start.20) | collective-permute-done | bytes 3145760 | tf_op jit(solution)/shard_map/ppermute | solution.py:911
  155.2 3.7 %fusion.3 = (bf16[4,192,512]{2,1,0:T(8,128)(2,1)S(1)}, bf16[4,192,512]{2,1,0:T(8,128)(2,1)S(1)}, bf16[4,192,512]{2,1,0:T(8,128)(2,1)S(1)}, bf16[4,192,512]{2,1,0:T(8,128)(2,1)}) fusion(bf16[4,4,192,512]{3,2,1,0:T(8,128)(2,1)S(1)} %bitcast.92, s32[]{:T(128)S(6)} %select_n.82, bf16[4,4,192,512]{3,2,1,0:T(8,128)(2,1)} %bitcast.91, s32[]{:T(128)S(6)} %select_n.81, ...), kind=kLoop, calls=%fused_computation.11 | loop fusion | flops 6291456 | bytes 9437200 | tf_op jit(solution)/shard_map/convert_element_type | solution.py:939
  162.5 35.7 %first_back.1 = (f32[1088,512]{1,0:T(8,128)}, f32[2,8,512]{2,1,0:T(8,128)}, bf16[1088,1536]{1,0:T(8,128)(2,1)}, bf16[16,192,512]{2,1,0:T(8,128)(2,1)}, bf16[16,192,512]{2,1,0:T(8,128)(2,1)}) custom-call(s32[1]{0:T(128)} %bitcast.core, f32[1088,512]{1,0:T(8,128)} %bitcast.93, bf16[1088,2048]{1,0:T(8,128)(2,1)} %get-tuple-element.76.slopes, ...), custom_call_target="tpu_custom_call" | custom-call | flops 100000000 | bytes 100000 | tf_op jit(solution)/shard_map/first_back/pallas_call | solution.py:710
  199.6 3.2 %fusion.15 = (bf16[192,512]{1,0:T(8,128)(2,1)S(1)}, bf16[192,512]{1,0:T(8,128)(2,1)S(1)}, bf16[192,512]{1,0:T(8,128)(2,1)}, bf16[192,512]{1,0:T(8,128)(2,1)S(1)}) fusion(bf16[4,192,512]{2,1,0:T(8,128)(2,1)} %copy-done.11, s32[]{:T(128)S(6)} %select_n.83, bf16[4,192,512]{2,1,0:T(8,128)(2,1)} %copy-done.12, bf16[4,192,512]{2,1,0:T(8,128)(2,1)} %copy-done.13, ...), kind=kLoop, calls=%fused_computation.51 | loop fusion | flops 3145728 | bytes 3932176 | tf_op jit(solution)/shard_map/add | solution.py:935
  205.5 2.5 fusion.7
  216.3 11.2 %collective-permute-done.32 = bf16[192,512]{1,0:T(8,128)(2,1)S(1)} collective-permute-done((bf16[192,512]{1,0:T(8,128)(2,1)}, bf16[192,512]{1,0:T(8,128)(2,1)S(1)}, u32[]{:S(2)}, u32[]{:S(2)}) %collective-permute-start.32) | collective-permute-done | bytes 196640 | tf_op jit(solution)/shard_map/ppermute | solution.py:911
  228.6 7.0 %first_input_back.1 = (f32[1088,512]{1,0:T(8,128)}, f32[2,8,512]{2,1,0:T(8,128)}) custom-call(bf16[1088,1536]{1,0:T(8,128)(2,1)} %get-tuple-element.88.projected_grad, bf16[1088,512]{1,0:T(8,128)(2,1)} %tokens.3, f32[1088,512]{1,0:T(8,128)} %get-tuple-element.89.middle_grad, bf16[32,80,512]{2,1,0:T(8,128)(2,1)} %arrange_early.1.weights, f32[4,512]{1,0:T(4,128)} %squeeze.66.gains), custom_call_target="tpu_custom_call" | custom-call | flops 100000000 | bytes 100000 | tf_op jit(solution)/shard_map/first_input_back/pallas_call | solution.py:786
  235.6 10.1 %collective-permute-done.25 = bf16[4,192,512]{2,1,0:T(8,128)(2,1)S(1)} collective-permute-done((bf16[4,192,512]{2,1,0:T(8,128)(2,1)}, bf16[4,192,512]{2,1,0:T(8,128)(2,1)S(1)}, u32[]{:S(2)}, u32[]{:S(2)}) %collective-permute-start.25) | collective-permute-done | bytes 786464 | tf_op jit(solution)/shard_map/ppermute | solution.py:911
  251.0 4.1 %collective-permute-done.30 = bf16[192,512]{1,0:T(8,128)(2,1)S(1)} collective-permute-done((bf16[192,512]{1,0:T(8,128)(2,1)S(1)}, bf16[192,512]{1,0:T(8,128)(2,1)S(1)}, u32[]{:S(2)}, u32[]{:S(2)}) %collective-permute-start.30) | collective-permute-done | bytes 196640 | tf_op jit(solution)/shard_map/ppermute | solution.py:911
  255.1 8.6 %collective-permute-done.29 = bf16[192,512]{1,0:T(8,128)(2,1)S(1)} collective-permute-done((bf16[192,512]{1,0:T(8,128)(2,1)S(1)}, bf16[192,512]{1,0:T(8,128)(2,1)S(1)}, u32[]{:S(2)}, u32[]{:S(2)}) %collective-permute-start.29) | collective-permute-done | bytes 196640 | tf_op jit(solution)/shard_map/ppermute | solution.py:911
  266.2 11.5 %all_to_all.9 = f32[32,1,144]{2,1,0:T(1,128)S(1)} all-to-all(f32[32,1,144]{2,1,0:T(1,128)S(1)} %all_to_all.6), channel_id=1, replica_groups=mesh['dp'=4,'fsdp'=8] {'dp','fsdp'}, dimensions={0} | all-to-all | bytes 36864 | tf_op jit(solution)/shard_map/all_to_all | solution.py:1078
  (192 shorter events, 47.9 us)
Async XLA Ops:
  7.2 93.1 %all-gather.3.cloned.1.call-start = ((), (), s32[]{:S(2)}) async-start(), calls=%async_computation.1 | async-start | bytes 6488064 | tf_op jit(solution)/shard_map/all_gather | solution.py:1013
  23.7 11.7 %collective-permute-start.5 = (bf16[4,80,512]{2,1,0:T(8,128)(2,1)S(1)}, bf16[4,80,512]{2,1,0:T(8,128)(2,1)S(1)}, u32[]{:S(2)}, u32[]{:S(2)}) collective-permute-start(bf16[4,80,512]{2,1,0:T(8,128)(2,1)S(1)} %pad_maximum_fusion.1.refs_0_), channel_id=1, source_target_pairs={{0,24},{1,25},{2,26},{3,27},{4,28},{5,29},{6,30},{7,31},{8,16},{9,... | collective-permute-start | bytes 983048 | tf_op jit(solution)/shard_map/ppermute | solution.py:911
  26.2 16.8 %collective-permute-start.4 = (bf16[4,80,512]{2,1,0:T(8,128)(2,1)S(1)}, bf16[4,80,512]{2,1,0:T(8,128)(2,1)S(1)}, u32[]{:S(2)}, u32[]{:S(2)}) collective-permute-start(bf16[4,80,512]{2,1,0:T(8,128)(2,1)S(1)} %pad_maximum_fusion.1.refs_0_), channel_id=1, source_target_pairs={{0,16},{1,17},{2,18},{3,19},{4,20},{5,21},{6,22},{7,23},{8,24},{9,... | collective-permute-start | bytes 983048 | tf_op jit(solution)/shard_map/ppermute | solution.py:911
  26.7 16.4 %collective-permute-start.3 = (bf16[4,80,512]{2,1,0:T(8,128)(2,1)S(1)}, bf16[4,80,512]{2,1,0:T(8,128)(2,1)S(1)}, u32[]{:S(2)}, u32[]{:S(2)}) collective-permute-start(bf16[4,80,512]{2,1,0:T(8,128)(2,1)S(1)} %pad_maximum_fusion.1.refs_0_), channel_id=1, source_target_pairs={{0,8},{1,9},{2,10},{3,11},{4,12},{5,13},{6,14},{7,15},{8,0},{9,1},... | collective-permute-start | bytes 983048 | tf_op jit(solution)/shard_map/ppermute | solution.py:911
  30.0 13.1 %collective-permute-start.11 = (bf16[128,512]{1,0:T(8,128)(2,1)}, bf16[128,512]{1,0:T(8,128)(2,1)S(1)}, u32[]{:S(2)}, u32[]{:S(2)}) collective-permute-start(bf16[128,512]{1,0:T(8,128)(2,1)} %get-tuple-element.63), channel_id=1, source_target_pairs={{0,4},{1,5},{2,6},{3,7},{4,0},{5,1},{6,2},{7,3},{8,12},{9,13},{10,... | collective-permute-start | bytes 393224 | tf_op jit(solution)/shard_map/ppermute | solution.py:911
  35.3 16.3 %collective-permute-start.6 = (bf16[4,80,512]{2,1,0:T(8,128)(2,1)S(1)}, bf16[4,80,512]{2,1,0:T(8,128)(2,1)}, u32[]{:S(2)}, u32[]{:S(2)}) collective-permute-start(bf16[4,80,512]{2,1,0:T(8,128)(2,1)S(1)} %pad_maximum_fusion.1.refs_0_), channel_id=1, source_target_pairs={{0,1},{1,0},{2,3},{3,2},{4,5},{5,4},{6,7},{7,6},{8,9},{9,8},{10,11... | collective-permute-start | bytes 983048 | tf_op jit(solution)/shard_map/ppermute | solution.py:911
  35.4 16.8 %collective-permute-start.9 = (bf16[4,80,512]{2,1,0:T(8,128)(2,1)S(1)}, bf16[4,80,512]{2,1,0:T(8,128)(2,1)}, u32[]{:S(2)}, u32[]{:S(2)}) collective-permute-start(bf16[4,80,512]{2,1,0:T(8,128)(2,1)S(1)} %collective-permute-done.5.refs_3_), channel_id=1, source_target_pairs={{0,1},{1,0},{2,3},{3,2},{4,5},{5,4},{6,7},{7,6},{8,9},{9,8},{10,11... | collective-permute-start | bytes 983048 | tf_op jit(solution)/shard_map/ppermute | solution.py:911
  43.1 10.3 %collective-permute-start.8 = (bf16[4,80,512]{2,1,0:T(8,128)(2,1)S(1)}, bf16[4,80,512]{2,1,0:T(8,128)(2,1)}, u32[]{:S(2)}, u32[]{:S(2)}) collective-permute-start(bf16[4,80,512]{2,1,0:T(8,128)(2,1)S(1)} %collective-permute-done.4.refs_2_), channel_id=1, source_target_pairs={{0,1},{1,0},{2,3},{3,2},{4,5},{5,4},{6,7},{7,6},{8,9},{9,8},{10,11... | collective-permute-start | bytes 983048 | tf_op jit(solution)/shard_map/ppermute | solution.py:911
  43.2 10.2 %collective-permute-start.7 = (bf16[4,80,512]{2,1,0:T(8,128)(2,1)S(1)}, bf16[4,80,512]{2,1,0:T(8,128)(2,1)}, u32[]{:S(2)}, u32[]{:S(2)}) collective-permute-start(bf16[4,80,512]{2,1,0:T(8,128)(2,1)S(1)} %collective-permute-done.3.refs_1_), channel_id=1, source_target_pairs={{0,1},{1,0},{2,3},{3,2},{4,5},{5,4},{6,7},{7,6},{8,9},{9,8},{10,11... | collective-permute-start | bytes 983048 | tf_op jit(solution)/shard_map/ppermute | solution.py:911
  49.2 25.3 %collective-permute-start.15 = (bf16[4,128,512]{2,1,0:T(8,128)(2,1)S(1)}, bf16[4,128,512]{2,1,0:T(8,128)(2,1)S(1)}, u32[]{:S(2)}, u32[]{:S(2)}) collective-permute-start(bf16[4,128,512]{2,1,0:T(8,128)(2,1)S(1)} %pad_maximum_fusion.refs_0_), channel_id=1, source_target_pairs={{0,24},{1,25},{2,26},{3,27},{4,28},{5,29},{6,30},{7,31},{8,16},{9,... | collective-permute-start | bytes 1572872 | tf_op jit(solution)/shard_map/ppermute | solution.py:911
  51.5 24.0 %collective-permute-start.14 = (bf16[4,128,512]{2,1,0:T(8,128)(2,1)S(1)}, bf16[4,128,512]{2,1,0:T(8,128)(2,1)S(1)}, u32[]{:S(2)}, u32[]{:S(2)}) collective-permute-start(bf16[4,128,512]{2,1,0:T(8,128)(2,1)S(1)} %pad_maximum_fusion.refs_0_), channel_id=1, source_target_pairs={{0,16},{1,17},{2,18},{3,19},{4,20},{5,21},{6,22},{7,23},{8,24},{9,... | collective-permute-start | bytes 1572872 | tf_op jit(solution)/shard_map/ppermute | solution.py:911
  52.3 29.8 %collective-permute-start.13 = (bf16[4,128,512]{2,1,0:T(8,128)(2,1)S(1)}, bf16[4,128,512]{2,1,0:T(8,128)(2,1)S(1)}, u32[]{:S(2)}, u32[]{:S(2)}) collective-permute-start(bf16[4,128,512]{2,1,0:T(8,128)(2,1)S(1)} %pad_maximum_fusion.refs_0_), channel_id=1, source_target_pairs={{0,8},{1,9},{2,10},{3,11},{4,12},{5,13},{6,14},{7,15},{8,0},{9,1},... | collective-permute-start | bytes 1572872 | tf_op jit(solution)/shard_map/ppermute | solution.py:911
  74.4 9.7 %collective-permute-start.16 = (bf16[4,128,512]{2,1,0:T(8,128)(2,1)S(1)}, bf16[4,128,512]{2,1,0:T(8,128)(2,1)S(1)}, u32[]{:S(2)}, u32[]{:S(2)}) collective-permute-start(bf16[4,128,512]{2,1,0:T(8,128)(2,1)S(1)} %pad_maximum_fusion.refs_0_), channel_id=1, source_target_pairs={{0,1},{1,0},{2,3},{3,2},{4,5},{5,4},{6,7},{7,6},{8,9},{9,8},{10,11... | collective-permute-start | bytes 1572872 | tf_op jit(solution)/shard_map/ppermute | solution.py:911
  159.0 39.2 %collective-permute-start.23 = (bf16[4,192,512]{2,1,0:T(8,128)(2,1)S(1)}, bf16[4,192,512]{2,1,0:T(8,128)(2,1)S(1)}, u32[]{:S(2)}, u32[]{:S(2)}) collective-permute-start(bf16[4,192,512]{2,1,0:T(8,128)(2,1)S(1)} %get-tuple-element.219), channel_id=1, source_target_pairs={{0,16},{1,17},{2,18},{3,19},{4,20},{5,21},{6,22},{7,23},{8,24},{9,... | collective-permute-start | bytes 2359304 | tf_op jit(solution)/shard_map/ppermute | solution.py:911
  159.7 38.5 %collective-permute-start.22 = (bf16[4,192,512]{2,1,0:T(8,128)(2,1)S(1)}, bf16[4,192,512]{2,1,0:T(8,128)(2,1)S(1)}, u32[]{:S(2)}, u32[]{:S(2)}) collective-permute-start(bf16[4,192,512]{2,1,0:T(8,128)(2,1)S(1)} %get-tuple-element.220), channel_id=1, source_target_pairs={{0,8},{1,9},{2,10},{3,11},{4,12},{5,13},{6,14},{7,15},{8,0},{9,1},... | collective-permute-start | bytes 2359304 | tf_op jit(solution)/shard_map/ppermute | solution.py:911
  161.0 37.2 %collective-permute-start.21 = (bf16[4,192,512]{2,1,0:T(8,128)(2,1)S(1)}, bf16[4,192,512]{2,1,0:T(8,128)(2,1)S(1)}, u32[]{:S(2)}, u32[]{:S(2)}) collective-permute-start(bf16[4,192,512]{2,1,0:T(8,128)(2,1)S(1)} %get-tuple-element.221), channel_id=1, source_target_pairs={{0,24},{1,25},{2,26},{3,27},{4,28},{5,29},{6,30},{7,31},{8,16},{9,... | collective-permute-start | bytes 2359304 | tf_op jit(solution)/shard_map/ppermute | solution.py:911
  202.8 9.6 %collective-permute-start.33 = (bf16[192,512]{1,0:T(8,128)(2,1)S(1)}, bf16[192,512]{1,0:T(8,128)(2,1)S(1)}, u32[]{:S(2)}, u32[]{:S(2)}) collective-permute-start(bf16[192,512]{1,0:T(8,128)(2,1)S(1)} %get-tuple-element.228), channel_id=1, source_target_pairs={{0,2},{1,3},{2,0},{3,1},{4,6},{5,7},{6,4},{7,5},{8,10},{9,11},{10,... | collective-permute-start | bytes 589832 | tf_op jit(solution)/shard_map/ppermute | solution.py:911
  207.9 27.7 %collective-permute-start.27 = (bf16[4,192,512]{2,1,0:T(8,128)(2,1)}, bf16[4,192,512]{2,1,0:T(8,128)(2,1)S(1)}, u32[]{:S(2)}, u32[]{:S(2)}) collective-permute-start(bf16[4,192,512]{2,1,0:T(8,128)(2,1)} %get-tuple-element.215), channel_id=1, source_target_pairs={{0,16},{1,17},{2,18},{3,19},{4,20},{5,21},{6,22},{7,23},{8,24},{9,... | collective-permute-start | bytes 2359304 | tf_op jit(solution)/shard_map/ppermute | solution.py:911
  208.7 26.9 %collective-permute-start.26 = (bf16[4,192,512]{2,1,0:T(8,128)(2,1)}, bf16[4,192,512]{2,1,0:T(8,128)(2,1)S(1)}, u32[]{:S(2)}, u32[]{:S(2)}) collective-permute-start(bf16[4,192,512]{2,1,0:T(8,128)(2,1)} %get-tuple-element.216), channel_id=1, source_target_pairs={{0,8},{1,9},{2,10},{3,11},{4,12},{5,13},{6,14},{7,15},{8,0},{9,1},... | collective-permute-start | bytes 2359304 | tf_op jit(solution)/shard_map/ppermute | solution.py:911
  210.0 35.8 %collective-permute-start.25 = (bf16[4,192,512]{2,1,0:T(8,128)(2,1)}, bf16[4,192,512]{2,1,0:T(8,128)(2,1)S(1)}, u32[]{:S(2)}, u32[]{:S(2)}) collective-permute-start(bf16[4,192,512]{2,1,0:T(8,128)(2,1)} %get-tuple-element.217), channel_id=1, source_target_pairs={{0,24},{1,25},{2,26},{3,27},{4,28},{5,29},{6,30},{7,31},{8,16},{9,... | collective-permute-start | bytes 2359304 | tf_op jit(solution)/shard_map/ppermute | solution.py:911
  211.4 16.1 %collective-permute-start.32 = (bf16[192,512]{1,0:T(8,128)(2,1)}, bf16[192,512]{1,0:T(8,128)(2,1)S(1)}, u32[]{:S(2)}, u32[]{:S(2)}) collective-permute-start(bf16[192,512]{1,0:T(8,128)(2,1)} %get-tuple-element.229), channel_id=1, source_target_pairs={{0,4},{1,5},{2,6},{3,7},{4,0},{5,1},{6,2},{7,3},{8,12},{9,13},{10,... | collective-permute-start | bytes 589832 | tf_op jit(solution)/shard_map/ppermute | solution.py:911
  212.4 15.2 %collective-permute-start.31 = (bf16[192,512]{1,0:T(8,128)(2,1)S(1)}, bf16[192,512]{1,0:T(8,128)(2,1)S(1)}, u32[]{:S(2)}, u32[]{:S(2)}) collective-permute-start(bf16[192,512]{1,0:T(8,128)(2,1)S(1)} %get-tuple-element.230), channel_id=1, source_target_pairs={{0,6},{1,7},{2,4},{3,5},{4,2},{5,3},{6,0},{7,1},{8,14},{9,15},{10,... | collective-permute-start | bytes 589832 | tf_op jit(solution)/shard_map/ppermute | solution.py:911
  247.2 16.6 %collective-permute-start.29 = (bf16[192,512]{1,0:T(8,128)(2,1)S(1)}, bf16[192,512]{1,0:T(8,128)(2,1)S(1)}, u32[]{:S(2)}, u32[]{:S(2)}) collective-permute-start(bf16[192,512]{1,0:T(8,128)(2,1)S(1)} %get-tuple-element.225), channel_id=1, source_target_pairs={{0,4},{1,5},{2,6},{3,7},{4,0},{5,1},{6,2},{7,3},{8,12},{9,13},{10,... | collective-permute-start | bytes 589832 | tf_op jit(solution)/shard_map/ppermute | solution.py:911
  248.3 15.5 %collective-permute-start.28 = (bf16[192,512]{1,0:T(8,128)(2,1)S(1)}, bf16[192,512]{1,0:T(8,128)(2,1)S(1)}, u32[]{:S(2)}, u32[]{:S(2)}) collective-permute-start(bf16[192,512]{1,0:T(8,128)(2,1)S(1)} %get-tuple-element.226), channel_id=1, source_target_pairs={{0,6},{1,7},{2,4},{3,5},{4,2},{5,3},{6,0},{7,1},{8,14},{9,15},{10,... | collective-permute-start | bytes 589832 | tf_op jit(solution)/shard_map/ppermute | solution.py:911
  (51 other events, 501.0 us)
Sparse Core Ops, SparseCore 0:
  11.6 88.0 all-gather.2

commit v6 on v5

--- a/solution.py
+++ b/solution.py
@@ -137,12 +137,23 @@
     return pl.multiple_of((step - first) * SLAB, SLAB)
 
 
-def grad_specs(rows):
-    return [pl.BlockSpec((BLOCKS // 2, rows, WIDTH), lambda i: (0, 0, 0))] * 2
-
-
 def grad_shapes(rows):
     return [jax.ShapeDtypeStruct((BLOCKS // 2, rows, WIDTH), jnp.bfloat16)] * 2
+
+
+def slab_place(row):
+    return slice(None), pl.ds(row, SLAB)
+
+
+def down_place(block):
+    return pl.ds(block, 4), pl.ds(8 * SLAB, 4 * SLAB)
+
+
+def grad_copies(pairs, sems, unit, place):
+    return [
+        pltpu.make_async_copy(ref.at[place], out.at[place], sems.at[index, unit])
+        for index, (ref, out) in enumerate(pairs)
+    ]
 
 
 def part_of(step, first):
@@ -326,16 +337,7 @@
         ]
 
     def stores(unit, place):
-        return [
-            pltpu.make_async_copy(ref.at[place], out.at[place], store_sems.at[index, unit])
-            for index, (ref, out) in enumerate(((mine, mine_out), (other, other_out)))
-        ]
-
-    def slab_place(row):
-        return slice(None), pl.ds(row, SLAB)
-
-    def down_place(block):
-        return pl.ds(block, 4), pl.ds(8 * SLAB, 4 * SLAB)
+        return grad_copies(((mine, mine_out), (other, other_out)), store_sems, unit, place)
 
     @pl.when(step == 0)
     def _():
@@ -603,11 +605,15 @@
 def first_back_kernel(
     core, upstream, slopes, middle, weights, weights_up, weights_down, gains, hidden, hidden_in,
     attended, queries_in, keys_in, values_in, probs, normed, middle_grad_out, sums, projected_grad_out,
-    mine, other, up_grads, out_grads, branch_grads, attended_grads, projected_grads,
+    mine_out, other_out, up_grads, out_grads, branch_grads, attended_grads, projected_grads,
+    mine, other, store_sems,
 ):
     step = pl.program_id(0)
     heads_at = TILES + 9
     last_at = heads_at + HEADS // 2
+
+    def stores(unit, place):
+        return grad_copies(((mine, mine_out), (other, other_out)), store_sems, unit, place)
 
     @pl.when(step == 0)
     def _():
@@ -640,16 +646,23 @@
     @pl.when((step >= TILES) & (step < TILES + 4))
     def _():
         right = up_grads[:, part_of(step, TILES)]
-        outer_store(core, hidden_in, right, mine, other, 0, slab_row(step, TILES), SLAB)
+        row = slab_row(step, TILES)
+        outer_store(core, hidden_in, right, mine, other, 0, row, SLAB)
+        for copy in stores(step - TILES, slab_place(row)):
+            copy.start()
 
     @pl.when((step >= TILES + 4) & (step < TILES + 8))
     def _():
         block = (step - TILES - 4) * 4
         outer_store(core, hidden, out_grads[...], mine, other, block, 8 * SLAB, 4 * SLAB)
+        for copy in stores(step - TILES, down_place(block)):
+            copy.start()
 
     @pl.when(step == TILES + 8)
     def _():
         outer_store(core, attended, branch_grads[...], mine, other, 0, 4 * SLAB, SLAB)
+        for copy in stores(8, slab_place(4 * SLAB)):
+            copy.start()
 
     @pl.when((step >= heads_at) & (step < last_at))
     def _():
@@ -680,7 +693,19 @@
     def _():
         right = projected_grads[:, part_of(step, last_at)]
         projected_grad_out[...] = right
-        outer_store(core, normed, right, mine, other, 0, slab_row(step, last_at - 5), SLAB)
+        row = slab_row(step, last_at - 5)
+        outer_store(core, normed, right, mine, other, 0, row, SLAB)
+        for copy in stores(step - last_at + 9, slab_place(row)):
+            copy.start()
+
+    @pl.when(step == last_at + 2)
+    def _():
+        places = [slab_place(SLAB * index) for index in range(4)]
+        places += [down_place(4 * index) for index in range(4)]
+        places += [slab_place(SLAB * index) for index in range(4, 8)]
+        for unit, place in enumerate(places):
+            for copy in stores(unit, place):
+                copy.wait()
 
 
 def first_back(
@@ -734,7 +759,8 @@
             tile(WIDTH),
             pl.BlockSpec((2, 8, WIDTH), lambda i: (0, 0, 0)),
             pl.BlockSpec((count, WIDTH), lambda i: (0, jnp.clip(i - last_at, 0, 2))),
-            *grad_specs(12 * SLAB),
+            pl.BlockSpec(memory_space=pl.ANY),
+            pl.BlockSpec(memory_space=pl.ANY),
         ],
         out_shape=[
             jax.ShapeDtypeStruct((count, WIDTH), jnp.float32),
@@ -748,6 +774,9 @@
             held(1),
             pltpu.VMEM((pairs, count, 128), jnp.bfloat16),
             held(3),
+            pltpu.VMEM((BLOCKS // 2, 12 * SLAB, WIDTH), jnp.bfloat16),
+            pltpu.VMEM((BLOCKS // 2, 12 * SLAB, WIDTH), jnp.bfloat16),
+            pltpu.SemaphoreType.DMA((2, 12)),
         ],
         compiler_params=pltpu.CompilerParams(vmem_limit_bytes=VMEM_BYTES),
         cost_estimate=COST,
@@ -844,10 +873,11 @@
             row = first + SLAB * index
             rest[row : row + SLAB, :] = narrow(w_up[block, :, columns])
         rest[first + 4 * SLAB : first + 8 * SLAB, :] = narrow(w_down[block])
-    early[4 * SLAB :, :] = narrow(norm[...])
-
-
-def pack_all(w_qkv, w_out, w_up, w_down, norm_rows):
+    row = jnp.concatenate([norm[...]] * (WIDTH // norm.shape[1]), axis=1)
+    early[4 * SLAB :, :] = narrow(jnp.broadcast_to(row, (SLAB, WIDTH)))
+
+
+def pack_all(w_qkv, w_out, w_up, w_down, norm_row):
     return pl.pallas_call(
         pack_kernel,
         out_shape=[
@@ -857,7 +887,7 @@
         compiler_params=pltpu.CompilerParams(vmem_limit_bytes=VMEM_BYTES),
         cost_estimate=COST,
         name="pack",
-    )(w_qkv, w_out, w_up, w_down, norm_rows)
+    )(w_qkv, w_out, w_up, w_down, norm_row)
 
 
 def adam_parts(gradient, first_moment, second_moment):
@@ -993,17 +1023,16 @@
     by_chips = (lax.axis_size("dp"), lax.axis_size("fsdp")) == (4, 8)
     fsdp = lax.axis_index("fsdp")
     place = jnp.stack([lax.axis_index("dp"), fsdp // 2, fsdp % 2]).astype(jnp.int32)
-    norm_rows = jnp.pad(
-        norm_params.reshape(1, -1), ((0, rows - 1), (0, WIDTH - 8 * rows))
-    )
+    norm_row = norm_params.reshape(1, -1)
     if by_chips:
-        *shard, second_shard = pack_all(w_qkv, w_out, w_up, w_down, norm_rows)
+        *shard, second_shard = pack_all(w_qkv, w_out, w_up, w_down, norm_row)
         early, late_pieces = gather_by_chips(shard)
         early = arrange(place, gather_cores(early), "arrange_early")
         norm_values = early[:, 4 * rows, : 8 * rows]
     else:
         shard = pack_weights(w_qkv[0], w_out[0], w_up[0], w_down[0])
         second_shard = pack_weights(w_qkv[1], w_out[1], w_up[1], w_down[1])
+        norm_rows = jnp.pad(norm_row, ((0, rows - 1), (0, WIDTH - 8 * rows)))
         shard = jnp.concatenate([shard, norm_rows.astype(jnp.bfloat16)], axis=0)
         gathered = lax.all_gather(shard, axes, axis=0)
         norm_values = gathered[:, 12 * rows, : 8 * rows]

time: 291 us -> 290 us (level)
  no operation moved by 1% of the time
where the time goes in v6:
time: 290 us; the launch traced here: 289 us
  Pallas kernels  127 us (44%)
  waiting for transfers between devices  74.7 us (26%)
  starting transfers between devices  32.9 us (11%)
  other arithmetic  21.4 us (7%)
  between operations  15.3 us (5%)
  blocking collectives  11.5 us (4%)
  local copies, waits for them, and re-layouts  6.52 us (2%)
    ppermute x34, waiting for transfers between devices, swap(): lax.ppermute(array, ('dp', 'fsdp'), [(device, device ^ mask) for device i...  74.7 us
    pallas_call x1, Pallas kernels, second_block(): pl.pallas_call(second_kernel, grid=(TILES + 12,), in_specs=[pl.BlockSpec(...  49 us
    pallas_call x1, Pallas kernels, first_back(): pl.pallas_call(first_back_kernel, grid=(last_at + 3,), in_specs=[pl.Block...  35.2 us
    ppermute x34, starting transfers between devices, swap(): lax.ppermute(array, ('dp', 'fsdp'), [(device, device ^ mask) for device i...  32.8 us
    pallas_call x1, Pallas kernels, first_attention(): pl.pallas_call(first_attention_kernel, grid=(2 * TILES + 1,), in_specs=[p...  15.9 us
    pallas_call x1, Pallas kernels, first_mlp(): pl.pallas_call(first_mlp_kernel, grid=(TILES,), in_specs=[pl.BlockSpec(me...  14.5 us
    all_to_all x1, blocking collectives, body(): arrived = jnp.sum(lax.all_to_all(message, axes, 0, 0, tiled=True), axis=0)  11.5 us
    pallas_call x1, Pallas kernels, first_input_back(): pl.pallas_call(first_input_back_kernel, grid=(TILES,), in_specs=[tile(3 *...  6.99 us
  transfers between devices with their start and end apart: 35, of which 17 were waited for; matrix products, arithmetic and copies ran while one was open for 5% of the time, Pallas kernels for 26%

profile of v6, /device:TPU:0, one launch (start us, length us, event | category | flops | bytes accessed | tf_op | source)
XLA Modules:
  0.0 289.2 jit_solution(13016784430507795167)
XLA Ops:
  10.5 5.1 %collective-permute-start.2 = (bf16[80,512]{1,0:T(8,128)(2,1)}, bf16[80,512]{1,0:T(8,128)(2,1)S(1)}, u32[]{:S(2)}, u32[]{:S(2)}) collective-permute-start(bf16[80,512]{1,0:T(8,128)(2,1)} %get-tuple-element.59), channel_id=1, source_target_pairs={{0,6},{1,7},{2,4},{3,5},{4,2},{5,3},{6,0},{7,1},{8,14},{9,15},{10,... | collective-permute-start | bytes 245768 | tf_op jit(solution)/shard_map/ppermute | solution.py:941
  16.2 2.6 collective-permute-done.2
  18.8 3.8 %collective-permute-done.1 = bf16[80,512]{1,0:T(8,128)(2,1)S(1)} collective-permute-done((bf16[80,512]{1,0:T(8,128)(2,1)}, bf16[80,512]{1,0:T(8,128)(2,1)S(1)}, u32[]{:S(2)}, u32[]{:S(2)}) %collective-permute-start.1) | collective-permute-done | bytes 81952 | tf_op jit(solution)/shard_map/ppermute | solution.py:941
  23.6 2.5 collective-permute-start.5
  27.2 2.7 collective-permute-start.12
  29.9 5.3 %collective-permute-done.12 = bf16[128,512]{1,0:T(8,128)(2,1)S(1)} collective-permute-done((bf16[128,512]{1,0:T(8,128)(2,1)}, bf16[128,512]{1,0:T(8,128)(2,1)S(1)}, u32[]{:S(2)}, u32[]{:S(2)}) %collective-permute-start.12) | collective-permute-done | bytes 131104 | tf_op jit(solution)/shard_map/ppermute | solution.py:941
  35.7 7.3 %collective-permute-done.11 = bf16[128,512]{1,0:T(8,128)(2,1)S(1)} collective-permute-done((bf16[128,512]{1,0:T(8,128)(2,1)}, bf16[128,512]{1,0:T(8,128)(2,1)S(1)}, u32[]{:S(2)}, u32[]{:S(2)}) %collective-permute-start.11) | collective-permute-done | bytes 131104 | tf_op jit(solution)/shard_map/ppermute | solution.py:941
  43.6 4.6 %collective-permute-done.10 = bf16[128,512]{1,0:T(8,128)(2,1)S(1)} collective-permute-done((bf16[128,512]{1,0:T(8,128)(2,1)}, bf16[128,512]{1,0:T(8,128)(2,1)S(1)}, u32[]{:S(2)}, u32[]{:S(2)}) %collective-permute-start.10) | collective-permute-done | bytes 131104 | tf_op jit(solution)/shard_map/ppermute | solution.py:941
  53.3 3.3 %arrange_early.1.weights = bf16[32,80,512]{2,1,0:T(8,128)(2,1)} custom-call(s32[3]{0:T(128)} %pad_add_fusion.place, bf16[4,80,512]{2,1,0:T(8,128)(2,1)} %copy-done.6, bf16[4,80,512]{2,1,0:T(8,128)(2,1)} %copy-done.24, bf16[4,80,512]{2,1,0:T(8,128)(2,1)} %copy-done.23, bf16[4,80,512]{2,1,0:T(8,128)(2,1)} %copy-done.22, ...), custom_call_target="tpu_custom_call" | custom-call | flops 100000000 | bytes 100000 | tf_op jit(solution)/shard_map/arrange_early/pallas_call | solution.py:850
  58.4 15.9 %first_attention.1 = (bf16[1088,512]{1,0:T(8,128)(2,1)}, bf16[1088,1536]{1,0:T(8,128)(2,1)}, bf16[9,4,256,128]{3,2,1,0:T(8,128)(2,1)}, bf16[1088,512]{1,0:T(8,12...) custom-call(bf16[1088,512]{1,0:T(8,128)(2,1)} %tokens.3, bf16[32,80,512]{2,1,0:T(8,128)(2,1)} %arrange_early.1.weights, ...), custom_call_target="tpu_custom_call" | custom-call | flops 100000000 | bytes 100000 | tf_op jit(solution)/shard_map/first_attention/pallas_call | solution.py:219
  75.5 6.6 %collective-permute-done.13.refs_1_ = bf16[4,128,512]{2,1,0:T(8,128)(2,1)S(1)} collective-permute-done((bf16[4,128,512]{2,1,0:T(8,128)(2,1)S(1)}, bf16[4,128,512]{2,1,0:T(8,128)(2,1)S(1)}, u32[]{:S(2)}, u32[]{:S(2)}) %collective-permute-start.13) | collective-permute-done | bytes 524320 | tf_op jit(solution)/shard_map/ppermute | solution.py:941
  85.7 14.5 %first_mlp.1 = (bf16[1088,2048]{1,0:T(8,128)(2,1)}, bf16[1088,2048]{1,0:T(8,128)(2,1)}, f32[1088,512]{1,0:T(8,128)}, bf16[32,128,512]{2,1,0:T(8,128)(2,1)}) custom-call(s32[3]{0:T(128)} %pad_add_fusion.place, f32[1088,512]{1,0:T(8,128)} %get-tuple-element.60.middle, bf16[1088,512]{1,0:T(8,128)(2,1)} %get-tuple-element.61.hidden_in, ...), custom_call_target="tpu_custom_call" | custom-call | flops 100000000 | bytes 100000 | tf_op jit(solution)/shard_map/first_mlp/pallas_call | solution.py:291
  100.3 49.0 %second_block.1 = (bf16[17,64,512]{2,1,0:T(8,128)(2,1)}, f32[17,64,512]{2,1,0:T(8,128)}, f32[4,8,512]{2,1,0:T(8,128)}, bf16[16,192,512]{2,1,0:T(8,128)(2,1)}, bf16[16,192,512]{2,1,0:T(8,128)(2,1)}) custom-call(s32[1]{0:T(128)S(6)} %copy.71.frame_count, s32[1]{0:T(128)} %bitcast.core, f32[17,64,512]{2,1,0:T(8,128)} %bitcast.94, ...), custom_call_target="tpu_custom_call" | custom-call | flops 100000000 | bytes 100000 | tf_op jit(solution)/shard_map/second_block/pallas_call | solution.py:538
  149.5 5.7 %collective-permute-done.20 = bf16[16,192,512]{2,1,0:T(8,128)(2,1)S(1)} collective-permute-done((bf16[16,192,512]{2,1,0:T(8,128)(2,1)}, bf16[16,192,512]{2,1,0:T(8,128)(2,1)S(1)}, u32[]{:S(2)}, u32[]{:S(2)}) %collective-permute-start.20) | collective-permute-done | bytes 3145760 | tf_op jit(solution)/shard_map/ppermute | solution.py:941
  155.2 3.7 %fusion.3 = (bf16[4,192,512]{2,1,0:T(8,128)(2,1)S(1)}, bf16[4,192,512]{2,1,0:T(8,128)(2,1)S(1)}, bf16[4,192,512]{2,1,0:T(8,128)(2,1)S(1)}, bf16[4,192,512]{2,1,0:T(8,128)(2,1)}) fusion(bf16[4,4,192,512]{3,2,1,0:T(8,128)(2,1)S(1)} %bitcast.92, s32[]{:T(128)S(6)} %select_n.82, bf16[4,4,192,512]{3,2,1,0:T(8,128)(2,1)} %bitcast.91, s32[]{:T(128)S(6)} %select_n.81, ...), kind=kLoop, calls=%fused_computation.11 | loop fusion | flops 6291456 | bytes 9437200 | tf_op jit(solution)/shard_map/convert_element_type | solution.py:969
  162.4 35.2 %first_back.1 = (f32[1088,512]{1,0:T(8,128)}, f32[2,8,512]{2,1,0:T(8,128)}, bf16[1088,1536]{1,0:T(8,128)(2,1)}, bf16[16,192,512]{2,1,0:T(8,128)(2,1)}, bf16[16,192,512]{2,1,0:T(8,128)(2,1)}) custom-call(s32[1]{0:T(128)} %bitcast.core, f32[1088,512]{1,0:T(8,128)} %bitcast.93, bf16[1088,2048]{1,0:T(8,128)(2,1)} %get-tuple-element.76.slopes, ...), custom_call_target="tpu_custom_call" | custom-call | flops 100000000 | bytes 100000 | tf_op jit(solution)/shard_map/first_back/pallas_call | solution.py:735
  199.1 3.2 %fusion.15 = (bf16[192,512]{1,0:T(8,128)(2,1)S(1)}, bf16[192,512]{1,0:T(8,128)(2,1)S(1)}, bf16[192,512]{1,0:T(8,128)(2,1)}, bf16[192,512]{1,0:T(8,128)(2,1)S(1)}) fusion(bf16[4,192,512]{2,1,0:T(8,128)(2,1)} %copy-done.11, s32[]{:T(128)S(6)} %select_n.83, bf16[4,192,512]{2,1,0:T(8,128)(2,1)} %copy-done.12, bf16[4,192,512]{2,1,0:T(8,128)(2,1)} %copy-done.13, ...), kind=kLoop, calls=%fused_computation.51 | loop fusion | flops 3145728 | bytes 3932176 | tf_op jit(solution)/shard_map/add | solution.py:965
  205.0 2.5 fusion.7
  215.8 11.2 %collective-permute-done.32 = bf16[192,512]{1,0:T(8,128)(2,1)S(1)} collective-permute-done((bf16[192,512]{1,0:T(8,128)(2,1)}, bf16[192,512]{1,0:T(8,128)(2,1)S(1)}, u32[]{:S(2)}, u32[]{:S(2)}) %collective-permute-start.32) | collective-permute-done | bytes 196640 | tf_op jit(solution)/shard_map/ppermute | solution.py:941
  228.1 7.0 %first_input_back.1 = (f32[1088,512]{1,0:T(8,128)}, f32[2,8,512]{2,1,0:T(8,128)}) custom-call(bf16[1088,1536]{1,0:T(8,128)(2,1)} %get-tuple-element.88.projected_grad, bf16[1088,512]{1,0:T(8,128)(2,1)} %tokens.3, f32[1088,512]{1,0:T(8,128)} %get-tuple-element.89.middle_grad, bf16[32,80,512]{2,1,0:T(8,128)(2,1)} %arrange_early.1.weights, f32[4,512]{1,0:T(4,128)} %squeeze.66.gains), custom_call_target="tpu_custom_call" | custom-call | flops 100000000 | bytes 100000 | tf_op jit(solution)/shard_map/first_input_back/pallas_call | solution.py:815
  235.1 10.1 %collective-permute-done.25 = bf16[4,192,512]{2,1,0:T(8,128)(2,1)S(1)} collective-permute-done((bf16[4,192,512]{2,1,0:T(8,128)(2,1)}, bf16[4,192,512]{2,1,0:T(8,128)(2,1)S(1)}, u32[]{:S(2)}, u32[]{:S(2)}) %collective-permute-start.25) | collective-permute-done | bytes 786464 | tf_op jit(solution)/shard_map/ppermute | solution.py:941
  250.5 4.1 %collective-permute-done.30 = bf16[192,512]{1,0:T(8,128)(2,1)S(1)} collective-permute-done((bf16[192,512]{1,0:T(8,128)(2,1)S(1)}, bf16[192,512]{1,0:T(8,128)(2,1)S(1)}, u32[]{:S(2)}, u32[]{:S(2)}) %collective-permute-start.30) | collective-permute-done | bytes 196640 | tf_op jit(solution)/shard_map/ppermute | solution.py:941
  254.6 8.6 %collective-permute-done.29 = bf16[192,512]{1,0:T(8,128)(2,1)S(1)} collective-permute-done((bf16[192,512]{1,0:T(8,128)(2,1)S(1)}, bf16[192,512]{1,0:T(8,128)(2,1)S(1)}, u32[]{:S(2)}, u32[]{:S(2)}) %collective-permute-start.29) | collective-permute-done | bytes 196640 | tf_op jit(solution)/shard_map/ppermute | solution.py:941
  265.7 11.5 %all_to_all.9 = f32[32,1,144]{2,1,0:T(1,128)S(1)} all-to-all(f32[32,1,144]{2,1,0:T(1,128)S(1)} %all_to_all.6), channel_id=1, replica_groups=mesh['dp'=4,'fsdp'=8] {'dp','fsdp'}, dimensions={0} | all-to-all | bytes 36864 | tf_op jit(solution)/shard_map/all_to_all | solution.py:1107
  (191 shorter events, 47.8 us)
Async XLA Ops:
  7.2 93.1 %all-gather.3.cloned.1.call-start = ((), (), s32[]{:S(2)}) async-start(), calls=%async_computation.1 | async-start | bytes 6488064 | tf_op jit(solution)/shard_map/all_gather | solution.py:1042
  23.6 11.7 %collective-permute-start.5 = (bf16[4,80,512]{2,1,0:T(8,128)(2,1)S(1)}, bf16[4,80,512]{2,1,0:T(8,128)(2,1)S(1)}, u32[]{:S(2)}, u32[]{:S(2)}) collective-permute-start(bf16[4,80,512]{2,1,0:T(8,128)(2,1)S(1)} %pad_maximum_fusion.1.refs_0_), channel_id=1, source_target_pairs={{0,24},{1,25},{2,26},{3,27},{4,28},{5,29},{6,30},{7,31},{8,16},{9,... | collective-permute-start | bytes 983048 | tf_op jit(solution)/shard_map/ppermute | solution.py:941
  26.1 16.8 %collective-permute-start.4 = (bf16[4,80,512]{2,1,0:T(8,128)(2,1)S(1)}, bf16[4,80,512]{2,1,0:T(8,128)(2,1)S(1)}, u32[]{:S(2)}, u32[]{:S(2)}) collective-permute-start(bf16[4,80,512]{2,1,0:T(8,128)(2,1)S(1)} %pad_maximum_fusion.1.refs_0_), channel_id=1, source_target_pairs={{0,16},{1,17},{2,18},{3,19},{4,20},{5,21},{6,22},{7,23},{8,24},{9,... | collective-permute-start | bytes 983048 | tf_op jit(solution)/shard_map/ppermute | solution.py:941
  26.6 16.4 %collective-permute-start.3 = (bf16[4,80,512]{2,1,0:T(8,128)(2,1)S(1)}, bf16[4,80,512]{2,1,0:T(8,128)(2,1)S(1)}, u32[]{:S(2)}, u32[]{:S(2)}) collective-permute-start(bf16[4,80,512]{2,1,0:T(8,128)(2,1)S(1)} %pad_maximum_fusion.1.refs_0_), channel_id=1, source_target_pairs={{0,8},{1,9},{2,10},{3,11},{4,12},{5,13},{6,14},{7,15},{8,0},{9,1},... | collective-permute-start | bytes 983048 | tf_op jit(solution)/shard_map/ppermute | solution.py:941
  29.9 13.1 %collective-permute-start.11 = (bf16[128,512]{1,0:T(8,128)(2,1)}, bf16[128,512]{1,0:T(8,128)(2,1)S(1)}, u32[]{:S(2)}, u32[]{:S(2)}) collective-permute-start(bf16[128,512]{1,0:T(8,128)(2,1)} %get-tuple-element.63), channel_id=1, source_target_pairs={{0,4},{1,5},{2,6},{3,7},{4,0},{5,1},{6,2},{7,3},{8,12},{9,13},{10,... | collective-permute-start | bytes 393224 | tf_op jit(solution)/shard_map/ppermute | solution.py:941
  35.2 16.3 %collective-permute-start.6 = (bf16[4,80,512]{2,1,0:T(8,128)(2,1)S(1)}, bf16[4,80,512]{2,1,0:T(8,128)(2,1)}, u32[]{:S(2)}, u32[]{:S(2)}) collective-permute-start(bf16[4,80,512]{2,1,0:T(8,128)(2,1)S(1)} %pad_maximum_fusion.1.refs_0_), channel_id=1, source_target_pairs={{0,1},{1,0},{2,3},{3,2},{4,5},{5,4},{6,7},{7,6},{8,9},{9,8},{10,11... | collective-permute-start | bytes 983048 | tf_op jit(solution)/shard_map/ppermute | solution.py:941
  35.3 16.9 %collective-permute-start.9 = (bf16[4,80,512]{2,1,0:T(8,128)(2,1)S(1)}, bf16[4,80,512]{2,1,0:T(8,128)(2,1)}, u32[]{:S(2)}, u32[]{:S(2)}) collective-permute-start(bf16[4,80,512]{2,1,0:T(8,128)(2,1)S(1)} %collective-permute-done.5.refs_3_), channel_id=1, source_target_pairs={{0,1},{1,0},{2,3},{3,2},{4,5},{5,4},{6,7},{7,6},{8,9},{9,8},{10,11... | collective-permute-start | bytes 983048 | tf_op jit(solution)/shard_map/ppermute | solution.py:941
  43.0 10.3 %collective-permute-start.8 = (bf16[4,80,512]{2,1,0:T(8,128)(2,1)S(1)}, bf16[4,80,512]{2,1,0:T(8,128)(2,1)}, u32[]{:S(2)}, u32[]{:S(2)}) collective-permute-start(bf16[4,80,512]{2,1,0:T(8,128)(2,1)S(1)} %collective-permute-done.4.refs_2_), channel_id=1, source_target_pairs={{0,1},{1,0},{2,3},{3,2},{4,5},{5,4},{6,7},{7,6},{8,9},{9,8},{10,11... | collective-permute-start | bytes 983048 | tf_op jit(solution)/shard_map/ppermute | solution.py:941
  43.1 10.2 %collective-permute-start.7 = (bf16[4,80,512]{2,1,0:T(8,128)(2,1)S(1)}, bf16[4,80,512]{2,1,0:T(8,128)(2,1)}, u32[]{:S(2)}, u32[]{:S(2)}) collective-permute-start(bf16[4,80,512]{2,1,0:T(8,128)(2,1)S(1)} %collective-permute-done.3.refs_1_), channel_id=1, source_target_pairs={{0,1},{1,0},{2,3},{3,2},{4,5},{5,4},{6,7},{7,6},{8,9},{9,8},{10,11... | collective-permute-start | bytes 983048 | tf_op jit(solution)/shard_map/ppermute | solution.py:941
  49.1 25.3 %collective-permute-start.15 = (bf16[4,128,512]{2,1,0:T(8,128)(2,1)S(1)}, bf16[4,128,512]{2,1,0:T(8,128)(2,1)S(1)}, u32[]{:S(2)}, u32[]{:S(2)}) collective-permute-start(bf16[4,128,512]{2,1,0:T(8,128)(2,1)S(1)} %pad_maximum_fusion.refs_0_), channel_id=1, source_target_pairs={{0,24},{1,25},{2,26},{3,27},{4,28},{5,29},{6,30},{7,31},{8,16},{9,... | collective-permute-start | bytes 1572872 | tf_op jit(solution)/shard_map/ppermute | solution.py:941
  51.5 24.0 %collective-permute-start.14 = (bf16[4,128,512]{2,1,0:T(8,128)(2,1)S(1)}, bf16[4,128,512]{2,1,0:T(8,128)(2,1)S(1)}, u32[]{:S(2)}, u32[]{:S(2)}) collective-permute-start(bf16[4,128,512]{2,1,0:T(8,128)(2,1)S(1)} %pad_maximum_fusion.refs_0_), channel_id=1, source_target_pairs={{0,16},{1,17},{2,18},{3,19},{4,20},{5,21},{6,22},{7,23},{8,24},{9,... | collective-permute-start | bytes 1572872 | tf_op jit(solution)/shard_map/ppermute | solution.py:941
  52.2 29.9 %collective-permute-start.13 = (bf16[4,128,512]{2,1,0:T(8,128)(2,1)S(1)}, bf16[4,128,512]{2,1,0:T(8,128)(2,1)S(1)}, u32[]{:S(2)}, u32[]{:S(2)}) collective-permute-start(bf16[4,128,512]{2,1,0:T(8,128)(2,1)S(1)} %pad_maximum_fusion.refs_0_), channel_id=1, source_target_pairs={{0,8},{1,9},{2,10},{3,11},{4,12},{5,13},{6,14},{7,15},{8,0},{9,1},... | collective-permute-start | bytes 1572872 | tf_op jit(solution)/shard_map/ppermute | solution.py:941
  74.3 9.7 %collective-permute-start.16 = (bf16[4,128,512]{2,1,0:T(8,128)(2,1)S(1)}, bf16[4,128,512]{2,1,0:T(8,128)(2,1)S(1)}, u32[]{:S(2)}, u32[]{:S(2)}) collective-permute-start(bf16[4,128,512]{2,1,0:T(8,128)(2,1)S(1)} %pad_maximum_fusion.refs_0_), channel_id=1, source_target_pairs={{0,1},{1,0},{2,3},{3,2},{4,5},{5,4},{6,7},{7,6},{8,9},{9,8},{10,11... | collective-permute-start | bytes 1572872 | tf_op jit(solution)/shard_map/ppermute | solution.py:941
  158.9 38.7 %collective-permute-start.23 = (bf16[4,192,512]{2,1,0:T(8,128)(2,1)S(1)}, bf16[4,192,512]{2,1,0:T(8,128)(2,1)S(1)}, u32[]{:S(2)}, u32[]{:S(2)}) collective-permute-start(bf16[4,192,512]{2,1,0:T(8,128)(2,1)S(1)} %get-tuple-element.219), channel_id=1, source_target_pairs={{0,16},{1,17},{2,18},{3,19},{4,20},{5,21},{6,22},{7,23},{8,24},{9,... | collective-permute-start | bytes 2359304 | tf_op jit(solution)/shard_map/ppermute | solution.py:941
  159.6 38.0 %collective-permute-start.22 = (bf16[4,192,512]{2,1,0:T(8,128)(2,1)S(1)}, bf16[4,192,512]{2,1,0:T(8,128)(2,1)S(1)}, u32[]{:S(2)}, u32[]{:S(2)}) collective-permute-start(bf16[4,192,512]{2,1,0:T(8,128)(2,1)S(1)} %get-tuple-element.220), channel_id=1, source_target_pairs={{0,8},{1,9},{2,10},{3,11},{4,12},{5,13},{6,14},{7,15},{8,0},{9,1},... | collective-permute-start | bytes 2359304 | tf_op jit(solution)/shard_map/ppermute | solution.py:941
  161.1 36.6 %collective-permute-start.21 = (bf16[4,192,512]{2,1,0:T(8,128)(2,1)S(1)}, bf16[4,192,512]{2,1,0:T(8,128)(2,1)S(1)}, u32[]{:S(2)}, u32[]{:S(2)}) collective-permute-start(bf16[4,192,512]{2,1,0:T(8,128)(2,1)S(1)} %get-tuple-element.221), channel_id=1, source_target_pairs={{0,24},{1,25},{2,26},{3,27},{4,28},{5,29},{6,30},{7,31},{8,16},{9,... | collective-permute-start | bytes 2359304 | tf_op jit(solution)/shard_map/ppermute | solution.py:941
  202.3 9.6 %collective-permute-start.33 = (bf16[192,512]{1,0:T(8,128)(2,1)S(1)}, bf16[192,512]{1,0:T(8,128)(2,1)S(1)}, u32[]{:S(2)}, u32[]{:S(2)}) collective-permute-start(bf16[192,512]{1,0:T(8,128)(2,1)S(1)} %get-tuple-element.228), channel_id=1, source_target_pairs={{0,2},{1,3},{2,0},{3,1},{4,6},{5,7},{6,4},{7,5},{8,10},{9,11},{10,... | collective-permute-start | bytes 589832 | tf_op jit(solution)/shard_map/ppermute | solution.py:941
  207.4 27.7 %collective-permute-start.27 = (bf16[4,192,512]{2,1,0:T(8,128)(2,1)}, bf16[4,192,512]{2,1,0:T(8,128)(2,1)S(1)}, u32[]{:S(2)}, u32[]{:S(2)}) collective-permute-start(bf16[4,192,512]{2,1,0:T(8,128)(2,1)} %get-tuple-element.215), channel_id=1, source_target_pairs={{0,16},{1,17},{2,18},{3,19},{4,20},{5,21},{6,22},{7,23},{8,24},{9,... | collective-permute-start | bytes 2359304 | tf_op jit(solution)/shard_map/ppermute | solution.py:941
  208.1 27.0 %collective-permute-start.26 = (bf16[4,192,512]{2,1,0:T(8,128)(2,1)}, bf16[4,192,512]{2,1,0:T(8,128)(2,1)S(1)}, u32[]{:S(2)}, u32[]{:S(2)}) collective-permute-start(bf16[4,192,512]{2,1,0:T(8,128)(2,1)} %get-tuple-element.216), channel_id=1, source_target_pairs={{0,8},{1,9},{2,10},{3,11},{4,12},{5,13},{6,14},{7,15},{8,0},{9,1},... | collective-permute-start | bytes 2359304 | tf_op jit(solution)/shard_map/ppermute | solution.py:941
  209.6 35.7 %collective-permute-start.25 = (bf16[4,192,512]{2,1,0:T(8,128)(2,1)}, bf16[4,192,512]{2,1,0:T(8,128)(2,1)S(1)}, u32[]{:S(2)}, u32[]{:S(2)}) collective-permute-start(bf16[4,192,512]{2,1,0:T(8,128)(2,1)} %get-tuple-element.217), channel_id=1, source_target_pairs={{0,24},{1,25},{2,26},{3,27},{4,28},{5,29},{6,30},{7,31},{8,16},{9,... | collective-permute-start | bytes 2359304 | tf_op jit(solution)/shard_map/ppermute | solution.py:941
  210.9 16.1 %collective-permute-start.32 = (bf16[192,512]{1,0:T(8,128)(2,1)}, bf16[192,512]{1,0:T(8,128)(2,1)S(1)}, u32[]{:S(2)}, u32[]{:S(2)}) collective-permute-start(bf16[192,512]{1,0:T(8,128)(2,1)} %get-tuple-element.229), channel_id=1, source_target_pairs={{0,4},{1,5},{2,6},{3,7},{4,0},{5,1},{6,2},{7,3},{8,12},{9,13},{10,... | collective-permute-start | bytes 589832 | tf_op jit(solution)/shard_map/ppermute | solution.py:941
  211.9 15.1 %collective-permute-start.31 = (bf16[192,512]{1,0:T(8,128)(2,1)S(1)}, bf16[192,512]{1,0:T(8,128)(2,1)S(1)}, u32[]{:S(2)}, u32[]{:S(2)}) collective-permute-start(bf16[192,512]{1,0:T(8,128)(2,1)S(1)} %get-tuple-element.230), channel_id=1, source_target_pairs={{0,6},{1,7},{2,4},{3,5},{4,2},{5,3},{6,0},{7,1},{8,14},{9,15},{10,... | collective-permute-start | bytes 589832 | tf_op jit(solution)/shard_map/ppermute | solution.py:941
  246.7 16.6 %collective-permute-start.29 = (bf16[192,512]{1,0:T(8,128)(2,1)S(1)}, bf16[192,512]{1,0:T(8,128)(2,1)S(1)}, u32[]{:S(2)}, u32[]{:S(2)}) collective-permute-start(bf16[192,512]{1,0:T(8,128)(2,1)S(1)} %get-tuple-element.225), channel_id=1, source_target_pairs={{0,4},{1,5},{2,6},{3,7},{4,0},{5,1},{6,2},{7,3},{8,12},{9,13},{10,... | collective-permute-start | bytes 589832 | tf_op jit(solution)/shard_map/ppermute | solution.py:941
  248.0 15.3 %collective-permute-start.28 = (bf16[192,512]{1,0:T(8,128)(2,1)S(1)}, bf16[192,512]{1,0:T(8,128)(2,1)S(1)}, u32[]{:S(2)}, u32[]{:S(2)}) collective-permute-start(bf16[192,512]{1,0:T(8,128)(2,1)S(1)} %get-tuple-element.226), channel_id=1, source_target_pairs={{0,6},{1,7},{2,4},{3,5},{4,2},{5,3},{6,0},{7,1},{8,14},{9,15},{10,... | collective-permute-start | bytes 589832 | tf_op jit(solution)/shard_map/ppermute | solution.py:941
  (51 other events, 501.1 us)
Sparse Core Ops, SparseCore 0:
  11.6 88.0 all-gather.2
